TPU v7x, 128 devices: a whole 4x4x4 slice. The times are simulated.
128 devices in a mesh: ctx: 32 (over y, z_hi, x), wt: 4 (over z_lo, core).
Axes of the slice: x: 4, y: 4, z: 4 (z_hi: 2, z_lo: 2; z = z_hi * 2 + z_lo), core: 2. Of those that a mesh axis runs over, the one named last changes fastest.
Arguments:
- stream: bfloat16 [8192, 2048], P('ctx'), may hold values from -6 to 6
- layer_input: bfloat16 [8192, 256], P('ctx', 'wt'), may hold values from -6 to 6
- out_grad: bfloat16 [8192, 2048], P('ctx'), may hold values from -6 to 6
- doc_lengths: int32 [8], replicated, may hold values from 1 to 4096, 8192 in all
- stretch_slots: int32 [64], replicated, may hold values from 0 to 63, each once
- gain_input: float32 [2048], replicated, may hold values from 0.5 to 1.5
- gain_query: float32 [256], replicated, may hold values from 0.6 to 1.4
- gain_key: float32 [256], replicated, may hold values from 0.6 to 1.4
- w_query: bfloat16 [2048, 2048], P(None, 'wt'), may hold values from -0.125 to 0.125
- w_key: bfloat16 [2048, 512], P(None, 'wt'), may hold values from -0.125 to 0.125
- w_value: bfloat16 [2048, 512], P(None, 'wt'), may hold values from -0.125 to 0.125
- w_attn_out: bfloat16 [2048, 2048], P('wt'), may hold values from -0.5 to 0.5
- gain_attn: float32 [2048], replicated, may hold values from 0.5 to 1.5
- laurel_left: bfloat16 [2048, 64], P(None, 'wt'), may hold values from -0.125 to 0.125
- laurel_right: bfloat16 [64, 2048], P('wt'), may hold values from -0.75 to 0.75
- gain_laurel: float32 [2048], replicated, may hold values from 0.5 to 1.5
- gain_pre_ff: float32 [2048], replicated, may hold values from 0.5 to 1.5
- w_gate: bfloat16 [2048, 8192], P(None, 'wt'), may hold values from -0.125 to 0.125
- w_up: bfloat16 [2048, 8192], P(None, 'wt'), may hold values from -0.125 to 0.125
- w_down: bfloat16 [8192, 2048], P('wt'), may hold values from -0.0625 to 0.0625
- gain_post_ff: float32 [2048], replicated, may hold values from 0.5 to 1.5
- join_gate: bfloat16 [2048, 256], P(None, 'wt'), may hold values from -0.125 to 0.125
- join_proj: bfloat16 [256, 2048], P('wt'), may hold values from -0.375 to 0.375
- gain_join: float32 [2048], replicated, may hold values from 0.5 to 1.5
Outputs:
- layer_out: float32 [8192, 2048], P('ctx')
- stream_grad: float32 [8192, 2048], P('ctx')
- layer_input_grad: float32 [8192, 256], P('ctx', 'wt')
- grad_gain_input: float32 [2048], P('ctx')
- grad_gain_query: float32 [256], P('ctx')
- grad_gain_key: float32 [256], P('ctx')
- grad_w_query: float32 [2048, 2048], P('ctx', 'wt')
- grad_w_key: float32 [2048, 512], P('ctx', 'wt')
- grad_w_value: float32 [2048, 512], P('ctx', 'wt')
- grad_w_attn_out: float32 [2048, 2048], P('wt', 'ctx')
- grad_gain_attn: float32 [2048], P('ctx')
- grad_laurel_left: float32 [2048, 64], P('ctx', 'wt')
- grad_laurel_right: float32 [64, 2048], P('wt', 'ctx')
- grad_gain_laurel: float32 [2048], P('ctx')
- grad_gain_pre_ff: float32 [2048], P('ctx')
- grad_w_gate: float32 [2048, 8192], P('ctx', 'wt')
- grad_w_up: float32 [2048, 8192], P('ctx', 'wt')
- grad_w_down: float32 [8192, 2048], P('wt', 'ctx')
- grad_gain_post_ff: float32 [2048], P('ctx')
- grad_join_gate: float32 [2048, 256], P('ctx', 'wt')
- grad_join_proj: float32 [256, 2048], P('wt', 'ctx')
- grad_gain_join: float32 [2048], P('ctx')
Inputs may be any that keep to these rules, and one draw needn't show every extreme that they name: doc_lengths sum to 8192; the longest document has exactly 4096 tokens; documents may span several stretches. stretch_slots names every stretch of the stream once.
All inputs are finite; a program needn't handle non-finite values.
Results may differ from a plain program's by a relative error of at most 0.035.
Values may be sent and summed in bfloat16 or wider, within the bound.
No kernel may reach another device: no remote copies, remote signals or barrier semaphores. Data moves between devices by JAX's collectives and lax.ppermute only.
A program may use at most 192 MiB of HBM per device.

v0:
```python
import jax
import jax.numpy as jnp
from jax import lax
from jax.experimental import pallas as pl
from jax.experimental.pallas import tpu as pltpu
from jax.sharding import PartitionSpec as P

EPS = 1e-06
ROPE_BASE = 1000000.0
ROOT_HALF = 0.7071067811865476
GELU_A = 0.7978845608028654
GELU_B = 0.044715
STRETCH = 128
HEAD = 256
SLOTS = 64
PAD_SLOTS = 72
CHUNK = 4
D = 2048
VMEM_GRANT = 60 * 1024 * 1024
BF = jnp.bfloat16
F32 = jnp.float32


def hop(value, axis, mask):
    return lax.ppermute(value, axis, [(i, i ^ mask) for i in range(lax.axis_size(axis))])


def pick(value, index, axis):
    return lax.dynamic_index_in_dim(value, index, axis, keepdims=False)


def ctx_of(y, z, x):
    return (y * 2 + z) * 4 + x


GROUP_X = [[ctx_of(y, z, x) for x in range(4)] for y in range(4) for z in range(2)]
GROUP_Y = [[ctx_of(y, z, x) for y in range(4)] for z in range(2) for x in range(4)]
GROUP_Z = [[ctx_of(y, z, x) for z in range(2)] for y in range(4) for x in range(4)]


def gather_group(value, groups):
    return lax.all_gather(value, "ctx", axis=0, axis_index_groups=groups)


def scatter_group(value, groups):
    return lax.psum_scatter(
        value, "ctx", scatter_dimension=0, axis_index_groups=groups, tiled=True
    )


def gate_kernel(*refs):
    pass


def hold(values, event):
    return pl.pallas_call(
        gate_kernel,
        out_shape=tuple(jax.ShapeDtypeStruct(value.shape, value.dtype) for value in values),
        in_specs=[pl.BlockSpec(memory_space=pl.ANY)] * (len(values) + 1),
        out_specs=(pl.BlockSpec(memory_space=pl.ANY),) * len(values),
        input_output_aliases={i: i for i in range(len(values))},
        name="gate",
    )(*values, event)


def ring_gather(block, near, other):
    one = hop(block, "ctx", near)
    two = hop(block, "ctx", other)
    half = block.shape[0] // 2
    return [
        block,
        one,
        two,
        hop(one[:half], "ctx", other),
        hop(two[half:], "ctx", near),
    ]


def gather_wt(own):
    near = hop(own, "wt", 2)
    core = hop(own, "wt", 1)
    far = hop(near, "wt", 1)
    return own, near, core, far


def scatter_wt(kept, sent):
    kept = kept + hop(sent, "wt", 1).astype(F32)
    quarter = kept.shape[0] // 2
    return kept[:quarter], hop(kept[quarter:].astype(BF), "wt", 2)


def fold(kept, sent, mask):
    return (kept.astype(F32) + hop(sent, "ctx", mask).astype(F32)).astype(BF)


def swap_halves(value):
    half = value.shape[0] // 2
    return jnp.concatenate([value[half:], value[:half]], axis=0)


def dot(left, right):
    return jnp.dot(left, right, preferred_element_type=F32)


def dot_rows(left, right):
    return lax.dot_general(left, right, (((0,), (0,)), ((), ())), preferred_element_type=F32)


def dot_cols(left, right):
    return lax.dot_general(left, right, (((1,), (1,)), ((), ())), preferred_element_type=F32)


def halves_of(value):
    high = value.astype(BF)
    return high, (value - high.astype(F32)).astype(BF)


def fine(left, right):
    high, low = halves_of(left)
    return dot(high, right) + dot(low, right)


def fine_cols(left, right):
    high, low = halves_of(left)
    return dot_cols(high, right) + dot_cols(low, right)


def rms(values):
    return lax.rsqrt(jnp.mean(values * values, axis=-1, keepdims=True) + EPS)


def norm_back(grad, normal, scale, gain):
    inner = grad * gain
    back = scale * (inner - normal * jnp.mean(inner * normal, axis=-1, keepdims=True))
    return back, jnp.sum(grad * normal, axis=0, keepdims=grad.ndim == 2)


def rotate(values, cosine, sine):
    half = values.shape[-1] // 2
    front, rear = values[..., :half], values[..., half:]
    return jnp.concatenate([front * cosine - rear * sine, rear * cosine + front * sine], axis=-1)


def gelu_parts(value):
    square = value * value
    bend = jnp.tanh(GELU_A * value * (1.0 + GELU_B * square))
    half = 0.5 * (1.0 + bend)
    slope = half + 0.5 * value * (1.0 - bend * bend) * GELU_A * (1.0 + 3.0 * GELU_B * square)
    return value * half, slope


AT_V = PAD_SLOTS
AT_HI = 2 * PAD_SLOTS
AT_LO = AT_HI + 2
AT_Z = AT_LO + 2
AT_ENDS = AT_Z + 1


def piece_copies(pieces, held, sem):
    copies, at = [], 0
    for i, piece in enumerate(pieces):
        count = piece.shape[0]
        place = held.at[pl.ds(at, count)]
        copies.append(pltpu.make_async_copy(piece, place, sem.at[i]))
        at += count
    return copies


def load_pieces(pieces, held, sem):
    copies = piece_copies(pieces, held, sem)
    for copy in copies:
        copy.start()
    for copy in copies:
        copy.wait()


def query_places(meta, tile, shape, along):
    row = lax.broadcasted_iota(jnp.int32, shape, along) & (STRETCH - 1)
    row = (row + 64 * meta[AT_Z]) & (STRETCH - 1)
    place = meta[AT_HI + tile] * STRETCH + row
    start = jnp.zeros(shape, jnp.int32)
    for j in range(8):
        end = meta[AT_ENDS + j]
        start = jnp.maximum(start, jnp.where(place >= end, end, 0))
    return place, start


def key_places(meta, first, shape, along):
    at = lax.broadcasted_iota(jnp.int32, shape, along)
    row = ((at & (STRETCH - 1)) + 64 * meta[AT_Z]) & (STRETCH - 1)
    return first * STRETCH + (at - (at & (STRETCH - 1))) + row


def tile_of(ref, tile):
    rows = pl.ds(tile * STRETCH, STRETCH)
    return jnp.concatenate([ref[rows, :HEAD], ref[rows, HEAD:]], axis=0)


def stretches(meta, held, at, first):
    return jnp.concatenate([held[meta[at + first + u]] for u in range(CHUNK)], axis=0)


def turns_of(meta, tile):
    return (meta[AT_HI + tile] - meta[AT_LO + tile] + CHUNK) // CHUNK


def forward_kernel(meta, q_ref, w_ref, *refs):
    pieces, (low_ref, full_ref, lse_ref, kept_ref, sent_ref) = refs[:20], refs[20:25]
    held, acc, total, sem = refs[25:]
    load_pieces(pieces, held, sem)
    for tile in range(2):
        query = tile_of(q_ref, tile)
        place, start = query_places(meta, tile, (2 * STRETCH, 1), 0)
        acc[...] = jnp.zeros_like(acc)
        total[...] = jnp.zeros_like(total)

        def turn(i, carry):
            first = meta[AT_LO + tile] + CHUNK * i
            keys = stretches(meta, held, 0, first)
            values = stretches(meta, held, AT_V, first)
            scores = dot_cols(query, keys)
            key_at = key_places(meta, first, (1, CHUNK * STRETCH), 1)
            allowed = (key_at <= place) & (key_at >= start)
            weights = jnp.where(allowed, jnp.exp(scores), 0.0)
            part = weights[:, :STRETCH]
            for u in range(1, CHUNK):
                part = part + weights[:, u * STRETCH : (u + 1) * STRETCH]
            total[...] += part
            acc[...] += dot(weights.astype(BF), values)
            return carry

        lax.fori_loop(0, turns_of(meta, tile), turn, 0)
        row_total = jnp.sum(total[...], axis=1, keepdims=True)
        result = acc[...] / row_total
        rows = pl.ds(tile * STRETCH, STRETCH)
        for head in range(2):
            block = result[head * STRETCH : (head + 1) * STRETCH]
            low_ref[rows, head * HEAD : (head + 1) * HEAD] = block.astype(BF)
            full_ref[rows, head * HEAD : (head + 1) * HEAD] = block
        logs = jnp.broadcast_to(jnp.log(row_total), (2 * STRETCH, STRETCH))
        lse_ref[tile] = jnp.transpose(logs)[:8]
    kept_ref[...] = dot(low_ref[:STRETCH], w_ref[...])
    sent_ref[...] = dot(low_ref[STRETCH:], w_ref[...]).astype(BF)


def backward_kernel(meta, q_ref, full_ref, lse_ref, w_ref, *refs):
    parts, pieces, dq_ref, outs = refs[:4], refs[4:24], refs[-10], refs[-9:-5]
    held, grads, acc, g_ref, sem = refs[-5:]
    copies = piece_copies(pieces, held, sem)
    for copy in copies:
        copy.start()
    for i, part in enumerate(parts):
        g_ref[64 * i : 64 * (i + 1)] = dot_cols(part[...], w_ref[...]).astype(BF)
    grads[...] = jnp.zeros_like(grads)
    for copy in copies:
        copy.wait()
    for tile in range(2):
        query = tile_of(q_ref, tile)
        grad = tile_of(g_ref, tile)
        full = tile_of(full_ref, tile)
        place, start = query_places(meta, tile, (1, 2 * STRETCH), 1)
        lse = lse_ref[tile][:1]
        delta = jnp.sum(grad.astype(F32) * full, axis=1, keepdims=True)
        delta = jnp.transpose(jnp.broadcast_to(delta, (2 * STRETCH, STRETCH)))[:1]
        acc[...] = jnp.zeros_like(acc)

        def turn(i, carry):
            first = meta[AT_LO + tile] + CHUNK * i
            keys = stretches(meta, held, 0, first)
            values = stretches(meta, held, AT_V, first)
            key_at = key_places(meta, first, (CHUNK * STRETCH, 1), 0)
            allowed = (key_at <= place) & (key_at >= start)
            weights = jnp.where(allowed, jnp.exp(dot_cols(keys, query) - lse), 0.0)
            slopes = (weights * (dot_cols(values, grad) - delta)).astype(BF)
            key_term = dot(slopes, query)
            value_term = dot(weights.astype(BF), grad)
            acc[...] += dot_rows(slopes, keys)
            for u in range(CHUNK):
                part = slice(u * STRETCH, (u + 1) * STRETCH)
                for at, term in ((meta[first + u], key_term), (meta[AT_V + first + u], value_term)):
                    grads[at] = (grads[at].astype(F32) + term[part]).astype(BF)
            return carry

        lax.fori_loop(0, turns_of(meta, tile), turn, 0)
        rows = pl.ds(tile * STRETCH, STRETCH)
        for head in range(2):
            block = acc[head * STRETCH : (head + 1) * STRETCH]
            dq_ref[rows, head * HEAD : (head + 1) * HEAD] = block * (HEAD**-0.5)
    copies = []
    for side in range(2):
        for h in range(2):
            at = 64 * side + 32 * h
            for out, first, count, begin in ((0, 24, 8, 8 * h), (1, 0, 24, 24 * h)):
                copies.append(
                    pltpu.make_async_copy(
                        grads.at[pl.ds(at + first, count)],
                        outs[2 * side + out].at[pl.ds(begin, count)],
                        sem.at[len(copies)],
                    )
                )
    for copy in copies:
        copy.start()
    for copy in copies:
        copy.wait()


def in_vmem():
    return pl.BlockSpec(memory_space=pltpu.VMEM)


def anywhere():
    return pl.BlockSpec(memory_space=pl.ANY)


def attend_forward(meta, query, w_attn_out, pieces):
    rows, width = query.shape[0], w_attn_out.shape[1]
    return pl.pallas_call(
        forward_kernel,
        out_shape=(
            jax.ShapeDtypeStruct((rows, 2 * HEAD), BF),
            jax.ShapeDtypeStruct((rows, 2 * HEAD), F32),
            jax.ShapeDtypeStruct((2, 8, 2 * STRETCH), F32),
            jax.ShapeDtypeStruct((STRETCH, width), F32),
            jax.ShapeDtypeStruct((STRETCH, width), BF),
        ),
        in_specs=[pl.BlockSpec(memory_space=pltpu.SMEM), in_vmem(), in_vmem()] + [anywhere()] * 20,
        out_specs=(in_vmem(),) * 5,
        scratch_shapes=[
            pltpu.VMEM((2 * SLOTS, STRETCH, HEAD), BF),
            pltpu.VMEM((2 * STRETCH, HEAD), F32),
            pltpu.VMEM((2 * STRETCH, STRETCH), F32),
            pltpu.SemaphoreType.DMA((20,)),
        ],
        compiler_params=pltpu.CompilerParams(vmem_limit_bytes=VMEM_GRANT),
        cost_estimate=pl.CostEstimate(
            flops=3 * 10**9, bytes_accessed=10**7, transcendentals=2 * 10**6
        ),
        name="attend_forward",
    )(meta, query, w_attn_out, *pieces)


def attend_backward(meta, query, full, lse, w_attn_out, parts, pieces, *events):
    rows = query.shape[0]
    outs = pl.pallas_call(
        backward_kernel,
        out_shape=(jax.ShapeDtypeStruct((rows, 2 * HEAD), F32),)
        + tuple(jax.ShapeDtypeStruct((count, STRETCH, HEAD), BF) for count in (16, 48, 16, 48)),
        in_specs=[pl.BlockSpec(memory_space=pltpu.SMEM)] + [in_vmem()] * 8
        + [anywhere()] * (20 + len(events)),
        out_specs=(in_vmem(),) + (anywhere(),) * 4,
        scratch_shapes=[
            pltpu.VMEM((2 * SLOTS, STRETCH, HEAD), BF),
            pltpu.VMEM((2 * SLOTS, STRETCH, HEAD), BF),
            pltpu.VMEM((2 * STRETCH, HEAD), F32),
            pltpu.VMEM((rows, 2 * HEAD), BF),
            pltpu.SemaphoreType.DMA((20,)),
        ],
        compiler_params=pltpu.CompilerParams(vmem_limit_bytes=VMEM_GRANT),
        cost_estimate=pl.CostEstimate(
            flops=10**10, bytes_accessed=2 * 10**7, transcendentals=2 * 10**6
        ),
        name="attend_backward",
    )(meta, query, full, lse, w_attn_out, *parts, *pieces, *events)
    return outs[0], outs[1:]


UNITS = 512


def ff_forward_kernel(*refs):
    parts, (w_gate, w_up, w_down) = refs[:4], refs[4:7]
    gate_out, up_out, pre_out, act_out, kept, sent = refs[7:13]
    now, acc = refs[13:]
    turn = pl.program_id(0)

    @pl.when(turn == 0)
    def first():
        for i, part in enumerate(parts):
            pre_out[64 * i : 64 * (i + 1)] = part[...]
        acc[...] = jnp.zeros_like(acc)

    gate = dot(pre_out[...], w_gate[...])
    up = dot(pre_out[...], w_up[...])
    gate_out[...] = gate
    up_out[...] = up
    now[...] = (gelu_parts(gate)[0] * up).astype(BF)
    act_out[...] = now[...]
    acc[...] += dot(now[...], w_down[...])

    @pl.when(turn == pl.num_programs(0) - 1)
    def last():
        kept[...] = acc[:STRETCH]
        sent[...] = acc[STRETCH:].astype(BF)


def ff_forward(parts, w_gate, w_up, w_down):
    width, units = w_gate.shape
    rows = 4 * parts[0].shape[0]
    whole = lambda shape: pl.BlockSpec(shape, lambda i: (0, 0))
    tall, flat = pl.BlockSpec((width, UNITS), lambda i: (0, i)), pl.BlockSpec((UNITS, width), lambda i: (i, 0))
    strip = pl.BlockSpec((rows, UNITS), lambda i: (0, i))
    return pl.pallas_call(
        ff_forward_kernel,
        grid=(units // UNITS,),
        out_shape=(
            jax.ShapeDtypeStruct((rows, units), F32),
            jax.ShapeDtypeStruct((rows, units), F32),
            jax.ShapeDtypeStruct((rows, width), BF),
            jax.ShapeDtypeStruct((rows, units), BF),
            jax.ShapeDtypeStruct((rows // 2, width), F32),
            jax.ShapeDtypeStruct((rows // 2, width), BF),
        ),
        in_specs=[whole((rows // 4, width))] * 4 + [tall, tall, flat],
        out_specs=(
            strip,
            strip,
            whole((rows, width)),
            strip,
            whole((rows // 2, width)),
            whole((rows // 2, width)),
        ),
        scratch_shapes=[pltpu.VMEM((rows, UNITS), BF), pltpu.VMEM((rows, width), F32)],
        compiler_params=pltpu.CompilerParams(vmem_limit_bytes=VMEM_GRANT),
        cost_estimate=pl.CostEstimate(
            flops=6 * rows * width * units, bytes_accessed=3 * 10**7, transcendentals=rows * units
        ),
        name="ff_forward",
    )(*parts, w_gate, w_up, w_down)


def ff_grads_kernel(me, *refs):
    parts, (gate_ref, up_ref, w_down) = refs[:4], refs[4:7]
    cuts, quarters, all_in = refs[7:11], refs[11:15], refs[15]
    block = pl.program_id(0)

    @pl.when(block == 0)
    def first():
        for i, part in enumerate(parts):
            all_in[64 * i : 64 * (i + 1)] = part[...]
        for k in range(4):
            at = pl.multiple_of((me[1] ^ k) * 512, 512)
            quarters[k][...] = all_in[:, pl.ds(at, 512)]

    grad_act = dot_cols(all_in[...], w_down[...])
    value, slope = gelu_parts(gate_ref[...])
    for k in range(4):

        @pl.when(block == k)
        def store():
            cuts[k][:, :UNITS] = (grad_act * up_ref[...] * slope).astype(BF)
            cuts[k][:, UNITS:] = (grad_act * value).astype(BF)


def ff_grads(me, parts, gate_pre, up_pre, w_down):
    units, width = w_down.shape
    rows = gate_pre.shape[0]
    whole = lambda shape: pl.BlockSpec(shape, lambda k, me: (0, 0))
    flat = pl.BlockSpec((UNITS, width), lambda k, me: (k ^ me[0], 0))
    strip = pl.BlockSpec((rows, UNITS), lambda k, me: (0, k ^ me[0]))
    outs = pl.pallas_call(
        ff_grads_kernel,
        grid_spec=pltpu.PrefetchScalarGridSpec(
            num_scalar_prefetch=1,
            grid=(4,),
            in_specs=[whole((rows // 4, width))] * 4 + [strip, strip, flat],
            out_specs=(whole((rows, 2 * UNITS)),) * 4 + (whole((rows, width // 4)),) * 4,
            scratch_shapes=[pltpu.VMEM((rows, width), BF)],
        ),
        out_shape=(jax.ShapeDtypeStruct((rows, 2 * UNITS), BF),) * 4
        + (jax.ShapeDtypeStruct((rows, width // 4), BF),) * 4,
        compiler_params=pltpu.CompilerParams(vmem_limit_bytes=VMEM_GRANT),
        cost_estimate=pl.CostEstimate(
            flops=2 * rows * width * units, bytes_accessed=10**7, transcendentals=rows * units
        ),
        name="ff_grads",
    )(me, *parts, gate_pre, up_pre, w_down)
    return outs[:4], outs[4:]


def ff_back_kernel(me, *refs):
    cuts, (w_gate, w_up, kept, sent, acc) = refs[:4], refs[4:]
    block = pl.program_id(0)

    @pl.when(block == 0)
    def first():
        acc[...] = jnp.zeros_like(acc)

    for k in range(4):

        @pl.when(block == k)
        def add():
            term = dot_cols(cuts[k][:, :UNITS], w_gate[...])
            acc[...] += term + dot_cols(cuts[k][:, UNITS:], w_up[...])

    @pl.when(block == 3)
    def last():
        kept[...] = acc[:STRETCH]
        sent[...] = acc[STRETCH:].astype(BF)


def ff_back(me, cuts, w_gate, w_up):
    width, units = w_gate.shape
    rows = cuts[0].shape[0]
    whole = lambda shape: pl.BlockSpec(shape, lambda k, me: (0, 0))
    tall = pl.BlockSpec((width, UNITS), lambda k, me: (0, k ^ me[0]))
    return pl.pallas_call(
        ff_back_kernel,
        grid_spec=pltpu.PrefetchScalarGridSpec(
            num_scalar_prefetch=1,
            grid=(4,),
            in_specs=[whole((rows, 2 * UNITS))] * 4 + [tall, tall],
            out_specs=(whole((rows // 2, width)),) * 2,
            scratch_shapes=[pltpu.VMEM((rows, width), F32)],
        ),
        out_shape=(
            jax.ShapeDtypeStruct((rows // 2, width), F32),
            jax.ShapeDtypeStruct((rows // 2, width), BF),
        ),
        compiler_params=pltpu.CompilerParams(vmem_limit_bytes=VMEM_GRANT),
        cost_estimate=pl.CostEstimate(
            flops=4 * rows * width * units, bytes_accessed=2 * 10**7, transcendentals=0
        ),
        name="ff_back",
    )(me, *cuts, w_gate, w_up)


def relative_rows(spots, stream):
    return jnp.concatenate(
        [stream[pl.ds(pl.multiple_of(spots[i], 64), 64)] for i in range(4)], axis=0
    )


def swapped(value):
    return jnp.concatenate([value[STRETCH:], value[:STRETCH]], axis=0)


def input_kernel(spots, stream, w_key, w_value, g_in, normed_out, mine, theirs):
    rows = relative_rows(spots, stream).astype(F32)
    normed_out[...] = (rows * rms(rows) * g_in[...]).astype(BF)
    key, value = dot(normed_out[...], w_key[...]), dot(normed_out[...], w_value[...])
    first = spots[4] == 0
    mine[...] = jnp.where(first, key, value)
    theirs[...] = swapped(jnp.where(first, value, key))


def kind_kernel(spots, mine, came, cosine, sine, gain, low_out, full_out):
    first = spots[4] == 0
    kind = jnp.concatenate(
        [jnp.where(first, mine[...], came[...]), jnp.where(first, came[...], mine[...])], axis=1
    )
    full_out[...] = kind
    turn = (jnp.where(first, cosine[...], 1.0), jnp.where(first, sine[...], 0.0))
    scaled = kind * rms(kind) * jnp.where(first, gain[...], 1.0)
    low_out[...] = rotate(scaled, *turn).astype(BF)


def lay_kernel(*refs):
    for h in range(2):
        for i in range(4):
            refs[8 + h][256 * i : 256 * (i + 1)] = refs[4 * h + i][...]


def kind_back_kernel(spots, sums_a, sums_b, came, kind_ref, cosine, sine, gain, event, home, away, gains):
    first = spots[4] == 0
    turn = (jnp.where(first, cosine[...], 1.0), jnp.where(first, -sine[...], 0.0))
    grad = jnp.concatenate([sums_a[...] + came[0].astype(F32), sums_b[...] + came[1].astype(F32)], axis=0)
    kind = kind_ref[...]
    scale = rms(kind)
    grad, gain_part = norm_back(
        rotate(grad, *turn), kind * scale, scale, jnp.where(first, gain[...], 1.0)
    )
    gains[...] = jnp.where(first, gain_part, 0.0)
    half = HEAD // 2
    home[...] = jnp.where(first, grad[:, :half], grad[:, half:]).astype(BF)
    away[...] = swapped(jnp.where(first, grad[:, half:], grad[:, :half])).astype(BF)


def query_kernel(normed, w_query, cosine, sine, gain, event, low_out, raw_out):
    for head in range(2):
        at = slice(head * HEAD, (head + 1) * HEAD)
        raw = dot(normed[...], w_query[:, at])
        raw_out[:, at] = raw
        turned = rotate(raw * rms(raw) * gain[...], cosine[...], sine[...]).astype(BF)
        low_out[:, at] = (turned.astype(F32) * HEAD**-0.5).astype(BF)


def query_back_kernel(grad_ref, raw_ref, cosine, sine, gain, event, low_out, gains):
    gains[...] = jnp.zeros_like(gains)
    for head in range(2):
        at = slice(head * HEAD, (head + 1) * HEAD)
        raw = raw_ref[:, at]
        scale = rms(raw)
        grad, part = norm_back(
            rotate(grad_ref[:, at], cosine[...], -sine[...]), raw * scale, scale, gain[...]
        )
        low_out[:, at] = grad.astype(BF)
        gains[...] += part


def normed_back_kernel(spots, home, came, query, w_query, w_key, w_value, stream, *outs):
    kept, sent, gain_out, cuts = outs[-7], outs[-6], outs[-5], outs[-4:]
    first = spots[4] == 0
    key = jnp.where(first, home[...].astype(F32), came[...].astype(F32)).astype(BF)
    value = jnp.where(first, came[...].astype(F32), home[...].astype(F32)).astype(BF)
    part = dot_cols(query[...], w_query[...])
    part = part + dot_cols(key, w_key[...]) + dot_cols(value, w_value[...])
    kept[...] = part[:STRETCH]
    sent[...] = part[STRETCH:].astype(BF)
    rows = relative_rows(spots, stream).astype(F32)
    gain_out[...] = jnp.sum(part * (rows * rms(rows)), axis=0, keepdims=True)
    for k, cut in enumerate(cuts):
        at = spots[5] ^ k
        cut[:, :128] = query[:, pl.ds(pl.multiple_of(at * 128, 128), 128)]
        side = jnp.where(at >= 2, value.astype(F32), key.astype(F32))
        side = jnp.where((at & 1) == 1, side[:, 64:], side[:, :64])
        cut[:, 128:] = side.astype(BF)


def far_kernel(own, came, *refs):
    for i, out in enumerate(refs[-4:]):
        at = slice(4 * i, 4 * i + 4)
        out[...] = (own[at].astype(F32) + came[at].astype(F32)).astype(BF)


def near_kernel(own, came, *refs):
    passed, (base_a, base_b), sends = refs[:4], refs[-6:-4], refs[-4:]

    def summed(first, count):
        at = slice(first, first + count)
        return own[at].astype(F32) + came[at].astype(F32)

    for h, base in enumerate((base_a, base_b)):
        near, other = sends[2 * h], sends[2 * h + 1]
        base[...] = summed(24 * h, 8)
        near[:4] = summed(24 * h + 8, 4).astype(BF)
        near[4:] = (summed(24 * h + 12, 4) + passed[2 * h + 1][...].astype(F32)).astype(BF)
        other[:4] = (summed(24 * h + 16, 4) + passed[2 * h][...].astype(F32)).astype(BF)
        other[4:] = summed(24 * h + 20, 4).astype(BF)


def inner_kernel(base_a, base_b, *refs):
    came, kept, sends = refs[:4], refs[-8:-6], refs[-6:]
    for h, base in enumerate((base_a, base_b)):
        total = base[...] + came[2 * h][...].astype(F32) + came[2 * h + 1][...].astype(F32)
        kept[h][...] = total[:2]
        for k in (1, 2, 3):
            sends[3 * h + k - 1][...] = total[2 * k : 2 * k + 2].astype(BF)


def last_kernel(kept_a, kept_b, *refs):
    came, kept, send = refs[:6], refs[6:8], refs[8]
    for h, base in enumerate((kept_a, kept_b)):
        total = base[...]
        for k in range(3):
            total = total + came[3 * h + k][...].astype(F32)
        kept[h][...] = total[0]
        send[h] = total[1].astype(BF)


def mid_kernel(kept, came, stream, left, right, g_in, g_attn, g_laurel, g_pre, *outs):
    pre_out, resid_out, attn_out, laurel_out, low_out = outs
    rows = stream[...].astype(F32)
    normed = rows * rms(rows) * g_in[...]
    attn = kept[...] + came[...].astype(F32)
    low = dot_cols(normed.astype(BF), left[...])
    laurel = fine(low, right[...])
    resid = (
        rows + attn * rms(attn) * g_attn[...] + normed + laurel * rms(laurel) * g_laurel[...]
    ) * ROOT_HALF
    pre_out[...] = (resid * rms(resid) * g_pre[...]).astype(BF)
    resid_out[...] = resid
    attn_out[...] = attn
    laurel_out[...] = laurel
    low_out[...] = low


def join_kernel(kept, came, resid, top, inputs, gate_t, proj, g_post, g_join, event, *outs):
    ff_out, after_out, results, gains, mine, theirs = outs
    ff = kept[...] + came[...].astype(F32)
    ff_scale = rms(ff)
    ff_normal = ff * ff_scale
    after = resid[...] + ff_normal * g_post[...]
    value, slope = gelu_parts(fine_cols(after, gate_t[...]))
    channels = inputs[...].astype(F32)
    joined = value * channels
    join = fine(joined, proj[...])
    join_scale = rms(join)
    join_normal = join * join_scale
    results[:, :D] = (after + join_normal * g_join[...]).astype(BF)
    grad = top[...].astype(F32)
    grad_join, gain_join = norm_back(grad, join_normal, join_scale, g_join[...])
    grad_joined = fine_cols(grad_join, proj[...])
    grad_pre = grad_joined * channels * slope
    results[:, D:] = (grad_joined * value).astype(BF)
    grad_after = grad + fine(grad_pre, gate_t[...])
    after_out[...] = grad_after
    grad_ff, gain_post = norm_back(grad_after, ff_normal, ff_scale, g_post[...])
    ff_out[...] = grad_ff.astype(BF)
    gains[...] = jnp.zeros_like(gains)
    gains[0:1] = gain_post
    gains[1:2] = gain_join
    low_gate = dot_rows(grad_pre.astype(BF), after.astype(BF)).astype(BF)
    low_proj = dot_rows(joined.astype(BF), grad_join.astype(BF)).astype(BF)
    for k, (out, i) in enumerate(((mine, 0), (theirs, 0), (mine, 1), (theirs, 1))):
        out[i, :64] = low_gate[64 * k : 64 * (k + 1)]
        out[i, 64:] = low_proj[64 * k : 64 * (k + 1)]


def resid_kernel(
    kept,
    came,
    resid,
    after,
    attn,
    laurel,
    low,
    stream,
    left,
    right,
    g_in,
    g_attn,
    g_laurel,
    g_pre,
    gates_mine,
    gates_sent,
    *refs,
):
    attn_out, branch_out, own_out, gains, mine, theirs = refs[-6:]
    mine[:, 32:] = gates_mine[...]
    theirs[:, 32:] = gates_sent[...]
    scale = rms(resid[...])
    grad = kept[...] + came[...].astype(F32)
    grad_resid, gain_pre = norm_back(grad, resid[...] * scale, scale, g_pre[...])
    branch = (after[...] + grad_resid) * ROOT_HALF
    branch_out[...] = branch
    scale = rms(attn[...])
    grad_attn, gain_attn = norm_back(branch, attn[...] * scale, scale, g_attn[...])
    attn_out[...] = grad_attn.astype(BF)
    scale = rms(laurel[...])
    grad_laurel, gain_laurel = norm_back(branch, laurel[...] * scale, scale, g_laurel[...])
    grad_low = fine_cols(grad_laurel, right[...])
    own = branch + fine(grad_low, left[...])
    own_out[...] = own
    rows = stream[...].astype(F32)
    normal = rows * rms(rows)
    gains[...] = jnp.zeros_like(gains)
    gains[0:1] = gain_attn
    gains[1:2] = gain_laurel
    gains[2:3] = gain_pre
    gains[3:4] = jnp.sum(own * normal, axis=0, keepdims=True)
    low_left = dot_rows(grad_low.astype(BF), (normal * g_in[...]).astype(BF)).astype(BF)
    low_right = dot_rows(low[...].astype(BF), grad_laurel.astype(BF)).astype(BF)
    for k, (out, i) in enumerate(((mine, 0), (theirs, 0), (mine, 1), (theirs, 1))):
        out[i, :16] = low_left[16 * k : 16 * (k + 1)]
        out[i, 16:32] = low_right[16 * k : 16 * (k + 1)]


def final_kernel(kept, came, own, branch, stream, g_in, event, out):
    rows = stream[...].astype(F32)
    scale = rms(rows)
    grad = own[...] + kept[...] + came[...].astype(F32)
    extra, _ = norm_back(grad, rows * scale, scale, g_in[...])
    out[...] = (branch[...] + extra).astype(BF)


def in_one(kernel, shapes, args, name, event=(), spots=(), scratch=()):
    return pl.pallas_call(
        kernel,
        out_shape=tuple(jax.ShapeDtypeStruct(shape, kind) for shape, kind in shapes),
        in_specs=[pl.BlockSpec(memory_space=pltpu.SMEM)] * len(spots)
        + [in_vmem()] * len(args)
        + [anywhere()] * len(event),
        out_specs=(in_vmem(),) * len(shapes),
        scratch_shapes=list(scratch),
        compiler_params=pltpu.CompilerParams(vmem_limit_bytes=VMEM_GRANT),
        cost_estimate=pl.CostEstimate(flops=10**9, bytes_accessed=5 * 10**6, transcendentals=10**5),
        name=name,
    )(*spots, *args, *event)


def pack_kernel(left, right, gate_w, proj, inputs, event, out):
    unit = (
        lax.broadcasted_iota(jnp.int32, (64, 64), 0) == lax.broadcasted_iota(jnp.int32, (64, 64), 1)
    ).astype(BF)
    out[:16] = dot_cols(unit[:16, :16], left[...]).astype(BF)
    out[16:32] = right[...]
    out[32:96] = dot_cols(unit, gate_w[...]).astype(BF)
    out[96:160] = proj[...]
    turned = dot_cols(unit, inputs[...]).astype(BF)
    out[160:] = jnp.zeros_like(out[160:])
    for i in range(4):
        out[160:, 256 * i : 256 * (i + 1)] = turned[16 * i : 16 * (i + 1)]


Y_FIRST = (0, 3, 1, 2)
Y_OTHER = (0, 1, 3, 2)


def group_sum(me, group, cuts, at, size):
    total = None
    for k, cut in enumerate(cuts):
        term = dot_rows(group[me ^ k, :, pl.ds(at, size)], cut)
        total = term if total is None else total + term
    return total


def wide_kernel(where, group, *refs):
    cuts, out = refs[:4], refs[-1]
    for at in range(0, D, 256):
        total = group_sum(where[0], group, [cut[...] for cut in cuts], at, 256)
        out[at : at + 256] = total.astype(BF)


def wide_product(where, group, cuts, event):
    return pl.pallas_call(
        wide_kernel,
        out_shape=jax.ShapeDtypeStruct((D, cuts[0].shape[1]), BF),
        in_specs=[pl.BlockSpec(memory_space=pltpu.SMEM)] + [in_vmem()] * 5 + [anywhere()],
        out_specs=in_vmem(),
        compiler_params=pltpu.CompilerParams(vmem_limit_bytes=VMEM_GRANT),
        cost_estimate=pl.CostEstimate(flops=5 * 10**9, bytes_accessed=10**7, transcendentals=0),
        name="wide_product",
    )(where, group, *cuts, event)


def turn_kernel(small, attn, *refs):
    parts, out, grads = refs[:4], refs[-2], refs[-1]
    low = small.shape[0]
    for i, part in enumerate(parts):
        grads[64 * i : 64 * (i + 1)] = part[...]
    unit = (
        lax.broadcasted_iota(jnp.int32, (low, 256), 0)
        == lax.broadcasted_iota(jnp.int32, (low, 256), 1)
    ).astype(BF)
    out[:, :512] = dot_rows(grads[...], attn[...]).astype(BF)
    out[:, 512:] = dot_rows(small[...], unit).astype(BF)


def token_kernel(where, group, gains, *refs):
    cuts, (kept, sent) = refs[:4], refs[4:]
    x, y, z = where[0], where[1], where[2]
    unit = (
        lax.broadcasted_iota(jnp.int32, (16, 64), 0) == lax.broadcasted_iota(jnp.int32, (16, 64), 1)
    ).astype(BF)
    for i, far_y in enumerate(Y_FIRST):
        for far_z in range(2):
            at = pl.multiple_of(((y ^ far_y) * 2 + (z ^ far_z)) * 256, 256)
            total = group_sum(x, group, [cut[...] for cut in cuts], at, 256)
            more = dot_rows(gains[:, pl.ds(at, 256)], unit)
            total = jnp.concatenate([total, more], axis=1).astype(BF)
            (kept, sent)[i // 2][i % 2, far_z] = total


def token_product(where, group, gains, cuts):
    shape = (2, 2, 256, cuts[0].shape[1] + 64)
    return pl.pallas_call(
        token_kernel,
        out_shape=(jax.ShapeDtypeStruct(shape, BF),) * 2,
        in_specs=[pl.BlockSpec(memory_space=pltpu.SMEM)] + [in_vmem()] * 6,
        out_specs=(in_vmem(),) * 2,
        compiler_params=pltpu.CompilerParams(vmem_limit_bytes=VMEM_GRANT),
        cost_estimate=pl.CostEstimate(flops=10**9, bytes_accessed=6 * 10**6, transcendentals=0),
        name="token_product",
    )(where, group, gains, *cuts)


def payload_kernel(where, wide, tokens, turn, *outs):
    for k, out in enumerate(outs):
        at = pl.ds(pl.multiple_of((where[0] ^ k) * 64, 64), 64)
        out[:, :1024] = wide[at]
        out[:, 1024:1280] = tokens[at]
        out[:, 1280:] = turn[at]


def share_kernel(where, *refs):
    shares, down_kept, down_came = refs[:4], refs[4], refs[5]
    gate, up, query, key, value, attn, left, right, join_g, join_p, gains, down = refs[6:]
    x = where[0]

    def turned(rows):
        rows = jnp.concatenate([rows, jnp.zeros_like(rows)], axis=0)
        return jnp.transpose(rows)[:, :64]

    for k, share in enumerate(shares):
        gate[:, pl.ds(pl.multiple_of((x ^ k) * 512, 512), 512)] = share[:, :512].astype(F32)
        up[:, pl.ds(pl.multiple_of((x ^ k) * 512, 512), 512)] = share[:, 512:1024].astype(F32)
        query[:, pl.ds(pl.multiple_of((x ^ k) * 128, 128), 128)] = share[:, 1024:1152].astype(F32)
    quarters = [share[:, 1152:1216].astype(F32) for share in shares]
    placed = []
    for q in range(4):
        choice = quarters[3]
        for k in range(3):
            choice = jnp.where((x ^ k) == q, quarters[k], choice)
        placed.append(choice)
    key[:, :64], key[:, 64:] = placed[0], placed[1]
    value[:, :64], value[:, 64:] = placed[2], placed[3]
    total = shares[0][:, 1216:].astype(F32)
    for share in shares[1:]:
        total = total + share[:, 1216:].astype(F32)
    gains[...] = total[:, :16]
    attn[...] = total[:, 64:576]
    small = total[:, 576:736]
    join_g[...] = small[:, 32:96]
    lines = turned(jnp.concatenate([small, jnp.zeros((64, 96), F32)], axis=1))
    left[...] = lines[:16]
    right[...] = lines[16:32]
    join_p[...] = lines[96:160]
    down[...] = down_kept[...].astype(F32) + down_came[...].astype(F32)


def down_kernel(where, group, *refs):
    cuts, out, total = refs[:4], refs[5], refs[6]
    x, y = where[0], where[1]
    units = group.shape[2]
    for first in range(0, units, 512):
        value = None
        for k, cut in enumerate(cuts):
            term = dot_rows(cut[...], group[y ^ k, :, first : first + 512])
            value = term if value is None else value + term
        total[...] = value
        for i, far_x in enumerate(Y_FIRST):
            for z in range(2):
                at = pl.multiple_of((z * 4 + (x ^ far_x)) * 64, 64)
                out[z, i, :, first : first + 512] = total[pl.ds(at, 64)].astype(BF)


def down_product(where, group, cuts, event):
    return pl.pallas_call(
        down_kernel,
        out_shape=jax.ShapeDtypeStruct((2, 4, 64, group.shape[2]), BF),
        in_specs=[pl.BlockSpec(memory_space=pltpu.SMEM)] + [in_vmem()] * 5 + [anywhere()],
        out_specs=in_vmem(),
        scratch_shapes=[pltpu.VMEM((512, 512), F32)],
        compiler_params=pltpu.CompilerParams(vmem_limit_bytes=VMEM_GRANT),
        cost_estimate=pl.CostEstimate(flops=3 * 10**9, bytes_accessed=10**7, transcendentals=0),
        name="down_product",
    )(where, group, *cuts, event)


def local(
    stream,
    layer_input,
    out_grad,
    doc_lengths,
    stretch_slots,
    gain_input,
    gain_query,
    gain_key,
    w_query,
    w_key,
    w_value,
    w_attn_out,
    gain_attn,
    laurel_left,
    laurel_right,
    gain_laurel,
    gain_pre_ff,
    w_gate,
    w_up,
    w_down,
    gain_post_ff,
    join_gate,
    join_proj,
    gain_join,
):
    wt = lax.axis_index("wt")
    core, zlo = wt & 1, wt >> 1
    ctx = lax.axis_index("ctx")
    at_x, at_z, at_y = ctx & 3, (ctx >> 2) & 1, ctx >> 3
    first_core = core == 0
    half = HEAD // 2

    def starts(k):
        return ((core ^ (k & 1)) * 2 + (zlo ^ (k >> 1))) * 64

    def natural(blocks):
        stacked = jnp.stack(blocks)
        return jnp.concatenate(
            [pick(stacked, wt ^ ((b & 1) * 2 + (b >> 1)), 0) for b in range(4)], axis=0
        )

    stream_own = lax.dynamic_slice_in_dim(stream, starts(0), 64, 0)
    grad_top = lax.dynamic_slice_in_dim(out_grad, starts(0), 64, 0)
    where = jnp.stack([at_x, at_y, at_z])
    spots = (jnp.stack([starts(0), starts(2), starts(1), starts(3), core, at_x]),)
    g_in, g_attn, g_laurel, g_pre, g_post, g_join = (
        gain[None, :]
        for gain in (gain_input, gain_attn, gain_laurel, gain_pre_ff, gain_post_ff, gain_join)
    )

    doc_ends = jnp.cumsum(doc_lengths)
    tiles = [lax.dynamic_index_in_dim(stretch_slots, 2 * ctx + (core ^ t), 0) for t in range(2)]
    hi = jnp.concatenate(tiles)
    lo = jnp.max(
        jnp.where(doc_ends[None, :] <= hi[:, None] * STRETCH, doc_ends[None, :], 0), axis=1
    )
    lo = lo // STRETCH
    row = (jnp.arange(STRETCH, dtype=jnp.int32) + 64 * zlo) & (STRETCH - 1)
    positions = (hi[:, None] * STRETCH + row[None, :]).reshape(-1)
    names = jnp.arange(SLOTS, dtype=jnp.int32)
    slot_of = jnp.sum(jnp.where(stretch_slots[None, :] == names[:, None], names[None, :], 0), axis=1)
    relative = (slot_of >> 1) ^ ctx
    rel_x, rel_z, rel_y = relative & 3, (relative >> 2) & 1, relative >> 3
    places = (
        (rel_y ^ (rel_y >> 1)) * 8 + rel_x * 2 + rel_z,
        SLOTS // 2 + (rel_x ^ (rel_x >> 1)) * 8 + rel_y * 2 + rel_z,
    )
    second = (slot_of & 1) == 1
    key_at = core * SLOTS + jnp.where(second, places[1], places[0])
    value_at = (1 - core) * SLOTS + jnp.where(second, places[0], places[1])
    blank = jnp.zeros((PAD_SLOTS - SLOTS,), jnp.int32)
    meta = jnp.concatenate([key_at, blank, value_at, blank, hi, lo, zlo[None], doc_ends]).astype(
        jnp.int32
    )
    exponents = jnp.arange(half, dtype=F32) * (2.0 / HEAD)
    angles = positions.astype(F32)[:, None] * (1.0 / ROPE_BASE**exponents)[None, :]
    cosine, sine = jnp.cos(angles), jnp.sin(angles)

    half_rows, heads_b = ((2 * STRETCH, half), F32), ((2 * STRETCH, 2 * HEAD), BF)
    normed_b, mine, theirs = in_one(
        input_kernel,
        (((2 * STRETCH, D), BF), half_rows, half_rows),
        (stream, w_key, w_value, g_in),
        "input",
        spots=spots,
    )
    kind_b, kind = in_one(
        kind_kernel,
        (((2 * STRETCH, HEAD), BF), ((2 * STRETCH, HEAD), F32)),
        (mine, hop(theirs, "wt", 1), cosine, sine, gain_key[None, :]),
        "kind",
        spots=spots,
    )

    across = hop(kind_b, "ctx", 4)
    groups = []
    for h, one in enumerate((1, 8)):
        rows = slice(h * STRETCH, (h + 1) * STRETCH)
        block = jnp.concatenate([kind_b[rows], across[rows]], axis=0)
        groups.append([block] + [hop(block, "ctx", k * one) for k in (1, 2, 3)])
    quads = in_one(lay_kernel, (((1024, HEAD), BF),) * 2, (*groups[0], *groups[1]), "lay")
    pieces = ring_gather(quads[0], 8, 24) + ring_gather(quads[1], 1, 3)
    pieces += [hop(piece, "wt", 1) for piece in pieces]
    pieces = [piece.reshape(-1, STRETCH, HEAD) for piece in pieces]

    (pack,) = in_one(
        pack_kernel,
        (((176, D), BF),),
        (laurel_left, laurel_right, join_gate, join_proj, layer_input),
        "pack",
        (quads[0],),
    )
    packs = lax.all_gather(pack, "wt", axis=0)

    query_b, query_raw = in_one(
        query_kernel,
        (heads_b, ((2 * STRETCH, 2 * HEAD), F32)),
        (normed_b, w_query, cosine, sine, gain_query[None, :]),
        "query",
        (pieces[0],),
    )

    attn_b, attn_full, lse, kept, sent = attend_forward(meta, query_b, w_attn_out, pieces)

    kept, came = scatter_wt(kept, sent)

    def from_packs(first, last):
        return jnp.concatenate([pick(packs, wt ^ k, 0)[first:last] for k in range(4)], axis=0)

    left_t, right_w = from_packs(0, 16), from_packs(16, 32)
    gate_t, proj_w = from_packs(32, 96), from_packs(96, 160)
    inputs = packs[:, 160:, :1024].reshape(4, 16, 4, 256).transpose(0, 2, 1, 3)
    inputs = lax.dynamic_slice_in_dim(inputs.reshape(4, 64, 256), starts(0), 64, 2)
    inputs = jnp.concatenate([pick(inputs, wt ^ k, 0) for k in range(4)], axis=0).T
    normed_group = gather_group(normed_b, GROUP_X)
    wide_f, wide_b = ((64, D), F32), ((64, D), BF)
    pre_b, resid, attn_sum, laurel_sum, laurel_mid = in_one(
        mid_kernel,
        (wide_b, wide_f, wide_f, wide_f, ((64, 64), F32)),
        (kept, came, stream_own, left_t, right_w, g_in, g_attn, g_laurel, g_pre),
        "mid",
    )

    gate_pre, up_pre, pre_all, act_b, kept, sent = ff_forward(
        gather_wt(pre_b), w_gate, w_up, w_down
    )
    kept, came = scatter_wt(kept, sent)
    pre_group = gather_group(pre_all, GROUP_X)
    act_group = gather_group(act_b, GROUP_Y)

    grad_ff, grad_after, results, gains_join, gates_mine, gates_sent = in_one(
        join_kernel,
        (
            wide_b,
            wide_f,
            ((64, D + 256), BF),
            ((8, D), F32),
            ((2, 128, D), BF),
            ((2, 128, D), BF),
        ),
        (kept, came, resid, grad_top, inputs, gate_t, proj_w, g_post, g_join),
        "join",
        (normed_group,),
    )

    grad_ff_parts = gather_wt(grad_ff)
    wide_cuts, down_cuts = ff_grads(where, grad_ff_parts, gate_pre, up_pre, w_down)
    kept, sent = ff_back(where, wide_cuts, w_gate, w_up)
    wide_cuts = [wide_cuts[0]] + [hop(wide_cuts[k], "ctx", k) for k in (1, 2, 3)]
    down_cuts = [down_cuts[0]] + [hop(down_cuts[k], "ctx", 8 * k) for k in (1, 2, 3)]
    kept, came = scatter_wt(kept, sent)

    grad_attn, branch, own_part, gains_resid, small_mine, small_sent = in_one(
        resid_kernel,
        (wide_b, wide_f, wide_f, ((8, D), F32), ((2, 160, D), BF), ((2, 160, D), BF)),
        (
            kept,
            came,
            resid,
            grad_after,
            attn_sum,
            laurel_sum,
            laurel_mid,
            stream_own,
            left_t,
            right_w,
            g_in,
            g_attn,
            g_laurel,
            g_pre,
            gates_mine,
            gates_sent,
        ),
        "resid",
        (pre_group,),
    )
    grad_attn_parts = gather_wt(grad_attn)

    grad_query_rot, grad_pieces = attend_backward(
        meta, query_b, attn_full, lse, w_attn_out, grad_attn_parts, pieces, *wide_cuts[1:]
    )
    wide = wide_product(where, pre_group, wide_cuts, grad_query_rot)
    def blocks(count, kind):
        return ((count, STRETCH, HEAD), kind)

    def hops(values, masks):
        return [hop(value, "ctx", mask) for value, mask in zip(values, masks)]

    own_far, own_rest, sent_far, sent_rest = grad_pieces
    came_rest = hop(sent_rest, "wt", 1)
    far = in_one(
        far_kernel,
        (blocks(4, BF),) * 4,
        (own_far, hop(sent_far, "wt", 1)),
        "far",
        (came_rest, wide),
    )
    wide = scatter_group(wide, GROUP_Y)
    down = down_product(where, act_group, down_cuts, far[0])
    grad_query_b, gain_query_part = in_one(
        query_back_kernel,
        (heads_b, ((1, HEAD), F32)),
        (grad_query_rot, query_raw, cosine, sine, gain_query[None, :]),
        "query_back",
        (far[0],),
    )
    bases = in_one(
        near_kernel,
        (blocks(8, F32),) * 2 + (blocks(8, BF),) * 4,
        (own_rest, came_rest, *hops(far, (8, 24, 1, 3))),
        "near",
    )
    (small_sent,) = hold((small_sent,), bases[2])
    small = small_mine.astype(F32) + hop(small_sent, "wt", 1).astype(F32)
    small_far = small[1].astype(BF)
    small = (small[0] + hop(small_far, "wt", 2).astype(F32)).astype(BF)
    down_event = down
    down = scatter_group(down, GROUP_Z).reshape(4, 64, -1)
    inner = in_one(
        inner_kernel,
        (blocks(2, F32),) * 2 + (blocks(2, BF),) * 6,
        (*bases[:2], *hops(bases[2:], (8, 24, 1, 3))),
        "inner",
        (grad_query_b, down_event),
    )
    last = in_one(
        last_kernel,
        (((STRETCH, HEAD), F32),) * 2 + (blocks(2, BF),),
        (*inner[:2], *hops(inner[2:], (1, 2, 3, 8, 16, 24))),
        "last",
    )
    across = hop(last[2], "ctx", 4)
    (turn,) = in_one(
        turn_kernel,
        (((D, 768), BF),),
        (small, attn_b, *grad_attn_parts),
        "turn",
        (last[2],),
        scratch=(pltpu.VMEM((2 * STRETCH, D), BF),),
    )
    turn_event = turn
    turn = scatter_group(turn, GROUP_Y)
    home, away, gain_key_part = in_one(
        kind_back_kernel,
        (((2 * STRETCH, half), BF), ((2 * STRETCH, half), BF), ((1, HEAD), F32)),
        (*last[:2], across, kind, cosine, sine, gain_key[None, :]),
        "kind_back",
        (turn_event,),
        spots=spots,
    )

    outs = in_one(
        normed_back_kernel,
        (((STRETCH, D), F32), ((STRETCH, D), BF), ((1, D), F32))
        + (((2 * STRETCH, 192), BF),) * 4,
        (home, hop(away, "wt", 1), grad_query_b, w_query, w_key, w_value, stream),
        "normed_back",
        (wide,),
        spots=spots,
    )
    def fold_z(value):
        value = value.reshape(2, 256, -1)
        return fold(pick(value, at_z, 0), pick(value, 1 - at_z, 0), 4)

    wide = fold_z(wide)
    turn = fold_z(turn)
    kept, sent, gain_input_part, token_cuts = outs[0], outs[1], outs[2], outs[3:]
    kept, came = scatter_wt(kept, sent)
    (stream_grad,) = in_one(
        final_kernel, (wide_b,), (kept, came, own_part, branch, stream_own, g_in), "final", (turn,)
    )

    first, near, core_rows, far_rows = gather_wt(stream_grad)
    stream_grad_all = natural([first, core_rows, near, far_rows]).astype(F32)
    heads = jnp.concatenate(
        [gain_query_part.reshape(32, 8), gain_key_part.reshape(32, 8), jnp.zeros((32, 48), F32)],
        axis=1,
    ).reshape(1, -1)
    line = jnp.arange(8)[:, None]
    late_gains = jnp.where(line == 0, heads, 0.0) + jnp.where(
        line == 1, gain_input_part, 0.0
    )
    late_gains = jnp.concatenate(
        [late_gains + jnp.roll(gains_join, 2, axis=0), gains_resid], axis=0
    )

    late_gains = late_gains + hop(late_gains, "wt", 1)
    late_gains = late_gains + hop(late_gains, "wt", 2)
    token_cuts = [token_cuts[0]] + [hop(token_cuts[k], "ctx", k) for k in (1, 2, 3)]
    (results,) = hold((results,), token_cuts[1])
    results = lax.all_gather(results, "wt", axis=0)
    layer_out_all = jnp.concatenate([results[i, :, :D] for i in (0, 2, 1, 3)]).astype(F32)
    grad_input_all = jnp.concatenate(
        [
            lax.dynamic_slice_in_dim(results[i], D + 64 * (wt ^ i), 64, 1)
            for i in (0, 2, 1, 3)
        ]
    ).astype(F32)

    (down,) = hold((down,), token_cuts[1])
    down = fold(down[:2], down[2:], 1)
    tokens = fold(*token_product(where, normed_group, late_gains.astype(BF), token_cuts), 8)
    tokens = fold(tokens[0], tokens[1], 24)
    tokens = fold(tokens[0], tokens[1], 4)
    shares = in_one(
        payload_kernel,
        (((64, 2048), BF),) * 4,
        (wide, tokens, turn),
        "payload",
        spots=(where,),
    )
    shares = [shares[0]] + [hop(shares[k], "ctx", k) for k in (1, 2, 3)]
    (
        grad_w_gate,
        grad_w_up,
        grad_w_query,
        grad_w_key,
        grad_w_value,
        grad_w_attn_out,
        grad_left,
        grad_right,
        grad_gate,
        grad_proj,
        gains,
        grad_w_down,
    ) = in_one(
        share_kernel,
        tuple(
            (shape, F32)
            for shape in (
                (64, D),
                (64, D),
                (64, 512),
                (64, half),
                (64, half),
                (64, 512),
                (16, 64),
                (16, 64),
                (64, 64),
                (64, 64),
                (64, 16),
                (64, D),
            )
        ),
        (*shares, down[0], hop(down[1], "ctx", 3)),
        "share",
        spots=(where,),
    )

    return (
        layer_out_all,
        stream_grad_all,
        grad_input_all,
        gains[:, 1] + gains[:, 11],
        gains[:8, 0],
        gains[8:16, 0],
        grad_w_query,
        grad_w_key,
        grad_w_value,
        grad_w_attn_out.T,
        gains[:, 8],
        grad_left.T,
        grad_right,
        gains[:, 9],
        gains[:, 10],
        grad_w_gate,
        grad_w_up,
        grad_w_down.T,
        gains[:, 2],
        grad_gate,
        grad_proj,
        gains[:, 3],
    )


def solution(mesh):
    rows, cols, tops = P("ctx", "wt"), P("wt", "ctx"), P("ctx")
    down, across = P(None, "wt"), P("wt", None)
    return jax.shard_map(
        local,
        mesh=mesh,
        in_specs=(
            P("ctx", None),
            P("ctx", "wt"),
            P("ctx", None),
            P(),
            P(),
            P(),
            P(),
            P(),
            down,
            down,
            down,
            across,
            P(),
            down,
            across,
            P(),
            P(),
            down,
            down,
            across,
            P(),
            down,
            across,
            P(),
        ),
        out_specs=(
            P("ctx", None),
            P("ctx", None),
            rows,
            tops,
            tops,
            tops,
            rows,
            rows,
            rows,
            cols,
            tops,
            rows,
            cols,
            tops,
            tops,
            rows,
            rows,
            cols,
            tops,
            rows,
            cols,
            tops,
        ),
        check_vma=False,
    )
```

profile of v0, /device:TPU:1, one launch (start us, length us, event | category | flops | bytes accessed | tf_op | source)
XLA Modules:
  0.0 494.0 jit_solution(8032425585648186494)
XLA Ops:
  7.9 3.2 input.1
  18.4 3.7 collective-permute-start.1
  23.0 3.2 collective-permute-done.1
  27.6 2.6 collective-permute-start.6
  31.5 2.4 collective-permute-start.3
  38.6 2.8 collective-permute-done.4.refs_3_
  42.1 2.3 lay.1
  44.4 2.7 pack.1
  48.0 2.7 collective-permute-start.9
  51.7 2.2 collective-permute-start.16
  54.0 5.9 %collective-permute-done.8 = bf16[1024,256]{1,0:T(8,128)(2,1)S(1)} collective-permute-done((bf16[1024,256]{1,0:T(8,128)(2,1)S(1)}, bf16[1024,256]{1,0:T(8,128)(2,1)S(1)}, u32[]{:S(2)}, u32[]{:S(2)}) %collective-permute-start.8) | collective-permute-done | bytes 524320 | tf_op jit(solution)/shard_map/ppermute | solution.py:25
  59.9 2.7 collective-permute-start.10
  63.4 2.8 collective-permute-start.21
  72.0 3.3 collective-permute-done.14
  80.2 3.5 query.1
  84.7 8.6 %attend_forward.1 = (bf16[256,512]{1,0:T(8,128)(2,1)}, f32[256,512]{1,0:T(8,128)}, f32[2,8,256]{2,1,0:T(8,128)}, f32[128,2048]{1,0:T(8,128)}, bf16[128,2048]{1,0:T(8,128)(2,1)}) custom-call(s32[157]{0:T(256)} %concatenate.52.meta, bf16[256,512]{1,0:T(8,128)(2,1)} %get-tuple-element.130.q_ref, bf16[512,2048]{1,0:T(8,128)(2,1)} %w_ref.3, ...), custom_call_target="tpu_custom_call" | custom-call | flops 3000000000 | bytes 10000000 | tf_op jit(solution)/shard_map/attend_forward/pallas_call | solution.py:317
  100.3 5.1 %collective-permute-done.27.came = bf16[64,2048]{1,0:T(8,128)(2,1)S(1)} collective-permute-done((bf16[64,2048]{1,0:T(8,128)(2,1)S(1)}, bf16[64,2048]{1,0:T(8,128)(2,1)S(1)}, u32[]{:S(2)}, u32[]{:S(2)}) %collective-permute-start.27) | collective-permute-done | bytes 262176 | tf_op jit(solution)/shard_map/ppermute | solution.py:25
  106.1 3.4 mid.1
  111.4 5.1 %collective-permute-done.28.refs_1_ = bf16[64,2048]{1,0:T(8,128)(2,1)S(1)} collective-permute-done((bf16[64,2048]{1,0:T(8,128)(2,1)}, bf16[64,2048]{1,0:T(8,128)(2,1)S(1)}, u32[]{:S(2)}, u32[]{:S(2)}) %collective-permute-start.28) | collective-permute-done | bytes 262176 | tf_op jit(solution)/shard_map/ppermute | solution.py:25
  120.3 15.8 %ff_forward.1 = (f32[256,2048]{1,0:T(8,128)}, f32[256,2048]{1,0:T(8,128)}, bf16[256,2048]{1,0:T(8,128)(2,1)}, bf16[256,2048]{1,0:T(8,128)(2,1)}, f32[128,2048]{1,0:T(8,128)}, /*index=5*/bf16[128,2048]{1,0:T(8,128)(2,1)}) custom-call(bf16[64,2048]{1,0:T(8,128)(2,1)} %get-tuple-element.134.refs_0_, bf16[64,2048]{1,0:T(8,128)(2,1)} %copy-done.17, ...), custom_call_target="tpu_custom_call" | custom-call | flops 6442450944 | bytes 30000000 | tf_op jit(solution)/shard_map/ff_forward/pallas_call | solution.py:402
  145.4 4.9 collective-permute-done.32.came
  151.0 8.2 %join.1 = (bf16[64,2048]{1,0:T(8,128)(2,1)}, f32[64,2048]{1,0:T(8,128)}, bf16[64,2304]{1,0:T(8,128)(2,1)}, f32[8,2048]{1,0:T(8,128)}, bf16[2,128,2048]{2,1,0:T(8,128)(2,1)}, /*index=5*/bf16[2,128,2048]{2,1,0:T(8,128)(2,1)}) custom-call(f32[64,2048]{1,0:T(8,128)} %slice.331.kept, bf16[64,2048]{1,0:T(8,128)(2,1)} %copy-done.31, ...), custom_call_target="tpu_custom_call" | custom-call | flops 1000000000 | bytes 5000000 | tf_op jit(solution)/shard_map/join/pallas_call | solution.py:767
  161.0 5.4 %collective-permute-done.33.refs_1_ = bf16[64,2048]{1,0:T(8,128)(2,1)S(1)} collective-permute-done((bf16[64,2048]{1,0:T(8,128)(2,1)}, bf16[64,2048]{1,0:T(8,128)(2,1)S(1)}, u32[]{:S(2)}, u32[]{:S(2)}) %collective-permute-start.33) | collective-permute-done | bytes 262176 | tf_op jit(solution)/shard_map/ppermute | solution.py:25
  170.4 11.0 %ff_grads.1 = (bf16[256,1024]{1,0:T(8,128)(2,1)}, bf16[256,1024]{1,0:T(8,128)(2,1)}, bf16[256,1024]{1,0:T(8,128)(2,1)}, bf16[256,1024]{1,0:T(8,128)(2,1)}, bf16[...) custom-call(s32[3]{0:T(128)} %pad_add_fusion.me.where, ...), custom_call_target="tpu_custom_call" | custom-call | flops 2147483648 | bytes 10000000 | tf_op jit(solution)/shard_map/ff_grads/pallas_call | solution.py:460
  181.4 11.0 %ff_back.1 = (f32[128,2048]{1,0:T(8,128)}, bf16[128,2048]{1,0:T(8,128)(2,1)}) custom-call(s32[3]{0:T(128)} %pad_add_fusion.me.where, bf16[256,1024]{1,0:T(8,128)(2,1)} %get-tuple-element.144.refs_0_, bf16[256,1024]{1,0:T(8,128)(2,1)} %get-tuple-element.145.refs_1_, bf16[256,1024]{1,0:T(8,128)(2,1)} %get-tuple-element.146.refs_2_, ...), custom_call_target="tpu_custom_call" | custom-call | flops 4294967296 | bytes 20000000 | tf_op jit(solution)/shard_map/ff_back/pallas_call | solution.py:506
  204.4 6.0 %resid.1 = (bf16[64,2048]{1,0:T(8,128)(2,1)}, f32[64,2048]{1,0:T(8,128)}, f32[64,2048]{1,0:T(8,128)}, f32[8,2048]{1,0:T(8,128)}, bf16[2,160,2048]{2,1,0:T(8,128)(2,1)}, /*index=5*/bf16[2,160,2048]{2,1,0:T(8,128)(2,1)}) custom-call(f32[64,2048]{1,0:T(8,128)} %slice.334.kept, bf16[64,2048]{1,0:T(8,128)(2,1)} %copy-done.28, ...), custom_call_target="tpu_custom_call" | custom-call | flops 1000000000 | bytes 5000000 | tf_op jit(solution)/shard_map/resid/pallas_call | solution.py:767
  212.4 5.0 %collective-permute-done.38.refs_1_ = bf16[64,2048]{1,0:T(8,128)(2,1)S(1)} collective-permute-done((bf16[64,2048]{1,0:T(8,128)(2,1)}, bf16[64,2048]{1,0:T(8,128)(2,1)S(1)}, u32[]{:S(2)}, u32[]{:S(2)}) %collective-permute-start.38) | collective-permute-done | bytes 262176 | tf_op jit(solution)/shard_map/ppermute | solution.py:25
  219.3 3.8 collective-permute-done.42.refs_25_.refs_2_
  226.3 11.7 %attend_backward.1 = (f32[256,512]{1,0:T(8,128)}, bf16[16,128,256]{2,1,0:T(8,128)(2,1)}, bf16[48,128,256]{2,1,0:T(8,128)(2,1)}, bf16[16,128,256]{2,1,0:T(8,128)(2,1)}, bf16[48,128,256]{2,1,0:T(8,128)(2,1)}) custom-call(s32[157]{0:T(256)} %concatenate.52.meta, bf16[256,512]{1,0:T(8,128)(2,1)} %get-tuple-element.130.q_ref, ...), custom_call_target="tpu_custom_call" | custom-call | flops 10000000000 | bytes 20000000 | tf_op jit(solution)/shard_map/attend_backward/pallas_call | solution.py:344
  238.0 9.3 %wide_product.1.refs_1_ = bf16[2048,1024]{1,0:T(8,128)(2,1)} custom-call(s32[3]{0:T(128)} %pad_add_fusion.me.where, bf16[4,256,2048]{2,1,0:T(8,128)(2,1)} %bitcast.160, bf16[256,1024]{1,0:T(8,128)(2,1)} %get-tuple-element.144.refs_0_, bf16[256,1024]{1,0:T(8,128)(2,1)} %copy-done.54, bf16[256,1024]{1,0:T(8,128)(2,1)} %copy-done.55, ...), custom_call_target="tpu_custom_call" | custom-call | flops 5000000000 | bytes 10000000 | tf_op jit(solution)/shard_map/wide_product/pallas_call | solution.py:815
  249.5 7.2 %collective-permute-start.54 = (bf16[256,512]{1,0:T(8,128)(2,1)}, bf16[256,512]{1,0:T(8,128)(2,1)S(1)}, u32[]{:S(2)}, u32[]{:S(2)}) collective-permute-start(bf16[256,512]{1,0:T(8,128)(2,1)} %get-tuple-element.177), channel_id=1, source_target_pairs={{0,32},{4,36},{8,40},{12,44},{16,48},{20,52},{24,56},{28,60},{32,0... | collective-permute-start | bytes 786440 | tf_op jit(solution)/shard_map/ppermute | solution.py:25
  261.8 2.6 far.1
  264.3 4.9 collective-permute-start.46
  273.0 7.5 %collective-permute-start.49 = (bf16[4,128,256]{2,1,0:T(8,128)(2,1)}, bf16[4,128,256]{2,1,0:T(8,128)(2,1)S(1)}, u32[]{:S(2)}, u32[]{:S(2)}) collective-permute-start(bf16[4,128,256]{2,1,0:T(8,128)(2,1)} %get-tuple-element.166), channel_id=1, source_target_pairs={{0,12},{4,8},{8,4},{12,0},{16,28},{20,24},{24,20},{28,16},{32,44},... | collective-permute-start | bytes 786440 | tf_op jit(solution)/shard_map/ppermute | solution.py:25
  280.5 6.2 %down_product.1.refs_5_ = bf16[2,4,64,2048]{3,2,1,0:T(8,128)(2,1)} custom-call(s32[3]{0:T(128)} %pad_add_fusion.me.where, bf16[4,256,2048]{2,1,0:T(8,128)(2,1)} %bitcast.209, bf16[256,512]{1,0:T(8,128)(2,1)} %get-tuple-element.176.refs_0_, bf16[256,512]{1,0:T(8,128)(2,1)} %copy-done.66, bf16[256,512]{1,0:T(8,128)(2,1)} %copy-done.67, ...), custom_call_target="tpu_custom_call" | custom-call | flops 3000000000 | bytes 10000000 | tf_op jit(solution)/shard_map/down_product/pallas_call | solution.py:928
  287.8 5.3 %near.1 = (f32[8,128,256]{2,1,0:T(8,128)}, f32[8,128,256]{2,1,0:T(8,128)}, bf16[8,128,256]{2,1,0:T(8,128)(2,1)}, bf16[8,128,256]{2,1,0:T(8,128)(2,1)}, bf16[8,12...) custom-call(bf16[48,128,256]{2,1,0:T(8,128)(2,1)} %get-tuple-element.158.own, bf16[48,128,256]{2,1,0:T(8,128)(2,1)} %copy-done.2, ...), custom_call_target="tpu_custom_call" | custom-call | flops 1000000000 | bytes 5000000 | tf_op jit(solution)/shard_map/near/pallas_call | solution.py:767
  293.1 2.9 collective-permute-start.64
  298.0 4.3 collective-permute-start.53
  303.7 2.3 query_back.1
  306.0 14.1 %collective-permute-done.50.refs_0_ = bf16[8,128,256]{2,1,0:T(8,128)(2,1)} collective-permute-done((bf16[8,128,256]{2,1,0:T(8,128)(2,1)}, bf16[8,128,256]{2,1,0:T(8,128)(2,1)}, u32[]{:S(2)}, u32[]{:S(2)}) %collective-permute-start.50) | collective-permute-done | bytes 524320 | tf_op jit(solution)/shard_map/ppermute | solution.py:25
  320.0 3.9 collective-permute-done.51.refs_1_
  323.9 3.2 inner.1
  327.2 3.8 collective-permute-start.58
  331.8 2.7 collective-permute-start.61
  334.5 2.3 collective-permute-done.58.refs_1_
  339.4 3.7 collective-permute-done.62.refs_5_
  345.1 2.3 collective-permute-start.63
  348.5 4.2 turn.1.event
  357.2 2.8 collective-permute-start.66
  361.7 5.0 %normed_back.1 = (f32[128,2048]{1,0:T(8,128)}, bf16[128,2048]{1,0:T(8,128)(2,1)}, f32[1,2048]{1,0:T(1,128)}, bf16[256,192]{1,0:T(8,128)(2,1)}, bf16[256,192]{1,0...) custom-call(s32[6]{0:T(128)} %stack.52.spots, bf16[256,128]{1,0:T(8,128)(2,1)} %get-tuple-element.195.home, ...), custom_call_target="tpu_custom_call" | custom-call | flops 1000000000 | bytes 5000000 | tf_op jit(solution)/shard_map/normed_back/pallas_call | solution.py:767
  366.7 4.9 collective-permute-done.67.refs_1_
  388.2 5.0 %token_product.1 = (bf16[2,2,256,256]{3,2,1,0:T(8,128)(2,1)}, bf16[2,2,256,256]{3,2,1,0:T(8,128)(2,1)}) custom-call(s32[3]{0:T(128)} %pad_add_fusion.me.where, bf16[4,256,2048]{2,1,0:T(8,128)(2,1)} %bitcast.156, bf16[16,2048]{1,0:T(8,128)(2,1)} %add_convert_fusion.2.gains, bf16[256,192]{1,0:T(8,128)(2,1)} %get-tuple-element.207.refs_0_, ...), custom_call_target="tpu_custom_call" | custom-call | flops 1000000000 | bytes 6000000 | tf_op jit(solution)/shard_map/token_product/pallas_call | solution.py:856
  393.3 12.2 %collective-permute-done.74 = bf16[256,1024]{1,0:T(8,128)(2,1)} collective-permute-done((bf16[256,1024]{1,0:T(8,128)(2,1)}, bf16[256,1024]{1,0:T(8,128)(2,1)}, u32[]{:S(2)}, u32[]{:S(2)}) %collective-permute-start.74) | collective-permute-done | bytes 524320 | tf_op jit(solution)/shard_map/ppermute | solution.py:25
  409.3 2.6 collective-permute-start.80
  412.0 7.5 %collective-permute-done.80 = bf16[2,256,256]{2,1,0:T(8,128)(2,1)S(1)} collective-permute-done((bf16[2,256,256]{2,1,0:T(8,128)(2,1)S(1)}, bf16[2,256,256]{2,1,0:T(8,128)(2,1)S(1)}, u32[]{:S(2)}, u32[]{:S(2)}) %collective-permute-start.80) | collective-permute-done | bytes 262176 | tf_op jit(solution)/shard_map/ppermute | solution.py:25
  422.3 2.8 collective-permute-done.81
  428.2 17.4 %reduce-scatter.6.cloned.1.call-done = bf16[512,768]{1,0:T(8,128)(2,1)} async-done(((bf16[2048,768]{1,0:T(8,128)(2,1)}), bf16[512,768]{1,0:T(8,128)(2,1)}) %reduce-scatter.6.cloned.1.call-update) | async-done | bytes 786448 | tf_op jit(solution)/shard_map/reduce_scatter | solution.py:46
  448.5 10.1 %collective-permute-done.70 = bf16[256,768]{1,0:T(8,128)(2,1)S(1)} collective-permute-done((bf16[256,768]{1,0:T(8,128)(2,1)S(1)}, bf16[256,768]{1,0:T(8,128)(2,1)S(1)}, u32[]{:S(2)}, u32[]{:S(2)}) %collective-permute-start.70) | collective-permute-done | bytes 393248 | tf_op jit(solution)/shard_map/ppermute | solution.py:25
  459.5 2.4 payload.1
  462.1 2.2 collective-permute-start.83
  466.4 2.5 final.1
  471.3 2.4 collective-permute-start.71
  474.9 3.0 collective-permute-start.73
  478.8 2.8 share.1
  (421 shorter events, 149.3 us)
Async XLA Ops:
  7.2 91.1 %all-gather.11.cloned.1.call-start = ((), (), s32[]{:S(2)}) async-start(), calls=%async_computation.6 | async-start | bytes 3604480 | tf_op jit(solution)/shard_map/all_gather | solution.py:1053
  27.6 9.3 %collective-permute-start.6 = (bf16[256,256]{1,0:T(8,128)(2,1)S(1)}, bf16[256,256]{1,0:T(8,128)(2,1)S(1)}, u32[]{:S(2)}, u32[]{:S(2)}) collective-permute-start(bf16[256,256]{1,0:T(8,128)(2,1)S(1)} %pad_maximum_fusion.6.refs_4_), channel_id=1, source_target_pairs={{0,64},{4,68},{8,72},{12,76},{16,80},{20,84},{24,88},{28,92},{32,9... | collective-permute-start | bytes 393224 | tf_op jit(solution)/shard_map/ppermute | solution.py:25
  30.2 8.3 %collective-permute-start.7 = (bf16[256,256]{1,0:T(8,128)(2,1)S(1)}, bf16[256,256]{1,0:T(8,128)(2,1)S(1)}, u32[]{:S(2)}, u32[]{:S(2)}) collective-permute-start(bf16[256,256]{1,0:T(8,128)(2,1)S(1)} %pad_maximum_fusion.6.refs_4_), channel_id=1, source_target_pairs={{0,96},{4,100},{8,104},{12,108},{16,112},{20,116},{24,120},{28,124... | collective-permute-start | bytes 393224 | tf_op jit(solution)/shard_map/ppermute | solution.py:25
  30.2 8.3 %collective-permute-start.2 = (bf16[256,256]{1,0:T(8,128)(2,1)S(1)}, bf16[256,256]{1,0:T(8,128)(2,1)S(1)}, u32[]{:S(2)}, u32[]{:S(2)}) collective-permute-start(bf16[256,256]{1,0:T(8,128)(2,1)S(1)} %pad_maximum_fusion.5.refs_0_), channel_id=1, source_target_pairs={{0,4},{4,0},{8,12},{12,8},{16,20},{20,16},{24,28},{28,24},{32,36},... | collective-permute-start | bytes 393224 | tf_op jit(solution)/shard_map/ppermute | solution.py:25
  47.1 103.1 %all-gather.13.cloned.1.call-start = ((), (), s32[]{:S(2)}) async-start(), calls=%async_computation.7 | async-start | bytes 5242880 | tf_op jit(solution)/shard_map/all_gather | solution.py:42
  47.9 155.8 %all-gather.15.cloned.1.call-start = ((), (), s32[]{:S(2)}) async-start(), calls=%async_computation.8 | async-start | bytes 5242880 | tf_op jit(solution)/shard_map/all_gather | solution.py:42
  48.0 11.9 %collective-permute-start.8 = (bf16[1024,256]{1,0:T(8,128)(2,1)S(1)}, bf16[1024,256]{1,0:T(8,128)(2,1)S(1)}, u32[]{:S(2)}, u32[]{:S(2)}) collective-permute-start(bf16[1024,256]{1,0:T(8,128)(2,1)S(1)} %copy-done.12), channel_id=1, source_target_pairs={{0,32},{4,36},{8,40},{12,44},{16,48},{20,52},{24,56},{28,60},{32,0... | collective-permute-start | bytes 1572872 | tf_op jit(solution)/shard_map/ppermute | solution.py:25
  48.0 14.5 %collective-permute-start.9 = (bf16[1024,256]{1,0:T(8,128)(2,1)S(1)}, bf16[1024,256]{1,0:T(8,128)(2,1)S(1)}, u32[]{:S(2)}, u32[]{:S(2)}) collective-permute-start(bf16[1024,256]{1,0:T(8,128)(2,1)S(1)} %copy-done.12), channel_id=1, source_target_pairs={{0,96},{4,100},{8,104},{12,108},{16,112},{20,116},{24,120},{28,124... | collective-permute-start | bytes 1572872 | tf_op jit(solution)/shard_map/ppermute | solution.py:25
  50.7 11.9 %collective-permute-start.12 = (bf16[1024,256]{1,0:T(8,128)(2,1)}, bf16[1024,256]{1,0:T(8,128)(2,1)S(1)}, u32[]{:S(2)}, u32[]{:S(2)}) collective-permute-start(bf16[1024,256]{1,0:T(8,128)(2,1)} %get-tuple-element.131), channel_id=1, source_target_pairs={{0,4},{4,0},{8,12},{12,8},{16,20},{20,16},{24,28},{28,24},{32,36},... | collective-permute-start | bytes 1572872 | tf_op jit(solution)/shard_map/ppermute | solution.py:25
  50.7 15.4 %collective-permute-start.13 = (bf16[1024,256]{1,0:T(8,128)(2,1)}, bf16[1024,256]{1,0:T(8,128)(2,1)S(1)}, u32[]{:S(2)}, u32[]{:S(2)}) collective-permute-start(bf16[1024,256]{1,0:T(8,128)(2,1)} %get-tuple-element.131), channel_id=1, source_target_pairs={{0,12},{4,8},{8,4},{12,0},{16,28},{20,24},{24,20},{28,16},{32,44},... | collective-permute-start | bytes 1572872 | tf_op jit(solution)/shard_map/ppermute | solution.py:25
  51.7 16.8 %collective-permute-start.16 = (bf16[1024,256]{1,0:T(8,128)(2,1)S(1)}, bf16[1024,256]{1,0:T(8,128)(2,1)}, u32[]{:S(2)}, u32[]{:S(2)}) collective-permute-start(bf16[1024,256]{1,0:T(8,128)(2,1)S(1)} %copy-done.12), channel_id=1, source_target_pairs={{0,1},{1,0},{2,3},{3,2},{4,5},{5,4},{6,7},{7,6},{8,9},{9,8},{10,11... | collective-permute-start | bytes 1572872 | tf_op jit(solution)/shard_map/ppermute | solution.py:25
  59.9 8.8 %collective-permute-start.10 = (bf16[512,256]{1,0:T(8,128)(2,1)S(1)}, bf16[512,256]{1,0:T(8,128)(2,1)S(1)}, u32[]{:S(2)}, u32[]{:S(2)}) collective-permute-start(bf16[512,256]{1,0:T(8,128)(2,1)S(1)} %slice.325), channel_id=1, source_target_pairs={{0,96},{4,100},{8,104},{12,108},{16,112},{20,116},{24,120},{28,124... | collective-permute-start | bytes 786440 | tf_op jit(solution)/shard_map/ppermute | solution.py:25
  63.4 13.2 %collective-permute-start.21 = (bf16[1024,256]{1,0:T(8,128)(2,1)}, bf16[1024,256]{1,0:T(8,128)(2,1)}, u32[]{:S(2)}, u32[]{:S(2)}) collective-permute-start(bf16[1024,256]{1,0:T(8,128)(2,1)} %get-tuple-element.131), channel_id=1, source_target_pairs={{0,1},{1,0},{2,3},{3,2},{4,5},{5,4},{6,7},{7,6},{8,9},{9,8},{10,11... | collective-permute-start | bytes 1572872 | tf_op jit(solution)/shard_map/ppermute | solution.py:25
  66.2 9.1 %collective-permute-start.14 = (bf16[512,256]{1,0:T(8,128)(2,1)S(1)}, bf16[512,256]{1,0:T(8,128)(2,1)}, u32[]{:S(2)}, u32[]{:S(2)}) collective-permute-start(bf16[512,256]{1,0:T(8,128)(2,1)S(1)} %slice.327), channel_id=1, source_target_pairs={{0,12},{4,8},{8,4},{12,0},{16,28},{20,24},{24,20},{28,16},{32,44},... | collective-permute-start | bytes 786440 | tf_op jit(solution)/shard_map/ppermute | solution.py:25
  68.6 8.0 %collective-permute-start.15 = (bf16[512,256]{1,0:T(8,128)(2,1)S(1)}, bf16[512,256]{1,0:T(8,128)(2,1)}, u32[]{:S(2)}, u32[]{:S(2)}) collective-permute-start(bf16[512,256]{1,0:T(8,128)(2,1)S(1)} %slice.328), channel_id=1, source_target_pairs={{0,4},{4,0},{8,12},{12,8},{16,20},{20,16},{24,28},{28,24},{32,36},... | collective-permute-start | bytes 786440 | tf_op jit(solution)/shard_map/ppermute | solution.py:25
  68.7 8.8 %collective-permute-start.19 = (bf16[512,256]{1,0:T(8,128)(2,1)S(1)}, bf16[512,256]{1,0:T(8,128)(2,1)}, u32[]{:S(2)}, u32[]{:S(2)}) collective-permute-start(bf16[512,256]{1,0:T(8,128)(2,1)S(1)} %collective-permute-done.10), channel_id=1, source_target_pairs={{0,1},{1,0},{2,3},{3,2},{4,5},{5,4},{6,7},{7,6},{8,9},{9,8},{10,11... | collective-permute-start | bytes 786440 | tf_op jit(solution)/shard_map/ppermute | solution.py:25
  110.0 8.4 %collective-permute-start.29 = (bf16[64,2048]{1,0:T(8,128)(2,1)}, bf16[64,2048]{1,0:T(8,128)(2,1)S(1)}, u32[]{:S(2)}, u32[]{:S(2)}) collective-permute-start(bf16[64,2048]{1,0:T(8,128)(2,1)} %get-tuple-element.134.refs_0_), channel_id=1, source_target_pairs={{0,1},{1,0},{2,3},{3,2},{4,5},{5,4},{6,7},{7,6},{8,9},{9,8},{10,11... | collective-permute-start | bytes 786440 | tf_op jit(solution)/shard_map/ppermute | solution.py:25
  136.1 144.4 %all-gather.17.cloned.1.call-start = ((), (), s32[]{:S(2)}) async-start(), calls=%async_computation.9 | async-start | bytes 5242880 | tf_op jit(solution)/shard_map/all_gather | solution.py:42
  136.7 224.4 %reduce-scatter.4.cloned.1.call-start = ((), (), s32[]{:S(2)}) async-start(), calls=%async_computation.3 | async-start | bytes 5242880 | tf_op jit(solution)/shard_map/reduce_scatter | solution.py:46
  142.4 7.8 %collective-permute-start.32 = (bf16[64,2048]{1,0:T(8,128)(2,1)S(1)}, bf16[64,2048]{1,0:T(8,128)(2,1)S(1)}, u32[]{:S(2)}, u32[]{:S(2)}) collective-permute-start(bf16[64,2048]{1,0:T(8,128)(2,1)S(1)} %slice.394), channel_id=1, source_target_pairs={{0,2},{1,3},{2,0},{3,1},{4,6},{5,7},{6,4},{7,5},{8,10},{9,11},{10,... | collective-permute-start | bytes 786440 | tf_op jit(solution)/shard_map/ppermute | solution.py:25
  159.8 9.3 %collective-permute-start.34 = (bf16[64,2048]{1,0:T(8,128)(2,1)}, bf16[64,2048]{1,0:T(8,128)(2,1)S(1)}, u32[]{:S(2)}, u32[]{:S(2)}) collective-permute-start(bf16[64,2048]{1,0:T(8,128)(2,1)} %get-tuple-element.141.refs_0_), channel_id=1, source_target_pairs={{0,1},{1,0},{2,3},{3,2},{4,5},{5,4},{6,7},{7,6},{8,9},{9,8},{10,11... | collective-permute-start | bytes 786440 | tf_op jit(solution)/shard_map/ppermute | solution.py:25
  196.7 22.6 %collective-permute-start.41 = (bf16[256,1024]{1,0:T(8,128)(2,1)S(1)}, bf16[256,1024]{1,0:T(8,128)(2,1)S(1)}, u32[]{:S(2)}, u32[]{:S(2)}) collective-permute-start(bf16[256,1024]{1,0:T(8,128)(2,1)S(1)} %copy-done.15), channel_id=1, source_target_pairs={{0,4},{4,0},{8,12},{12,8},{16,20},{20,16},{24,28},{28,24},{32,36},... | collective-permute-start | bytes 1572872 | tf_op jit(solution)/shard_map/ppermute | solution.py:25
  198.4 24.7 %collective-permute-start.42 = (bf16[256,1024]{1,0:T(8,128)(2,1)S(1)}, bf16[256,1024]{1,0:T(8,128)(2,1)S(1)}, u32[]{:S(2)}, u32[]{:S(2)}) collective-permute-start(bf16[256,1024]{1,0:T(8,128)(2,1)S(1)} %copy-done.14), channel_id=1, source_target_pairs={{0,8},{4,12},{8,0},{12,4},{16,24},{20,28},{24,16},{28,20},{32,40},... | collective-permute-start | bytes 1572872 | tf_op jit(solution)/shard_map/ppermute | solution.py:25
  200.5 24.8 %collective-permute-start.43 = (bf16[256,1024]{1,0:T(8,128)(2,1)S(1)}, bf16[256,1024]{1,0:T(8,128)(2,1)S(1)}, u32[]{:S(2)}, u32[]{:S(2)}) collective-permute-start(bf16[256,1024]{1,0:T(8,128)(2,1)S(1)} %copy-done.13), channel_id=1, source_target_pairs={{0,12},{4,8},{8,4},{12,0},{16,28},{20,24},{24,20},{28,16},{32,44},... | collective-permute-start | bytes 1572872 | tf_op jit(solution)/shard_map/ppermute | solution.py:25
  211.0 14.3 %collective-permute-start.39 = (bf16[64,2048]{1,0:T(8,128)(2,1)}, bf16[64,2048]{1,0:T(8,128)(2,1)S(1)}, u32[]{:S(2)}, u32[]{:S(2)}) collective-permute-start(bf16[64,2048]{1,0:T(8,128)(2,1)} %get-tuple-element.157.refs_0_), channel_id=1, source_target_pairs={{0,1},{1,0},{2,3},{3,2},{4,5},{5,4},{6,7},{7,6},{8,9},{9,8},{10,11... | collective-permute-start | bytes 786440 | tf_op jit(solution)/shard_map/ppermute | solution.py:25
  217.4 7.9 %collective-permute-start.40 = (bf16[64,2048]{1,0:T(8,128)(2,1)S(1)}, bf16[64,2048]{1,0:T(8,128)(2,1)S(1)}, u32[]{:S(2)}, u32[]{:S(2)}) collective-permute-start(bf16[64,2048]{1,0:T(8,128)(2,1)S(1)} %collective-permute-done.38.refs_1_), channel_id=1, source_target_pairs={{0,1},{1,0},{2,3},{3,2},{4,5},{5,4},{6,7},{7,6},{8,9},{9,8},{10,11... | collective-permute-start | bytes 786440 | tf_op jit(solution)/shard_map/ppermute | solution.py:25
  247.2 137.0 %reduce-scatter.8.cloned.1.call-start = ((), (), s32[]{:S(2)}) async-start(), calls=%async_computation.5 | async-start | bytes 3145728 | tf_op jit(solution)/shard_map/reduce_scatter | solution.py:46
  247.3 11.8 %collective-permute-start.44 = (bf16[48,128,256]{2,1,0:T(8,128)(2,1)}, bf16[48,128,256]{2,1,0:T(8,128)(2,1)S(1)}, u32[]{:S(2)}, u32[]{:S(2)}) collective-permute-start(bf16[48,128,256]{2,1,0:T(8,128)(2,1)} %get-tuple-element.159), channel_id=1, source_target_pairs={{0,1},{1,0},{2,3},{3,2},{4,5},{5,4},{6,7},{7,6},{8,9},{9,8},{10,11... | collective-permute-start | bytes 9437192 | tf_op jit(solution)/shard_map/ppermute | solution.py:25
  249.4 9.7 %collective-permute-start.45 = (bf16[16,128,256]{2,1,0:T(8,128)(2,1)}, bf16[16,128,256]{2,1,0:T(8,128)(2,1)S(1)}, u32[]{:S(2)}, u32[]{:S(2)}) collective-permute-start(bf16[16,128,256]{2,1,0:T(8,128)(2,1)} %get-tuple-element.161), channel_id=1, source_target_pairs={{0,1},{1,0},{2,3},{3,2},{4,5},{5,4},{6,7},{7,6},{8,9},{9,8},{10,11... | collective-permute-start | bytes 3145736 | tf_op jit(solution)/shard_map/ppermute | solution.py:25
  249.5 21.6 %collective-permute-start.54 = (bf16[256,512]{1,0:T(8,128)(2,1)}, bf16[256,512]{1,0:T(8,128)(2,1)S(1)}, u32[]{:S(2)}, u32[]{:S(2)}) collective-permute-start(bf16[256,512]{1,0:T(8,128)(2,1)} %get-tuple-element.177), channel_id=1, source_target_pairs={{0,32},{4,36},{8,40},{12,44},{16,48},{20,52},{24,56},{28,60},{32,0... | collective-permute-start | bytes 786440 | tf_op jit(solution)/shard_map/ppermute | solution.py:25
  256.7 15.6 %collective-permute-start.55 = (bf16[256,512]{1,0:T(8,128)(2,1)}, bf16[256,512]{1,0:T(8,128)(2,1)S(1)}, u32[]{:S(2)}, u32[]{:S(2)}) collective-permute-start(bf16[256,512]{1,0:T(8,128)(2,1)} %get-tuple-element.178), channel_id=1, source_target_pairs={{0,64},{4,68},{8,72},{12,76},{16,80},{20,84},{24,88},{28,92},{32,9... | collective-permute-start | bytes 786440 | tf_op jit(solution)/shard_map/ppermute | solution.py:25
  258.3 22.2 %collective-permute-start.56 = (bf16[256,512]{1,0:T(8,128)(2,1)S(1)}, bf16[256,512]{1,0:T(8,128)(2,1)}, u32[]{:S(2)}, u32[]{:S(2)}) collective-permute-start(bf16[256,512]{1,0:T(8,128)(2,1)S(1)} %copy-done.60), channel_id=1, source_target_pairs={{0,96},{4,100},{8,104},{12,108},{16,112},{20,116},{24,120},{28,124... | collective-permute-start | bytes 786440 | tf_op jit(solution)/shard_map/ppermute | solution.py:25
  264.3 22.4 %collective-permute-start.46 = (bf16[4,128,256]{2,1,0:T(8,128)(2,1)}, bf16[4,128,256]{2,1,0:T(8,128)(2,1)S(1)}, u32[]{:S(2)}, u32[]{:S(2)}) collective-permute-start(bf16[4,128,256]{2,1,0:T(8,128)(2,1)} %get-tuple-element.163.event.refs_4_), channel_id=1, source_target_pairs={{0,32},{4,36},{8,40},{12,44},{16,48},{20,52},{24,56},{28,60},{32,0... | collective-permute-start | bytes 786440 | tf_op jit(solution)/shard_map/ppermute | solution.py:25
  269.3 17.5 %collective-permute-start.47 = (bf16[4,128,256]{2,1,0:T(8,128)(2,1)}, bf16[4,128,256]{2,1,0:T(8,128)(2,1)S(1)}, u32[]{:S(2)}, u32[]{:S(2)}) collective-permute-start(bf16[4,128,256]{2,1,0:T(8,128)(2,1)} %get-tuple-element.164), channel_id=1, source_target_pairs={{0,96},{4,100},{8,104},{12,108},{16,112},{20,116},{24,120},{28,124... | collective-permute-start | bytes 786440 | tf_op jit(solution)/shard_map/ppermute | solution.py:25
  271.1 15.7 %collective-permute-start.48 = (bf16[4,128,256]{2,1,0:T(8,128)(2,1)}, bf16[4,128,256]{2,1,0:T(8,128)(2,1)S(1)}, u32[]{:S(2)}, u32[]{:S(2)}) collective-permute-start(bf16[4,128,256]{2,1,0:T(8,128)(2,1)} %get-tuple-element.165), channel_id=1, source_target_pairs={{0,4},{4,0},{8,12},{12,8},{16,20},{20,16},{24,28},{28,24},{32,36},... | collective-permute-start | bytes 786440 | tf_op jit(solution)/shard_map/ppermute | solution.py:25
  273.0 13.8 %collective-permute-start.49 = (bf16[4,128,256]{2,1,0:T(8,128)(2,1)}, bf16[4,128,256]{2,1,0:T(8,128)(2,1)S(1)}, u32[]{:S(2)}, u32[]{:S(2)}) collective-permute-start(bf16[4,128,256]{2,1,0:T(8,128)(2,1)} %get-tuple-element.166), channel_id=1, source_target_pairs={{0,12},{4,8},{8,4},{12,0},{16,28},{20,24},{24,20},{28,16},{32,44},... | collective-permute-start | bytes 786440 | tf_op jit(solution)/shard_map/ppermute | solution.py:25
  286.7 139.0 %all-gather.19.cloned.1.call-start = ((), (), s32[]{:S(2)}) async-start(), calls=%async_computation.10 | async-start | bytes 1474560 | tf_op jit(solution)/shard_map/all_gather | solution.py:1251
  293.1 9.3 %collective-permute-start.64 = (bf16[2,160,2048]{2,1,0:T(8,128)(2,1)}, bf16[2,160,2048]{2,1,0:T(8,128)(2,1)S(1)}, u32[]{:S(2)}, u32[]{:S(2)}) collective-permute-start(bf16[2,160,2048]{2,1,0:T(8,128)(2,1)} %gate.3), channel_id=1, source_target_pairs={{0,1},{1,0},{2,3},{3,2},{4,5},{5,4},{6,7},{7,6},{8,9},{9,8},{10,11... | collective-permute-start | bytes 3932168 | tf_op jit(solution)/shard_map/ppermute | solution.py:25
  296.0 24.0 %collective-permute-start.50 = (bf16[8,128,256]{2,1,0:T(8,128)(2,1)}, bf16[8,128,256]{2,1,0:T(8,128)(2,1)}, u32[]{:S(2)}, u32[]{:S(2)}) collective-permute-start(bf16[8,128,256]{2,1,0:T(8,128)(2,1)} %get-tuple-element.169.refs_1_), channel_id=1, source_target_pairs={{0,32},{4,36},{8,40},{12,44},{16,48},{20,52},{24,56},{28,60},{32,0... | collective-permute-start | bytes 1572872 | tf_op jit(solution)/shard_map/ppermute | solution.py:25
  298.0 25.9 %collective-permute-start.51 = (bf16[8,128,256]{2,1,0:T(8,128)(2,1)}, bf16[8,128,256]{2,1,0:T(8,128)(2,1)}, u32[]{:S(2)}, u32[]{:S(2)}) collective-permute-start(bf16[8,128,256]{2,1,0:T(8,128)(2,1)} %get-tuple-element.170), channel_id=1, source_target_pairs={{0,96},{4,100},{8,104},{12,108},{16,112},{20,116},{24,120},{28,124... | collective-permute-start | bytes 1572872 | tf_op jit(solution)/shard_map/ppermute | solution.py:25
  298.0 25.9 %collective-permute-start.52 = (bf16[8,128,256]{2,1,0:T(8,128)(2,1)}, bf16[8,128,256]{2,1,0:T(8,128)(2,1)}, u32[]{:S(2)}, u32[]{:S(2)}) collective-permute-start(bf16[8,128,256]{2,1,0:T(8,128)(2,1)} %get-tuple-element.171), channel_id=1, source_target_pairs={{0,4},{4,0},{8,12},{12,8},{16,20},{20,16},{24,28},{28,24},{32,36},... | collective-permute-start | bytes 1572872 | tf_op jit(solution)/shard_map/ppermute | solution.py:25
  298.0 25.9 %collective-permute-start.53 = (bf16[8,128,256]{2,1,0:T(8,128)(2,1)}, bf16[8,128,256]{2,1,0:T(8,128)(2,1)}, u32[]{:S(2)}, u32[]{:S(2)}) collective-permute-start(bf16[8,128,256]{2,1,0:T(8,128)(2,1)} %get-tuple-element.172), channel_id=1, source_target_pairs={{0,12},{4,8},{8,4},{12,0},{16,28},{20,24},{24,20},{28,16},{32,44},... | collective-permute-start | bytes 1572872 | tf_op jit(solution)/shard_map/ppermute | solution.py:25
  302.9 44.6 %collective-permute-start.65 = (bf16[160,2048]{1,0:T(8,128)(2,1)S(1)}, bf16[160,2048]{1,0:T(8,128)(2,1)S(1)}, u32[]{:S(2)}, u32[]{:S(2)}) collective-permute-start(bf16[160,2048]{1,0:T(8,128)(2,1)S(1)} %fusion.4), channel_id=1, source_target_pairs={{0,2},{1,3},{2,0},{3,1},{4,6},{5,7},{6,4},{7,5},{8,10},{9,11},{10,... | collective-permute-start | bytes 1966088 | tf_op jit(solution)/shard_map/ppermute | solution.py:25
  327.2 9.6 %collective-permute-start.58 = (bf16[2,128,256]{2,1,0:T(8,128)(2,1)}, bf16[2,128,256]{2,1,0:T(8,128)(2,1)}, u32[]{:S(2)}, u32[]{:S(2)}) collective-permute-start(bf16[2,128,256]{2,1,0:T(8,128)(2,1)} %get-tuple-element.183), channel_id=1, source_target_pairs={{0,8},{4,12},{8,0},{12,4},{16,24},{20,28},{24,16},{28,20},{32,40},... | collective-permute-start | bytes 393224 | tf_op jit(solution)/shard_map/ppermute | solution.py:25
  331.0 8.3 %collective-permute-start.59 = (bf16[2,128,256]{2,1,0:T(8,128)(2,1)}, bf16[2,128,256]{2,1,0:T(8,128)(2,1)}, u32[]{:S(2)}, u32[]{:S(2)}) collective-permute-start(bf16[2,128,256]{2,1,0:T(8,128)(2,1)} %get-tuple-element.184), channel_id=1, source_target_pairs={{0,12},{4,8},{8,4},{12,0},{16,28},{20,24},{24,20},{28,16},{32,44},... | collective-permute-start | bytes 393224 | tf_op jit(solution)/shard_map/ppermute | solution.py:25
  331.0 8.3 %collective-permute-start.60 = (bf16[2,128,256]{2,1,0:T(8,128)(2,1)}, bf16[2,128,256]{2,1,0:T(8,128)(2,1)}, u32[]{:S(2)}, u32[]{:S(2)}) collective-permute-start(bf16[2,128,256]{2,1,0:T(8,128)(2,1)} %get-tuple-element.185), channel_id=1, source_target_pairs={{0,32},{4,36},{8,40},{12,44},{16,48},{20,52},{24,56},{28,60},{32,0... | collective-permute-start | bytes 393224 | tf_op jit(solution)/shard_map/ppermute | solution.py:25
  345.1 9.3 %collective-permute-start.63 = (bf16[2,128,256]{2,1,0:T(8,128)(2,1)}, bf16[2,128,256]{2,1,0:T(8,128)(2,1)S(1)}, u32[]{:S(2)}, u32[]{:S(2)}) collective-permute-start(bf16[2,128,256]{2,1,0:T(8,128)(2,1)} %get-tuple-element.190.refs_4_), channel_id=1, source_target_pairs={{0,16},{4,20},{8,24},{12,28},{16,0},{20,4},{24,8},{28,12},{32,48},... | collective-permute-start | bytes 393224 | tf_op jit(solution)/shard_map/ppermute | solution.py:25
  372.3 73.4 %reduce-scatter.6.cloned.1.call-start = ((), (), s32[]{:S(2)}) async-start(), calls=%async_computation.4 | async-start | bytes 3932160 | tf_op jit(solution)/shard_map/reduce_scatter | solution.py:46
  377.1 8.2 %collective-permute-start.76 = (f32[16,2048]{1,0:T(8,128)S(1)}, f32[16,2048]{1,0:T(8,128)S(1)}, u32[]{:S(2)}, u32[]{:S(2)}) collective-permute-start(f32[16,2048]{1,0:T(8,128)S(1)} %fusion.17), channel_id=1, source_target_pairs={{0,2},{1,3},{2,0},{3,1},{4,6},{5,7},{6,4},{7,5},{8,10},{9,11},{10,... | collective-permute-start | bytes 393224 | tf_op jit(solution)/shard_map/ppermute | solution.py:25
  377.7 8.4 %collective-permute-start.77 = (bf16[256,192]{1,0:T(8,128)(2,1)S(1)}, bf16[256,192]{1,0:T(8,128)(2,1)S(1)}, u32[]{:S(2)}, u32[]{:S(2)}) collective-permute-start(bf16[256,192]{1,0:T(8,128)(2,1)S(1)} %copy-done.70), channel_id=1, source_target_pairs={{0,8},{4,12},{8,0},{12,4},{16,24},{20,28},{24,16},{28,20},{32,40},... | collective-permute-start | bytes 294920 | tf_op jit(solution)/shard_map/ppermute | solution.py:25
  379.0 8.6 %collective-permute-start.78 = (bf16[256,192]{1,0:T(8,128)(2,1)S(1)}, bf16[256,192]{1,0:T(8,128)(2,1)S(1)}, u32[]{:S(2)}, u32[]{:S(2)}) collective-permute-start(bf16[256,192]{1,0:T(8,128)(2,1)S(1)} %copy-done.69), channel_id=1, source_target_pairs={{0,12},{4,8},{8,4},{12,0},{16,28},{20,24},{24,20},{28,16},{32,44},... | collective-permute-start | bytes 294920 | tf_op jit(solution)/shard_map/ppermute | solution.py:25
  380.9 24.6 %collective-permute-start.74 = (bf16[256,1024]{1,0:T(8,128)(2,1)}, bf16[256,1024]{1,0:T(8,128)(2,1)}, u32[]{:S(2)}, u32[]{:S(2)}) collective-permute-start(bf16[256,1024]{1,0:T(8,128)(2,1)} %dynamic-slice_bitcast_fusion), channel_id=1, source_target_pairs={{0,16},{4,20},{8,24},{12,28},{16,0},{20,4},{24,8},{28,12},{32,48},... | collective-permute-start | bytes 1572872 | tf_op jit(solution)/shard_map/ppermute | solution.py:25
  382.8 10.4 %collective-permute-start.68 = (bf16[128,2048]{1,0:T(8,128)(2,1)}, bf16[128,2048]{1,0:T(8,128)(2,1)S(1)}, u32[]{:S(2)}, u32[]{:S(2)}) collective-permute-start(bf16[128,2048]{1,0:T(8,128)(2,1)} %get-tuple-element.199), channel_id=1, source_target_pairs={{0,1},{1,0},{2,3},{3,2},{4,5},{5,4},{6,7},{7,6},{8,9},{9,8},{10,11... | collective-permute-start | bytes 1572872 | tf_op jit(solution)/shard_map/ppermute | solution.py:25
  385.3 26.5 %collective-permute-start.85 = (bf16[2,64,2048]{2,1,0:T(8,128)(2,1)S(1)}, bf16[2,64,2048]{2,1,0:T(8,128)(2,1)S(1)}, u32[]{:S(2)}, u32[]{:S(2)}) collective-permute-start(bf16[2,64,2048]{2,1,0:T(8,128)(2,1)S(1)} %slice.353), channel_id=1, source_target_pairs={{0,4},{4,0},{8,12},{12,8},{16,20},{20,16},{24,28},{28,24},{32,36},... | collective-permute-start | bytes 1572872 | tf_op jit(solution)/shard_map/ppermute | solution.py:25
  393.2 16.0 %collective-permute-start.79 = (bf16[2,2,256,256]{3,2,1,0:T(8,128)(2,1)}, bf16[2,2,256,256]{3,2,1,0:T(8,128)(2,1)S(1)}, u32[]{:S(2)}, u32[]{:S(2)}) collective-permute-start(bf16[2,2,256,256]{3,2,1,0:T(8,128)(2,1)} %get-tuple-element.211), channel_id=1, source_target_pairs={{0,32},{4,36},{8,40},{12,44},{16,48},{20,52},{24,56},{28,60},{32,0... | collective-permute-start | bytes 1572872 | tf_op jit(solution)/shard_map/ppermute | solution.py:25
  408.4 57.3 %collective-permute-start.69 = (bf16[64,2048]{1,0:T(8,128)(2,1)S(1)}, bf16[64,2048]{1,0:T(8,128)(2,1)S(1)}, u32[]{:S(2)}, u32[]{:S(2)}) collective-permute-start(bf16[64,2048]{1,0:T(8,128)(2,1)S(1)} %slice.392), channel_id=1, source_target_pairs={{0,2},{1,3},{2,0},{3,1},{4,6},{5,7},{6,4},{7,5},{8,10},{9,11},{10,... | collective-permute-start | bytes 786440 | tf_op jit(solution)/shard_map/ppermute | solution.py:25
  409.3 10.2 %collective-permute-start.80 = (bf16[2,256,256]{2,1,0:T(8,128)(2,1)S(1)}, bf16[2,256,256]{2,1,0:T(8,128)(2,1)S(1)}, u32[]{:S(2)}, u32[]{:S(2)}) collective-permute-start(bf16[2,256,256]{2,1,0:T(8,128)(2,1)S(1)} %slice_bitcast_fusion.3), channel_id=1, source_target_pairs={{0,96},{4,100},{8,104},{12,108},{16,112},{20,116},{24,120},{28,124... | collective-permute-start | bytes 786440 | tf_op jit(solution)/shard_map/ppermute | solution.py:25
  420.4 50.9 %collective-permute-start.86 = (bf16[64,2048]{1,0:T(8,128)(2,1)S(1)}, bf16[64,2048]{1,0:T(8,128)(2,1)S(1)}, u32[]{:S(2)}, u32[]{:S(2)}) collective-permute-start(bf16[64,2048]{1,0:T(8,128)(2,1)S(1)} %get-tuple-element.333), channel_id=1, source_target_pairs={{0,12},{4,8},{8,4},{12,0},{16,28},{20,24},{24,20},{28,16},{32,44},... | collective-permute-start | bytes 786440 | tf_op jit(solution)/shard_map/ppermute | solution.py:25
  446.8 11.9 %collective-permute-start.70 = (bf16[256,768]{1,0:T(8,128)(2,1)S(1)}, bf16[256,768]{1,0:T(8,128)(2,1)S(1)}, u32[]{:S(2)}, u32[]{:S(2)}) collective-permute-start(bf16[256,768]{1,0:T(8,128)(2,1)S(1)} %dynamic-slice_bitcast_fusion.1), channel_id=1, source_target_pairs={{0,16},{4,20},{8,24},{12,28},{16,0},{20,4},{24,8},{28,12},{32,48},... | collective-permute-start | bytes 1179656 | tf_op jit(solution)/shard_map/ppermute | solution.py:25
  461.8 16.0 %collective-permute-start.82 = (bf16[64,2048]{1,0:T(8,128)(2,1)}, bf16[64,2048]{1,0:T(8,128)(2,1)S(1)}, u32[]{:S(2)}, u32[]{:S(2)}) collective-permute-start(bf16[64,2048]{1,0:T(8,128)(2,1)} %get-tuple-element.213), channel_id=1, source_target_pairs={{0,4},{4,0},{8,12},{12,8},{16,20},{20,16},{24,28},{28,24},{32,36},... | collective-permute-start | bytes 786440 | tf_op jit(solution)/shard_map/ppermute | solution.py:25
  462.1 15.8 %collective-permute-start.83 = (bf16[64,2048]{1,0:T(8,128)(2,1)}, bf16[64,2048]{1,0:T(8,128)(2,1)S(1)}, u32[]{:S(2)}, u32[]{:S(2)}) collective-permute-start(bf16[64,2048]{1,0:T(8,128)(2,1)} %get-tuple-element.214), channel_id=1, source_target_pairs={{0,8},{4,12},{8,0},{12,4},{16,24},{20,28},{24,16},{28,20},{32,40},... | collective-permute-start | bytes 786440 | tf_op jit(solution)/shard_map/ppermute | solution.py:25
  464.3 13.6 %collective-permute-start.84 = (bf16[64,2048]{1,0:T(8,128)(2,1)}, bf16[64,2048]{1,0:T(8,128)(2,1)S(1)}, u32[]{:S(2)}, u32[]{:S(2)}) collective-permute-start(bf16[64,2048]{1,0:T(8,128)(2,1)} %get-tuple-element.215), channel_id=1, source_target_pairs={{0,12},{4,8},{8,4},{12,0},{16,28},{20,24},{24,20},{28,16},{32,44},... | collective-permute-start | bytes 786440 | tf_op jit(solution)/shard_map/ppermute | solution.py:25
  471.3 13.6 %collective-permute-start.71 = (bf16[64,2048]{1,0:T(8,128)(2,1)S(1)}, bf16[64,2048]{1,0:T(8,128)(2,1)S(1)}, u32[]{:S(2)}, u32[]{:S(2)}) collective-permute-start(bf16[64,2048]{1,0:T(8,128)(2,1)S(1)} %copy-done.34), channel_id=1, source_target_pairs={{0,1},{1,0},{2,3},{3,2},{4,5},{5,4},{6,7},{7,6},{8,9},{9,8},{10,11... | collective-permute-start | bytes 786440 | tf_op jit(solution)/shard_map/ppermute | solution.py:25
  474.9 10.0 %collective-permute-start.73 = (bf16[64,2048]{1,0:T(8,128)(2,1)S(1)}, bf16[64,2048]{1,0:T(8,128)(2,1)S(1)}, u32[]{:S(2)}, u32[]{:S(2)}) collective-permute-start(bf16[64,2048]{1,0:T(8,128)(2,1)S(1)} %collective-permute-done.72), channel_id=1, source_target_pairs={{0,1},{1,0},{2,3},{3,2},{4,5},{5,4},{6,7},{7,6},{8,9},{9,8},{10,11... | collective-permute-start | bytes 786440 | tf_op jit(solution)/shard_map/ppermute | solution.py:25
  (111 other events, 722.0 us)
Sparse Core Ops, SparseCore 0:
  47.3 36.3 all-gather.10
  85.4 48.6 all-gather.12
  136.2 49.7 all-gather.14
  187.5 48.6 all-gather.16
  247.4 77.0 reduce-scatter.3
  327.3 40.7 reduce-scatter.7
  372.4 30.2 all-gather.18
  405.1 40.5 reduce-scatter.5
where the time goes:
time: 504 us; the launch traced here: 494 us
  Pallas kernels  144 us (29%)
  waiting for transfers between devices  143 us (28%)
  starting transfers between devices  126 us (25%)
  local copies, waits for them, and re-layouts  43.2 us (9%)
  other arithmetic  22.6 us (4%)
  between operations  15.6 us (3%)
    ppermute x87, starting transfers between devices, hop(): lax.ppermute(value, axis, [(i, i ^ mask) for i in range(lax.axis_size(axi...  125 us
    ppermute x87, waiting for transfers between devices, hop(): lax.ppermute(value, axis, [(i, i ^ mask) for i in range(lax.axis_size(axi...  124 us
    pallas_call x19, Pallas kernels, in_one(): pl.pallas_call(kernel, out_shape=tuple((jax.ShapeDtypeStruct(shape, kind)...  65.5 us
    unnamed x164, local copies, waits for them, and re-layouts  20 us
    reduce_scatter x3, waiting for transfers between devices, scatter_group(): lax.psum_scatter(value, 'ctx', scatter_dimension=0, axis_index_groups=gro...  17.4 us
    pallas_call x1, Pallas kernels, ff_forward(): pl.pallas_call(ff_forward_kernel, grid=(units // UNITS,), out_shape=(jax....  15.8 us
    pallas_call x1, Pallas kernels, attend_backward(): pl.pallas_call(backward_kernel, out_shape=(jax.ShapeDtypeStruct((rows, 2...  11.7 us
    pallas_call x1, Pallas kernels, ff_grads(): pl.pallas_call(ff_grads_kernel, grid_spec=pltpu.PrefetchScalarGridSpec(nu...  11 us
  transfers between devices with their start and end apart: 95, of which 37 were waited for; matrix products, arithmetic and copies ran while one was open for 9% of the time, Pallas kernels for 27%

commit v1 on v0

--- a/solution.py
+++ b/solution.py
@@ -1247,7 +1247,7 @@
     late_gains = late_gains + hop(late_gains, "wt", 1)
     late_gains = late_gains + hop(late_gains, "wt", 2)
     token_cuts = [token_cuts[0]] + [hop(token_cuts[k], "ctx", k) for k in (1, 2, 3)]
-    (results,) = hold((results,), token_cuts[1])
+    (results,) = hold((results,), turn)
     results = lax.all_gather(results, "wt", axis=0)
     layer_out_all = jnp.concatenate([results[i, :, :D] for i in (0, 2, 1, 3)]).astype(F32)
     grad_input_all = jnp.concatenate(

time: 504 us -> 479 us (0.950)
  waiting for transfers between devices: 143 us -> 116 us
  Pallas kernels: 144 us -> 154 us
  starting transfers between devices: 126 us -> 118 us
    reduce_scatter x3, waiting for transfers between devices: 17.4 us -> 0.01 us  [scatter_group(): lax.psum_scatter(value, 'ctx', scatter_dimension=0, axis_index_groups=gro...]
    ppermute x87, waiting for transfers between devices: 124 us -> 114 us  [hop(): lax.ppermute(value, axis, [(i, i ^ mask) for i in range(lax.axis_size(axi...]
    ppermute x87, starting transfers between devices: 125 us -> 117 us  [hop(): lax.ppermute(value, axis, [(i, i ^ mask) for i in range(lax.axis_size(axi...]
    pallas_call x1, Pallas kernels: 11.7 us -> 18 us  [attend_backward(): pl.pallas_call(backward_kernel, out_shape=(jax.ShapeDtypeStruct((rows, 2...]
    unnamed x164 -> x166, local copies, waits for them, and re-layouts: 20 us -> 20.3 us
  transfers between devices with their start and end apart: 95 -> 95, of which waited for: 37 -> 37; matrix products, arithmetic and copies ran while one was open for 9% -> 10% of each run, Pallas kernels for 27% -> 31%
where the time goes in v1:
time: 479 us; the launch traced here: 471 us
  Pallas kernels  154 us (32%)
  starting transfers between devices  118 us (25%)
  waiting for transfers between devices  116 us (24%)
  local copies, waits for them, and re-layouts  44.3 us (9%)
  other arithmetic  22.8 us (5%)
  between operations  15.6 us (3%)
    ppermute x87, starting transfers between devices, hop(): lax.ppermute(value, axis, [(i, i ^ mask) for i in range(lax.axis_size(axi...  117 us
    ppermute x87, waiting for transfers between devices, hop(): lax.ppermute(value, axis, [(i, i ^ mask) for i in range(lax.axis_size(axi...  114 us
    pallas_call x19, Pallas kernels, in_one(): pl.pallas_call(kernel, out_shape=tuple((jax.ShapeDtypeStruct(shape, kind)...  65.7 us
    unnamed x166, local copies, waits for them, and re-layouts  20.3 us
    pallas_call x1, Pallas kernels, attend_backward(): pl.pallas_call(backward_kernel, out_shape=(jax.ShapeDtypeStruct((rows, 2...  18 us
    pallas_call x1, Pallas kernels, ff_forward(): pl.pallas_call(ff_forward_kernel, grid=(units // UNITS,), out_shape=(jax....  15.7 us
    pallas_call x1, Pallas kernels, attend_forward(): pl.pallas_call(forward_kernel, out_shape=(jax.ShapeDtypeStruct((rows, 2 *...  12.6 us
    pallas_call x1, Pallas kernels, ff_back(): pl.pallas_call(ff_back_kernel, grid_spec=pltpu.PrefetchScalarGridSpec(num...  11 us
  transfers between devices with their start and end apart: 95, of which 37 were waited for; matrix products, arithmetic and copies ran while one was open for 10% of the time, Pallas kernels for 31%

profile of v1, /device:TPU:1, one launch (start us, length us, event | category | flops | bytes accessed | tf_op | source)
XLA Modules:
  0.0 470.5 jit_solution(13301775091366645351)
XLA Ops:
  7.9 3.2 input.1
  18.4 3.7 collective-permute-start.1
  23.0 3.2 collective-permute-done.1
  27.6 2.6 collective-permute-start.6
  31.5 2.4 collective-permute-start.3
  38.6 2.8 collective-permute-done.4.refs_3_
  42.1 2.3 lay.1
  44.4 2.7 pack.1
  48.0 2.7 collective-permute-start.9
  51.7 2.2 collective-permute-start.16
  54.0 5.9 %collective-permute-done.8 = bf16[1024,256]{1,0:T(8,128)(2,1)S(1)} collective-permute-done((bf16[1024,256]{1,0:T(8,128)(2,1)S(1)}, bf16[1024,256]{1,0:T(8,128)(2,1)S(1)}, u32[]{:S(2)}, u32[]{:S(2)}) %collective-permute-start.8) | collective-permute-done | bytes 524320 | tf_op jit(solution)/shard_map/ppermute | solution.py:25
  59.9 2.7 collective-permute-start.10
  63.4 2.8 collective-permute-start.21
  72.0 3.4 collective-permute-done.14
  80.2 3.5 query.1
  84.7 12.6 %attend_forward.1 = (bf16[256,512]{1,0:T(8,128)(2,1)}, f32[256,512]{1,0:T(8,128)}, f32[2,8,256]{2,1,0:T(8,128)}, f32[128,2048]{1,0:T(8,128)}, bf16[128,2048]{1,0:T(8,128)(2,1)}) custom-call(s32[157]{0:T(256)} %concatenate.52.meta, bf16[256,512]{1,0:T(8,128)(2,1)} %get-tuple-element.130.q_ref, bf16[512,2048]{1,0:T(8,128)(2,1)} %w_ref.3, ...), custom_call_target="tpu_custom_call" | custom-call | flops 3000000000 | bytes 10000000 | tf_op jit(solution)/shard_map/attend_forward/pallas_call | solution.py:317
  104.3 5.1 %collective-permute-done.27.came = bf16[64,2048]{1,0:T(8,128)(2,1)S(1)} collective-permute-done((bf16[64,2048]{1,0:T(8,128)(2,1)S(1)}, bf16[64,2048]{1,0:T(8,128)(2,1)S(1)}, u32[]{:S(2)}, u32[]{:S(2)}) %collective-permute-start.27) | collective-permute-done | bytes 262176 | tf_op jit(solution)/shard_map/ppermute | solution.py:25
  110.0 3.4 mid.1
  115.4 5.0 %collective-permute-done.28.refs_1_ = bf16[64,2048]{1,0:T(8,128)(2,1)S(1)} collective-permute-done((bf16[64,2048]{1,0:T(8,128)(2,1)}, bf16[64,2048]{1,0:T(8,128)(2,1)S(1)}, u32[]{:S(2)}, u32[]{:S(2)}) %collective-permute-start.28) | collective-permute-done | bytes 262176 | tf_op jit(solution)/shard_map/ppermute | solution.py:25
  124.2 15.7 %ff_forward.1 = (f32[256,2048]{1,0:T(8,128)}, f32[256,2048]{1,0:T(8,128)}, bf16[256,2048]{1,0:T(8,128)(2,1)}, bf16[256,2048]{1,0:T(8,128)(2,1)}, f32[128,2048]{1,0:T(8,128)}, /*index=5*/bf16[128,2048]{1,0:T(8,128)(2,1)}) custom-call(bf16[64,2048]{1,0:T(8,128)(2,1)} %get-tuple-element.134.refs_0_, bf16[64,2048]{1,0:T(8,128)(2,1)} %copy-done.17, ...), custom_call_target="tpu_custom_call" | custom-call | flops 6442450944 | bytes 30000000 | tf_op jit(solution)/shard_map/ff_forward/pallas_call | solution.py:402
  149.3 5.0 %collective-permute-done.32.came = bf16[64,2048]{1,0:T(8,128)(2,1)S(1)} collective-permute-done((bf16[64,2048]{1,0:T(8,128)(2,1)S(1)}, bf16[64,2048]{1,0:T(8,128)(2,1)S(1)}, u32[]{:S(2)}, u32[]{:S(2)}) %collective-permute-start.32) | collective-permute-done | bytes 262176 | tf_op jit(solution)/shard_map/ppermute | solution.py:25
  155.0 8.2 %join.1 = (bf16[64,2048]{1,0:T(8,128)(2,1)}, f32[64,2048]{1,0:T(8,128)}, bf16[64,2304]{1,0:T(8,128)(2,1)}, f32[8,2048]{1,0:T(8,128)}, bf16[2,128,2048]{2,1,0:T(8,128)(2,1)}, /*index=5*/bf16[2,128,2048]{2,1,0:T(8,128)(2,1)}) custom-call(f32[64,2048]{1,0:T(8,128)} %slice.331.kept, bf16[64,2048]{1,0:T(8,128)(2,1)} %copy-done.29, ...), custom_call_target="tpu_custom_call" | custom-call | flops 1000000000 | bytes 5000000 | tf_op jit(solution)/shard_map/join/pallas_call | solution.py:767
  164.9 5.7 %collective-permute-done.33.refs_1_ = bf16[64,2048]{1,0:T(8,128)(2,1)S(1)} collective-permute-done((bf16[64,2048]{1,0:T(8,128)(2,1)}, bf16[64,2048]{1,0:T(8,128)(2,1)S(1)}, u32[]{:S(2)}, u32[]{:S(2)}) %collective-permute-start.33) | collective-permute-done | bytes 262176 | tf_op jit(solution)/shard_map/ppermute | solution.py:25
  174.4 10.9 %ff_grads.1 = (bf16[256,1024]{1,0:T(8,128)(2,1)}, bf16[256,1024]{1,0:T(8,128)(2,1)}, bf16[256,1024]{1,0:T(8,128)(2,1)}, bf16[256,1024]{1,0:T(8,128)(2,1)}, bf16[...) custom-call(s32[3]{0:T(128)} %pad_add_fusion.me.where, ...), custom_call_target="tpu_custom_call" | custom-call | flops 2147483648 | bytes 10000000 | tf_op jit(solution)/shard_map/ff_grads/pallas_call | solution.py:460
  185.4 11.0 %ff_back.1 = (f32[128,2048]{1,0:T(8,128)}, bf16[128,2048]{1,0:T(8,128)(2,1)}) custom-call(s32[3]{0:T(128)} %pad_add_fusion.me.where, bf16[256,1024]{1,0:T(8,128)(2,1)} %get-tuple-element.142.refs_0_, bf16[256,1024]{1,0:T(8,128)(2,1)} %get-tuple-element.143.refs_1_, bf16[256,1024]{1,0:T(8,128)(2,1)} %get-tuple-element.144.refs_2_, ...), custom_call_target="tpu_custom_call" | custom-call | flops 4294967296 | bytes 20000000 | tf_op jit(solution)/shard_map/ff_back/pallas_call | solution.py:506
  200.8 2.4 collective-permute-start.42
  205.4 2.3 collective-permute-done.37.came
  208.5 5.9 %resid.1 = (bf16[64,2048]{1,0:T(8,128)(2,1)}, f32[64,2048]{1,0:T(8,128)}, f32[64,2048]{1,0:T(8,128)}, f32[8,2048]{1,0:T(8,128)}, bf16[2,160,2048]{2,1,0:T(8,128)(2,1)}, /*index=5*/bf16[2,160,2048]{2,1,0:T(8,128)(2,1)}) custom-call(f32[64,2048]{1,0:T(8,128)} %slice.334.kept, bf16[64,2048]{1,0:T(8,128)(2,1)} %copy-done.24, ...), custom_call_target="tpu_custom_call" | custom-call | flops 1000000000 | bytes 5000000 | tf_op jit(solution)/shard_map/resid/pallas_call | solution.py:767
  216.4 5.0 %collective-permute-done.38.refs_1_ = bf16[64,2048]{1,0:T(8,128)(2,1)S(1)} collective-permute-done((bf16[64,2048]{1,0:T(8,128)(2,1)}, bf16[64,2048]{1,0:T(8,128)(2,1)S(1)}, u32[]{:S(2)}, u32[]{:S(2)}) %collective-permute-start.38) | collective-permute-done | bytes 262176 | tf_op jit(solution)/shard_map/ppermute | solution.py:25
  223.3 2.5 collective-permute-done.42.refs_25_.refs_2_
  228.9 18.0 %attend_backward.1 = (f32[256,512]{1,0:T(8,128)}, bf16[16,128,256]{2,1,0:T(8,128)(2,1)}, bf16[48,128,256]{2,1,0:T(8,128)(2,1)}, bf16[16,128,256]{2,1,0:T(8,128)(2,1)}, bf16[48,128,256]{2,1,0:T(8,128)(2,1)}) custom-call(s32[157]{0:T(256)} %concatenate.52.meta, bf16[256,512]{1,0:T(8,128)(2,1)} %get-tuple-element.130.q_ref, ...), custom_call_target="tpu_custom_call" | custom-call | flops 10000000000 | bytes 20000000 | tf_op jit(solution)/shard_map/attend_backward/pallas_call | solution.py:344
  246.9 9.4 %wide_product.1.refs_1_ = bf16[2048,1024]{1,0:T(8,128)(2,1)} custom-call(s32[3]{0:T(128)} %pad_add_fusion.me.where, bf16[4,256,2048]{2,1,0:T(8,128)(2,1)} %bitcast.160, bf16[256,1024]{1,0:T(8,128)(2,1)} %get-tuple-element.142.refs_0_, bf16[256,1024]{1,0:T(8,128)(2,1)} %copy-done.53, bf16[256,1024]{1,0:T(8,128)(2,1)} %copy-done.54, ...), custom_call_target="tpu_custom_call" | custom-call | flops 5000000000 | bytes 10000000 | tf_op jit(solution)/shard_map/wide_product/pallas_call | solution.py:815
  258.9 3.5 collective-permute-start.58
  262.4 3.0 collective-permute-done.45.came
  268.2 2.9 far.1
  272.2 3.5 collective-permute-done.58.refs_3_
  275.7 6.2 %down_product.1.refs_5_ = bf16[2,4,64,2048]{3,2,1,0:T(8,128)(2,1)} custom-call(s32[3]{0:T(128)} %pad_add_fusion.me.where, bf16[4,256,2048]{2,1,0:T(8,128)(2,1)} %bitcast.209, bf16[256,512]{1,0:T(8,128)(2,1)} %get-tuple-element.179.refs_0_, bf16[256,512]{1,0:T(8,128)(2,1)} %collective-permute-done.56.refs_1_, ...), custom_call_target="tpu_custom_call" | custom-call | flops 3000000000 | bytes 10000000 | tf_op jit(solution)/shard_map/down_product/pallas_call | solution.py:928
  284.9 10.7 %collective-permute-done.46.refs_0_ = bf16[4,128,256]{2,1,0:T(8,128)(2,1)S(1)} collective-permute-done((bf16[4,128,256]{2,1,0:T(8,128)(2,1)S(1)}, bf16[4,128,256]{2,1,0:T(8,128)(2,1)S(1)}, u32[]{:S(2)}, u32[]{:S(2)}) %collective-permute-start.46) | collective-permute-done | bytes 262176 | tf_op jit(solution)/shard_map/ppermute | solution.py:25
  297.8 5.2 %near.1 = (f32[8,128,256]{2,1,0:T(8,128)}, f32[8,128,256]{2,1,0:T(8,128)}, bf16[8,128,256]{2,1,0:T(8,128)(2,1)}, bf16[8,128,256]{2,1,0:T(8,128)(2,1)}, bf16[8,12...) custom-call(bf16[48,128,256]{2,1,0:T(8,128)(2,1)} %get-tuple-element.160.own, bf16[48,128,256]{2,1,0:T(8,128)(2,1)} %copy-done.2, ...), custom_call_target="tpu_custom_call" | custom-call | flops 1000000000 | bytes 5000000 | tf_op jit(solution)/shard_map/near/pallas_call | solution.py:767
  303.0 4.7 %collective-permute-start.50 = (bf16[2,160,2048]{2,1,0:T(8,128)(2,1)}, bf16[2,160,2048]{2,1,0:T(8,128)(2,1)S(1)}, u32[]{:S(2)}, u32[]{:S(2)}) collective-permute-start(bf16[2,160,2048]{2,1,0:T(8,128)(2,1)} %gate.3), channel_id=1, source_target_pairs={{0,1},{1,0},{2,3},{3,2},{4,5},{5,4},{6,7},{7,6},{8,9},{9,8},{10,11... | collective-permute-start | bytes 3932168 | tf_op jit(solution)/shard_map/ppermute | solution.py:25
  312.4 2.3 query_back.1
  314.7 8.6 %collective-permute-done.52.refs_0_ = bf16[8,128,256]{2,1,0:T(8,128)(2,1)} collective-permute-done((bf16[8,128,256]{2,1,0:T(8,128)(2,1)}, bf16[8,128,256]{2,1,0:T(8,128)(2,1)}, u32[]{:S(2)}, u32[]{:S(2)}) %collective-permute-start.52) | collective-permute-done | bytes 524320 | tf_op jit(solution)/shard_map/ppermute | solution.py:25
  325.4 3.2 inner.1
  333.2 3.1 collective-permute-start.63
  336.6 2.6 collective-permute-start.64
  339.3 2.2 collective-permute-done.63.refs_4_
  341.5 2.9 collective-permute-done.64.refs_5_
  347.4 4.2 turn.1.event
  352.5 4.8 %collective-permute-start.66 = (bf16[2,128,256]{2,1,0:T(8,128)(2,1)S(1)}, bf16[2,128,256]{2,1,0:T(8,128)(2,1)S(1)}, u32[]{:S(2)}, u32[]{:S(2)}) collective-permute-start(bf16[2,128,256]{2,1,0:T(8,128)(2,1)S(1)} %copy-done.35), channel_id=1, source_target_pairs={{0,16},{4,20},{8,24},{12,28},{16,0},{20,4},{24,8},{28,12},{32,48},... | collective-permute-start | bytes 393224 | tf_op jit(solution)/shard_map/ppermute | solution.py:25
  362.4 3.4 collective-permute-start.67
  368.0 5.2 %normed_back.1 = (f32[128,2048]{1,0:T(8,128)}, bf16[128,2048]{1,0:T(8,128)(2,1)}, f32[1,2048]{1,0:T(1,128)}, bf16[256,192]{1,0:T(8,128)(2,1)}, bf16[256,192]{1,0...) custom-call(s32[6]{0:T(128)} %stack.52.spots, bf16[256,128]{1,0:T(8,128)(2,1)} %get-tuple-element.195.home, ...), custom_call_target="tpu_custom_call" | custom-call | flops 1000000000 | bytes 5000000 | tf_op jit(solution)/shard_map/normed_back/pallas_call | solution.py:767
  380.3 3.4 collective-permute-start.73
  388.3 5.0 %token_product.1 = (bf16[2,2,256,256]{3,2,1,0:T(8,128)(2,1)}, bf16[2,2,256,256]{3,2,1,0:T(8,128)(2,1)}) custom-call(s32[3]{0:T(128)} %pad_add_fusion.me.where, bf16[4,256,2048]{2,1,0:T(8,128)(2,1)} %bitcast.156, bf16[16,2048]{1,0:T(8,128)(2,1)} %add_convert_fusion.2.gains, bf16[256,192]{1,0:T(8,128)(2,1)} %get-tuple-element.206.refs_0_, ...), custom_call_target="tpu_custom_call" | custom-call | flops 1000000000 | bytes 6000000 | tf_op jit(solution)/shard_map/token_product/pallas_call | solution.py:856
  396.6 3.3 collective-permute-done.85
  400.0 8.2 %collective-permute-done.79 = bf16[2,2,256,256]{3,2,1,0:T(8,128)(2,1)S(1)} collective-permute-done((bf16[2,2,256,256]{3,2,1,0:T(8,128)(2,1)}, bf16[2,2,256,256]{3,2,1,0:T(8,128)(2,1)S(1)}, u32[]{:S(2)}, u32[]{:S(2)}) %collective-permute-start.79) | collective-permute-done | bytes 524320 | tf_op jit(solution)/shard_map/ppermute | solution.py:25
  411.1 2.3 collective-permute-start.86
  414.5 2.9 collective-permute-start.65
  417.5 2.1 collective-permute-start.81
  419.6 5.8 %collective-permute-done.65 = bf16[256,768]{1,0:T(8,128)(2,1)S(1)} collective-permute-done((bf16[256,768]{1,0:T(8,128)(2,1)S(1)}, bf16[256,768]{1,0:T(8,128)(2,1)S(1)}, u32[]{:S(2)}, u32[]{:S(2)}) %collective-permute-start.65) | collective-permute-done | bytes 393248 | tf_op jit(solution)/shard_map/ppermute | solution.py:25
  428.9 2.3 payload.1
  431.9 2.5 final.1
  439.4 3.5 collective-permute-start.70
  444.8 4.8 %collective-permute-start.72 = (bf16[64,2048]{1,0:T(8,128)(2,1)S(1)}, bf16[64,2048]{1,0:T(8,128)(2,1)S(1)}, u32[]{:S(2)}, u32[]{:S(2)}) collective-permute-start(bf16[64,2048]{1,0:T(8,128)(2,1)S(1)} %collective-permute-done.71), channel_id=1, source_target_pairs={{0,1},{1,0},{2,3},{3,2},{4,5},{5,4},{6,7},{7,6},{8,9},{9,8},{10,11... | collective-permute-start | bytes 786440 | tf_op jit(solution)/shard_map/ppermute | solution.py:25
  451.3 2.8 share.1
  (423 shorter events, 149.9 us)
Async XLA Ops:
  7.2 95.1 %all-gather.11.cloned.1.call-start = ((), (), s32[]{:S(2)}) async-start(), calls=%async_computation.6 | async-start | bytes 3604480 | tf_op jit(solution)/shard_map/all_gather | solution.py:1053
  27.6 9.3 %collective-permute-start.6 = (bf16[256,256]{1,0:T(8,128)(2,1)S(1)}, bf16[256,256]{1,0:T(8,128)(2,1)S(1)}, u32[]{:S(2)}, u32[]{:S(2)}) collective-permute-start(bf16[256,256]{1,0:T(8,128)(2,1)S(1)} %pad_maximum_fusion.6.refs_4_), channel_id=1, source_target_pairs={{0,64},{4,68},{8,72},{12,76},{16,80},{20,84},{24,88},{28,92},{32,9... | collective-permute-start | bytes 393224 | tf_op jit(solution)/shard_map/ppermute | solution.py:25
  30.2 8.3 %collective-permute-start.7 = (bf16[256,256]{1,0:T(8,128)(2,1)S(1)}, bf16[256,256]{1,0:T(8,128)(2,1)S(1)}, u32[]{:S(2)}, u32[]{:S(2)}) collective-permute-start(bf16[256,256]{1,0:T(8,128)(2,1)S(1)} %pad_maximum_fusion.6.refs_4_), channel_id=1, source_target_pairs={{0,96},{4,100},{8,104},{12,108},{16,112},{20,116},{24,120},{28,124... | collective-permute-start | bytes 393224 | tf_op jit(solution)/shard_map/ppermute | solution.py:25
  30.2 8.3 %collective-permute-start.2 = (bf16[256,256]{1,0:T(8,128)(2,1)S(1)}, bf16[256,256]{1,0:T(8,128)(2,1)S(1)}, u32[]{:S(2)}, u32[]{:S(2)}) collective-permute-start(bf16[256,256]{1,0:T(8,128)(2,1)S(1)} %pad_maximum_fusion.5.refs_0_), channel_id=1, source_target_pairs={{0,4},{4,0},{8,12},{12,8},{16,20},{20,16},{24,28},{28,24},{32,36},... | collective-permute-start | bytes 393224 | tf_op jit(solution)/shard_map/ppermute | solution.py:25
  47.1 107.2 %all-gather.13.cloned.1.call-start = ((), (), s32[]{:S(2)}) async-start(), calls=%async_computation.7 | async-start | bytes 5242880 | tf_op jit(solution)/shard_map/all_gather | solution.py:42
  47.9 159.9 %all-gather.15.cloned.1.call-start = ((), (), s32[]{:S(2)}) async-start(), calls=%async_computation.8 | async-start | bytes 5242880 | tf_op jit(solution)/shard_map/all_gather | solution.py:42
  47.9 11.9 %collective-permute-start.8 = (bf16[1024,256]{1,0:T(8,128)(2,1)S(1)}, bf16[1024,256]{1,0:T(8,128)(2,1)S(1)}, u32[]{:S(2)}, u32[]{:S(2)}) collective-permute-start(bf16[1024,256]{1,0:T(8,128)(2,1)S(1)} %copy-done.11), channel_id=1, source_target_pairs={{0,32},{4,36},{8,40},{12,44},{16,48},{20,52},{24,56},{28,60},{32,0... | collective-permute-start | bytes 1572872 | tf_op jit(solution)/shard_map/ppermute | solution.py:25
  48.0 14.5 %collective-permute-start.9 = (bf16[1024,256]{1,0:T(8,128)(2,1)S(1)}, bf16[1024,256]{1,0:T(8,128)(2,1)S(1)}, u32[]{:S(2)}, u32[]{:S(2)}) collective-permute-start(bf16[1024,256]{1,0:T(8,128)(2,1)S(1)} %copy-done.11), channel_id=1, source_target_pairs={{0,96},{4,100},{8,104},{12,108},{16,112},{20,116},{24,120},{28,124... | collective-permute-start | bytes 1572872 | tf_op jit(solution)/shard_map/ppermute | solution.py:25
  50.7 11.9 %collective-permute-start.12 = (bf16[1024,256]{1,0:T(8,128)(2,1)}, bf16[1024,256]{1,0:T(8,128)(2,1)S(1)}, u32[]{:S(2)}, u32[]{:S(2)}) collective-permute-start(bf16[1024,256]{1,0:T(8,128)(2,1)} %get-tuple-element.131), channel_id=1, source_target_pairs={{0,4},{4,0},{8,12},{12,8},{16,20},{20,16},{24,28},{28,24},{32,36},... | collective-permute-start | bytes 1572872 | tf_op jit(solution)/shard_map/ppermute | solution.py:25
  50.7 15.5 %collective-permute-start.13 = (bf16[1024,256]{1,0:T(8,128)(2,1)}, bf16[1024,256]{1,0:T(8,128)(2,1)S(1)}, u32[]{:S(2)}, u32[]{:S(2)}) collective-permute-start(bf16[1024,256]{1,0:T(8,128)(2,1)} %get-tuple-element.131), channel_id=1, source_target_pairs={{0,12},{4,8},{8,4},{12,0},{16,28},{20,24},{24,20},{28,16},{32,44},... | collective-permute-start | bytes 1572872 | tf_op jit(solution)/shard_map/ppermute | solution.py:25
  51.7 16.8 %collective-permute-start.16 = (bf16[1024,256]{1,0:T(8,128)(2,1)S(1)}, bf16[1024,256]{1,0:T(8,128)(2,1)}, u32[]{:S(2)}, u32[]{:S(2)}) collective-permute-start(bf16[1024,256]{1,0:T(8,128)(2,1)S(1)} %copy-done.11), channel_id=1, source_target_pairs={{0,1},{1,0},{2,3},{3,2},{4,5},{5,4},{6,7},{7,6},{8,9},{9,8},{10,11... | collective-permute-start | bytes 1572872 | tf_op jit(solution)/shard_map/ppermute | solution.py:25
  59.9 8.8 %collective-permute-start.10 = (bf16[512,256]{1,0:T(8,128)(2,1)S(1)}, bf16[512,256]{1,0:T(8,128)(2,1)S(1)}, u32[]{:S(2)}, u32[]{:S(2)}) collective-permute-start(bf16[512,256]{1,0:T(8,128)(2,1)S(1)} %slice.325), channel_id=1, source_target_pairs={{0,96},{4,100},{8,104},{12,108},{16,112},{20,116},{24,120},{28,124... | collective-permute-start | bytes 786440 | tf_op jit(solution)/shard_map/ppermute | solution.py:25
  63.4 13.2 %collective-permute-start.21 = (bf16[1024,256]{1,0:T(8,128)(2,1)}, bf16[1024,256]{1,0:T(8,128)(2,1)}, u32[]{:S(2)}, u32[]{:S(2)}) collective-permute-start(bf16[1024,256]{1,0:T(8,128)(2,1)} %get-tuple-element.131), channel_id=1, source_target_pairs={{0,1},{1,0},{2,3},{3,2},{4,5},{5,4},{6,7},{7,6},{8,9},{9,8},{10,11... | collective-permute-start | bytes 1572872 | tf_op jit(solution)/shard_map/ppermute | solution.py:25
  66.2 9.1 %collective-permute-start.14 = (bf16[512,256]{1,0:T(8,128)(2,1)S(1)}, bf16[512,256]{1,0:T(8,128)(2,1)}, u32[]{:S(2)}, u32[]{:S(2)}) collective-permute-start(bf16[512,256]{1,0:T(8,128)(2,1)S(1)} %slice.327), channel_id=1, source_target_pairs={{0,12},{4,8},{8,4},{12,0},{16,28},{20,24},{24,20},{28,16},{32,44},... | collective-permute-start | bytes 786440 | tf_op jit(solution)/shard_map/ppermute | solution.py:25
  68.6 8.0 %collective-permute-start.15 = (bf16[512,256]{1,0:T(8,128)(2,1)S(1)}, bf16[512,256]{1,0:T(8,128)(2,1)}, u32[]{:S(2)}, u32[]{:S(2)}) collective-permute-start(bf16[512,256]{1,0:T(8,128)(2,1)S(1)} %slice.328), channel_id=1, source_target_pairs={{0,4},{4,0},{8,12},{12,8},{16,20},{20,16},{24,28},{28,24},{32,36},... | collective-permute-start | bytes 786440 | tf_op jit(solution)/shard_map/ppermute | solution.py:25
  68.7 8.8 %collective-permute-start.19 = (bf16[512,256]{1,0:T(8,128)(2,1)S(1)}, bf16[512,256]{1,0:T(8,128)(2,1)}, u32[]{:S(2)}, u32[]{:S(2)}) collective-permute-start(bf16[512,256]{1,0:T(8,128)(2,1)S(1)} %collective-permute-done.10), channel_id=1, source_target_pairs={{0,1},{1,0},{2,3},{3,2},{4,5},{5,4},{6,7},{7,6},{8,9},{9,8},{10,11... | collective-permute-start | bytes 786440 | tf_op jit(solution)/shard_map/ppermute | solution.py:25
  114.0 8.3 %collective-permute-start.29 = (bf16[64,2048]{1,0:T(8,128)(2,1)}, bf16[64,2048]{1,0:T(8,128)(2,1)S(1)}, u32[]{:S(2)}, u32[]{:S(2)}) collective-permute-start(bf16[64,2048]{1,0:T(8,128)(2,1)} %get-tuple-element.134.refs_0_), channel_id=1, source_target_pairs={{0,1},{1,0},{2,3},{3,2},{4,5},{5,4},{6,7},{7,6},{8,9},{9,8},{10,11... | collective-permute-start | bytes 786440 | tf_op jit(solution)/shard_map/ppermute | solution.py:25
  139.9 135.8 %all-gather.17.cloned.1.call-start = ((), (), s32[]{:S(2)}) async-start(), calls=%async_computation.9 | async-start | bytes 5242880 | tf_op jit(solution)/shard_map/all_gather | solution.py:42
  140.5 226.9 %reduce-scatter.6.cloned.1.call-start = ((), (), s32[]{:S(2)}) async-start(), calls=%async_computation.4 | async-start | bytes 5242880 | tf_op jit(solution)/shard_map/reduce_scatter | solution.py:46
  146.2 8.1 %collective-permute-start.32 = (bf16[64,2048]{1,0:T(8,128)(2,1)S(1)}, bf16[64,2048]{1,0:T(8,128)(2,1)S(1)}, u32[]{:S(2)}, u32[]{:S(2)}) collective-permute-start(bf16[64,2048]{1,0:T(8,128)(2,1)S(1)} %slice.394), channel_id=1, source_target_pairs={{0,2},{1,3},{2,0},{3,1},{4,6},{5,7},{6,4},{7,5},{8,10},{9,11},{10,... | collective-permute-start | bytes 786440 | tf_op jit(solution)/shard_map/ppermute | solution.py:25
  163.8 9.4 %collective-permute-start.34 = (bf16[64,2048]{1,0:T(8,128)(2,1)}, bf16[64,2048]{1,0:T(8,128)(2,1)S(1)}, u32[]{:S(2)}, u32[]{:S(2)}) collective-permute-start(bf16[64,2048]{1,0:T(8,128)(2,1)} %get-tuple-element.139.refs_0_), channel_id=1, source_target_pairs={{0,1},{1,0},{2,3},{3,2},{4,5},{5,4},{6,7},{7,6},{8,9},{9,8},{10,11... | collective-permute-start | bytes 786440 | tf_op jit(solution)/shard_map/ppermute | solution.py:25
  200.8 22.6 %collective-permute-start.41 = (bf16[256,1024]{1,0:T(8,128)(2,1)S(1)}, bf16[256,1024]{1,0:T(8,128)(2,1)S(1)}, u32[]{:S(2)}, u32[]{:S(2)}) collective-permute-start(bf16[256,1024]{1,0:T(8,128)(2,1)S(1)} %copy-done.14), channel_id=1, source_target_pairs={{0,4},{4,0},{8,12},{12,8},{16,20},{20,16},{24,28},{28,24},{32,36},... | collective-permute-start | bytes 1572872 | tf_op jit(solution)/shard_map/ppermute | solution.py:25
  200.8 25.0 %collective-permute-start.42 = (bf16[256,1024]{1,0:T(8,128)(2,1)S(1)}, bf16[256,1024]{1,0:T(8,128)(2,1)S(1)}, u32[]{:S(2)}, u32[]{:S(2)}) collective-permute-start(bf16[256,1024]{1,0:T(8,128)(2,1)S(1)} %copy-done.13), channel_id=1, source_target_pairs={{0,8},{4,12},{8,0},{12,4},{16,24},{20,28},{24,16},{28,20},{32,40},... | collective-permute-start | bytes 1572872 | tf_op jit(solution)/shard_map/ppermute | solution.py:25
  203.2 24.8 %collective-permute-start.43 = (bf16[256,1024]{1,0:T(8,128)(2,1)S(1)}, bf16[256,1024]{1,0:T(8,128)(2,1)S(1)}, u32[]{:S(2)}, u32[]{:S(2)}) collective-permute-start(bf16[256,1024]{1,0:T(8,128)(2,1)S(1)} %copy-done.12), channel_id=1, source_target_pairs={{0,12},{4,8},{8,4},{12,0},{16,28},{20,24},{24,20},{28,16},{32,44},... | collective-permute-start | bytes 1572872 | tf_op jit(solution)/shard_map/ppermute | solution.py:25
  215.0 12.9 %collective-permute-start.39 = (bf16[64,2048]{1,0:T(8,128)(2,1)}, bf16[64,2048]{1,0:T(8,128)(2,1)S(1)}, u32[]{:S(2)}, u32[]{:S(2)}) collective-permute-start(bf16[64,2048]{1,0:T(8,128)(2,1)} %get-tuple-element.159.refs_0_), channel_id=1, source_target_pairs={{0,1},{1,0},{2,3},{3,2},{4,5},{5,4},{6,7},{7,6},{8,9},{9,8},{10,11... | collective-permute-start | bytes 786440 | tf_op jit(solution)/shard_map/ppermute | solution.py:25
  256.3 128.7 %reduce-scatter.8.cloned.1.call-start = ((), (), s32[]{:S(2)}) async-start(), calls=%async_computation.5 | async-start | bytes 3145728 | tf_op jit(solution)/shard_map/reduce_scatter | solution.py:46
  256.3 9.1 %collective-permute-start.44 = (bf16[48,128,256]{2,1,0:T(8,128)(2,1)}, bf16[48,128,256]{2,1,0:T(8,128)(2,1)S(1)}, u32[]{:S(2)}, u32[]{:S(2)}) collective-permute-start(bf16[48,128,256]{2,1,0:T(8,128)(2,1)} %get-tuple-element.161), channel_id=1, source_target_pairs={{0,1},{1,0},{2,3},{3,2},{4,5},{5,4},{6,7},{7,6},{8,9},{9,8},{10,11... | collective-permute-start | bytes 9437192 | tf_op jit(solution)/shard_map/ppermute | solution.py:25
  258.6 12.5 %collective-permute-start.56 = (bf16[256,512]{1,0:T(8,128)(2,1)}, bf16[256,512]{1,0:T(8,128)(2,1)}, u32[]{:S(2)}, u32[]{:S(2)}) collective-permute-start(bf16[256,512]{1,0:T(8,128)(2,1)} %get-tuple-element.180), channel_id=1, source_target_pairs={{0,32},{4,36},{8,40},{12,44},{16,48},{20,52},{24,56},{28,60},{32,0... | collective-permute-start | bytes 786440 | tf_op jit(solution)/shard_map/ppermute | solution.py:25
  258.6 13.7 %collective-permute-start.57 = (bf16[256,512]{1,0:T(8,128)(2,1)}, bf16[256,512]{1,0:T(8,128)(2,1)}, u32[]{:S(2)}, u32[]{:S(2)}) collective-permute-start(bf16[256,512]{1,0:T(8,128)(2,1)} %get-tuple-element.181), channel_id=1, source_target_pairs={{0,64},{4,68},{8,72},{12,76},{16,80},{20,84},{24,88},{28,92},{32,9... | collective-permute-start | bytes 786440 | tf_op jit(solution)/shard_map/ppermute | solution.py:25
  258.9 16.8 %collective-permute-start.58 = (bf16[256,512]{1,0:T(8,128)(2,1)S(1)}, bf16[256,512]{1,0:T(8,128)(2,1)}, u32[]{:S(2)}, u32[]{:S(2)}) collective-permute-start(bf16[256,512]{1,0:T(8,128)(2,1)S(1)} %copy-done.59), channel_id=1, source_target_pairs={{0,96},{4,100},{8,104},{12,108},{16,112},{20,116},{24,120},{28,124... | collective-permute-start | bytes 786440 | tf_op jit(solution)/shard_map/ppermute | solution.py:25
  281.9 131.5 %reduce-scatter.4.cloned.1.call-start = ((), (), s32[]{:S(2)}) async-start(), calls=%async_computation.3 | async-start | bytes 3932160 | tf_op jit(solution)/shard_map/reduce_scatter | solution.py:46
  282.8 12.7 %collective-permute-start.46 = (bf16[4,128,256]{2,1,0:T(8,128)(2,1)S(1)}, bf16[4,128,256]{2,1,0:T(8,128)(2,1)S(1)}, u32[]{:S(2)}, u32[]{:S(2)}) collective-permute-start(bf16[4,128,256]{2,1,0:T(8,128)(2,1)S(1)} %copy-done.61), channel_id=1, source_target_pairs={{0,32},{4,36},{8,40},{12,44},{16,48},{20,52},{24,56},{28,60},{32,0... | collective-permute-start | bytes 786440 | tf_op jit(solution)/shard_map/ppermute | solution.py:25
  282.9 14.0 %collective-permute-start.47 = (bf16[4,128,256]{2,1,0:T(8,128)(2,1)S(1)}, bf16[4,128,256]{2,1,0:T(8,128)(2,1)S(1)}, u32[]{:S(2)}, u32[]{:S(2)}) collective-permute-start(bf16[4,128,256]{2,1,0:T(8,128)(2,1)S(1)} %copy-done.70), channel_id=1, source_target_pairs={{0,96},{4,100},{8,104},{12,108},{16,112},{20,116},{24,120},{28,124... | collective-permute-start | bytes 786440 | tf_op jit(solution)/shard_map/ppermute | solution.py:25
  283.4 13.5 %collective-permute-start.48 = (bf16[4,128,256]{2,1,0:T(8,128)(2,1)S(1)}, bf16[4,128,256]{2,1,0:T(8,128)(2,1)S(1)}, u32[]{:S(2)}, u32[]{:S(2)}) collective-permute-start(bf16[4,128,256]{2,1,0:T(8,128)(2,1)S(1)} %copy-done.69), channel_id=1, source_target_pairs={{0,4},{4,0},{8,12},{12,8},{16,20},{20,16},{24,28},{28,24},{32,36},... | collective-permute-start | bytes 786440 | tf_op jit(solution)/shard_map/ppermute | solution.py:25
  283.4 13.5 %collective-permute-start.49 = (bf16[4,128,256]{2,1,0:T(8,128)(2,1)S(1)}, bf16[4,128,256]{2,1,0:T(8,128)(2,1)S(1)}, u32[]{:S(2)}, u32[]{:S(2)}) collective-permute-start(bf16[4,128,256]{2,1,0:T(8,128)(2,1)S(1)} %copy-done.68), channel_id=1, source_target_pairs={{0,12},{4,8},{8,4},{12,0},{16,28},{20,24},{24,20},{28,16},{32,44},... | collective-permute-start | bytes 786440 | tf_op jit(solution)/shard_map/ppermute | solution.py:25
  303.0 7.8 %collective-permute-start.50 = (bf16[2,160,2048]{2,1,0:T(8,128)(2,1)}, bf16[2,160,2048]{2,1,0:T(8,128)(2,1)S(1)}, u32[]{:S(2)}, u32[]{:S(2)}) collective-permute-start(bf16[2,160,2048]{2,1,0:T(8,128)(2,1)} %gate.3), channel_id=1, source_target_pairs={{0,1},{1,0},{2,3},{3,2},{4,5},{5,4},{6,7},{7,6},{8,9},{9,8},{10,11... | collective-permute-start | bytes 3932168 | tf_op jit(solution)/shard_map/ppermute | solution.py:25
  307.8 15.5 %collective-permute-start.52 = (bf16[8,128,256]{2,1,0:T(8,128)(2,1)}, bf16[8,128,256]{2,1,0:T(8,128)(2,1)}, u32[]{:S(2)}, u32[]{:S(2)}) collective-permute-start(bf16[8,128,256]{2,1,0:T(8,128)(2,1)} %get-tuple-element.169.refs_1_), channel_id=1, source_target_pairs={{0,32},{4,36},{8,40},{12,44},{16,48},{20,52},{24,56},{28,60},{32,0... | collective-permute-start | bytes 1572872 | tf_op jit(solution)/shard_map/ppermute | solution.py:25
  308.1 17.3 %collective-permute-start.53 = (bf16[8,128,256]{2,1,0:T(8,128)(2,1)}, bf16[8,128,256]{2,1,0:T(8,128)(2,1)}, u32[]{:S(2)}, u32[]{:S(2)}) collective-permute-start(bf16[8,128,256]{2,1,0:T(8,128)(2,1)} %get-tuple-element.173), channel_id=1, source_target_pairs={{0,96},{4,100},{8,104},{12,108},{16,112},{20,116},{24,120},{28,124... | collective-permute-start | bytes 1572872 | tf_op jit(solution)/shard_map/ppermute | solution.py:25
  309.7 15.6 %collective-permute-start.54 = (bf16[8,128,256]{2,1,0:T(8,128)(2,1)}, bf16[8,128,256]{2,1,0:T(8,128)(2,1)}, u32[]{:S(2)}, u32[]{:S(2)}) collective-permute-start(bf16[8,128,256]{2,1,0:T(8,128)(2,1)} %get-tuple-element.174), channel_id=1, source_target_pairs={{0,4},{4,0},{8,12},{12,8},{16,20},{20,16},{24,28},{28,24},{32,36},... | collective-permute-start | bytes 1572872 | tf_op jit(solution)/shard_map/ppermute | solution.py:25
  309.7 15.6 %collective-permute-start.55 = (bf16[8,128,256]{2,1,0:T(8,128)(2,1)}, bf16[8,128,256]{2,1,0:T(8,128)(2,1)}, u32[]{:S(2)}, u32[]{:S(2)}) collective-permute-start(bf16[8,128,256]{2,1,0:T(8,128)(2,1)} %get-tuple-element.175), channel_id=1, source_target_pairs={{0,12},{4,8},{8,4},{12,0},{16,28},{20,24},{24,20},{28,16},{32,44},... | collective-permute-start | bytes 1572872 | tf_op jit(solution)/shard_map/ppermute | solution.py:25
  311.4 35.0 %collective-permute-start.51 = (bf16[160,2048]{1,0:T(8,128)(2,1)S(1)}, bf16[160,2048]{1,0:T(8,128)(2,1)S(1)}, u32[]{:S(2)}, u32[]{:S(2)}) collective-permute-start(bf16[160,2048]{1,0:T(8,128)(2,1)S(1)} %fusion.4), channel_id=1, source_target_pairs={{0,2},{1,3},{2,0},{3,1},{4,6},{5,7},{6,4},{7,5},{8,10},{9,11},{10,... | collective-permute-start | bytes 1966088 | tf_op jit(solution)/shard_map/ppermute | solution.py:25
  328.6 8.1 %collective-permute-start.60 = (bf16[2,128,256]{2,1,0:T(8,128)(2,1)}, bf16[2,128,256]{2,1,0:T(8,128)(2,1)}, u32[]{:S(2)}, u32[]{:S(2)}) collective-permute-start(bf16[2,128,256]{2,1,0:T(8,128)(2,1)} %get-tuple-element.186), channel_id=1, source_target_pairs={{0,8},{4,12},{8,0},{12,4},{16,24},{20,28},{24,16},{28,20},{32,40},... | collective-permute-start | bytes 393224 | tf_op jit(solution)/shard_map/ppermute | solution.py:25
  330.5 8.7 %collective-permute-start.61 = (bf16[2,128,256]{2,1,0:T(8,128)(2,1)}, bf16[2,128,256]{2,1,0:T(8,128)(2,1)}, u32[]{:S(2)}, u32[]{:S(2)}) collective-permute-start(bf16[2,128,256]{2,1,0:T(8,128)(2,1)} %get-tuple-element.187), channel_id=1, source_target_pairs={{0,12},{4,8},{8,4},{12,0},{16,28},{20,24},{24,20},{28,16},{32,44},... | collective-permute-start | bytes 393224 | tf_op jit(solution)/shard_map/ppermute | solution.py:25
  333.2 8.3 %collective-permute-start.63 = (bf16[2,128,256]{2,1,0:T(8,128)(2,1)}, bf16[2,128,256]{2,1,0:T(8,128)(2,1)}, u32[]{:S(2)}, u32[]{:S(2)}) collective-permute-start(bf16[2,128,256]{2,1,0:T(8,128)(2,1)} %get-tuple-element.189), channel_id=1, source_target_pairs={{0,64},{4,68},{8,72},{12,76},{16,80},{20,84},{24,88},{28,92},{32,9... | collective-permute-start | bytes 393224 | tf_op jit(solution)/shard_map/ppermute | solution.py:25
  351.6 107.4 %all-gather.19.cloned.1.call-start = ((), (), s32[]{:S(2)}) async-start(), calls=%async_computation.10 | async-start | bytes 1474560 | tf_op jit(solution)/shard_map/all_gather | solution.py:1251
  375.4 11.4 %collective-permute-start.75 = (f32[16,2048]{1,0:T(8,128)S(1)}, f32[16,2048]{1,0:T(8,128)S(1)}, u32[]{:S(2)}, u32[]{:S(2)}) collective-permute-start(f32[16,2048]{1,0:T(8,128)S(1)} %fusion.17), channel_id=1, source_target_pairs={{0,2},{1,3},{2,0},{3,1},{4,6},{5,7},{6,4},{7,5},{8,10},{9,11},{10,... | collective-permute-start | bytes 393224 | tf_op jit(solution)/shard_map/ppermute | solution.py:25
  375.5 8.2 %collective-permute-start.76 = (bf16[256,192]{1,0:T(8,128)(2,1)}, bf16[256,192]{1,0:T(8,128)(2,1)S(1)}, u32[]{:S(2)}, u32[]{:S(2)}) collective-permute-start(bf16[256,192]{1,0:T(8,128)(2,1)} %get-tuple-element.207), channel_id=1, source_target_pairs={{0,4},{4,0},{8,12},{12,8},{16,20},{20,16},{24,28},{28,24},{32,36},... | collective-permute-start | bytes 294920 | tf_op jit(solution)/shard_map/ppermute | solution.py:25
  375.6 11.9 %collective-permute-start.77 = (bf16[256,192]{1,0:T(8,128)(2,1)}, bf16[256,192]{1,0:T(8,128)(2,1)S(1)}, u32[]{:S(2)}, u32[]{:S(2)}) collective-permute-start(bf16[256,192]{1,0:T(8,128)(2,1)} %get-tuple-element.208), channel_id=1, source_target_pairs={{0,8},{4,12},{8,0},{12,4},{16,24},{20,28},{24,16},{28,20},{32,40},... | collective-permute-start | bytes 294920 | tf_op jit(solution)/shard_map/ppermute | solution.py:25
  377.5 10.0 %collective-permute-start.78 = (bf16[256,192]{1,0:T(8,128)(2,1)}, bf16[256,192]{1,0:T(8,128)(2,1)S(1)}, u32[]{:S(2)}, u32[]{:S(2)}) collective-permute-start(bf16[256,192]{1,0:T(8,128)(2,1)} %get-tuple-element.209), channel_id=1, source_target_pairs={{0,12},{4,8},{8,4},{12,0},{16,28},{20,24},{24,20},{28,16},{32,44},... | collective-permute-start | bytes 294920 | tf_op jit(solution)/shard_map/ppermute | solution.py:25
  380.3 15.3 %collective-permute-start.73 = (bf16[256,1024]{1,0:T(8,128)(2,1)}, bf16[256,1024]{1,0:T(8,128)(2,1)S(1)}, u32[]{:S(2)}, u32[]{:S(2)}) collective-permute-start(bf16[256,1024]{1,0:T(8,128)(2,1)} %dynamic-slice_bitcast_fusion), channel_id=1, source_target_pairs={{0,16},{4,20},{8,24},{12,28},{16,0},{20,4},{24,8},{28,12},{32,48},... | collective-permute-start | bytes 1572872 | tf_op jit(solution)/shard_map/ppermute | solution.py:25
  383.7 9.6 %collective-permute-start.68 = (bf16[128,2048]{1,0:T(8,128)(2,1)}, bf16[128,2048]{1,0:T(8,128)(2,1)S(1)}, u32[]{:S(2)}, u32[]{:S(2)}) collective-permute-start(bf16[128,2048]{1,0:T(8,128)(2,1)} %get-tuple-element.198), channel_id=1, source_target_pairs={{0,1},{1,0},{2,3},{3,2},{4,5},{5,4},{6,7},{7,6},{8,9},{9,8},{10,11... | collective-permute-start | bytes 1572872 | tf_op jit(solution)/shard_map/ppermute | solution.py:25
  386.9 13.0 %collective-permute-start.85 = (bf16[2,64,2048]{2,1,0:T(8,128)(2,1)}, bf16[2,64,2048]{2,1,0:T(8,128)(2,1)S(1)}, u32[]{:S(2)}, u32[]{:S(2)}) collective-permute-start(bf16[2,64,2048]{2,1,0:T(8,128)(2,1)} %slice.353), channel_id=1, source_target_pairs={{0,4},{4,0},{8,12},{12,8},{16,20},{20,16},{24,28},{28,24},{32,36},... | collective-permute-start | bytes 1572872 | tf_op jit(solution)/shard_map/ppermute | solution.py:25
  393.3 15.0 %collective-permute-start.79 = (bf16[2,2,256,256]{3,2,1,0:T(8,128)(2,1)}, bf16[2,2,256,256]{3,2,1,0:T(8,128)(2,1)S(1)}, u32[]{:S(2)}, u32[]{:S(2)}) collective-permute-start(bf16[2,2,256,256]{3,2,1,0:T(8,128)(2,1)} %get-tuple-element.211), channel_id=1, source_target_pairs={{0,32},{4,36},{8,40},{12,44},{16,48},{20,52},{24,56},{28,60},{32,0... | collective-permute-start | bytes 1572872 | tf_op jit(solution)/shard_map/ppermute | solution.py:25
  394.3 36.9 %collective-permute-start.69 = (bf16[64,2048]{1,0:T(8,128)(2,1)S(1)}, bf16[64,2048]{1,0:T(8,128)(2,1)S(1)}, u32[]{:S(2)}, u32[]{:S(2)}) collective-permute-start(bf16[64,2048]{1,0:T(8,128)(2,1)S(1)} %slice.392), channel_id=1, source_target_pairs={{0,2},{1,3},{2,0},{3,1},{4,6},{5,7},{6,4},{7,5},{8,10},{9,11},{10,... | collective-permute-start | bytes 786440 | tf_op jit(solution)/shard_map/ppermute | solution.py:25
  408.4 9.0 %collective-permute-start.80 = (bf16[2,256,256]{2,1,0:T(8,128)(2,1)S(1)}, bf16[2,256,256]{2,1,0:T(8,128)(2,1)S(1)}, u32[]{:S(2)}, u32[]{:S(2)}) collective-permute-start(bf16[2,256,256]{2,1,0:T(8,128)(2,1)S(1)} %slice_bitcast_fusion.3), channel_id=1, source_target_pairs={{0,96},{4,100},{8,104},{12,108},{16,112},{20,116},{24,120},{28,124... | collective-permute-start | bytes 786440 | tf_op jit(solution)/shard_map/ppermute | solution.py:25
  411.1 28.3 %collective-permute-start.86 = (bf16[64,2048]{1,0:T(8,128)(2,1)S(1)}, bf16[64,2048]{1,0:T(8,128)(2,1)S(1)}, u32[]{:S(2)}, u32[]{:S(2)}) collective-permute-start(bf16[64,2048]{1,0:T(8,128)(2,1)S(1)} %get-tuple-element.333), channel_id=1, source_target_pairs={{0,12},{4,8},{8,4},{12,0},{16,28},{20,24},{24,20},{28,16},{32,44},... | collective-permute-start | bytes 786440 | tf_op jit(solution)/shard_map/ppermute | solution.py:25
  414.5 10.9 %collective-permute-start.65 = (bf16[256,768]{1,0:T(8,128)(2,1)S(1)}, bf16[256,768]{1,0:T(8,128)(2,1)S(1)}, u32[]{:S(2)}, u32[]{:S(2)}) collective-permute-start(bf16[256,768]{1,0:T(8,128)(2,1)S(1)} %dynamic-slice_bitcast_fusion.1), channel_id=1, source_target_pairs={{0,16},{4,20},{8,24},{12,28},{16,0},{20,4},{24,8},{28,12},{32,48},... | collective-permute-start | bytes 1179656 | tf_op jit(solution)/shard_map/ppermute | solution.py:25
  417.5 10.7 %collective-permute-start.81 = (bf16[256,256]{1,0:T(8,128)(2,1)S(1)}, bf16[256,256]{1,0:T(8,128)(2,1)S(1)}, u32[]{:S(2)}, u32[]{:S(2)}) collective-permute-start(bf16[256,256]{1,0:T(8,128)(2,1)S(1)} %slice_bitcast_fusion.9), channel_id=1, source_target_pairs={{0,16},{4,20},{8,24},{12,28},{16,0},{20,4},{24,8},{28,12},{32,48},... | collective-permute-start | bytes 393224 | tf_op jit(solution)/shard_map/ppermute | solution.py:25
  431.2 18.4 %collective-permute-start.82 = (bf16[64,2048]{1,0:T(8,128)(2,1)}, bf16[64,2048]{1,0:T(8,128)(2,1)S(1)}, u32[]{:S(2)}, u32[]{:S(2)}) collective-permute-start(bf16[64,2048]{1,0:T(8,128)(2,1)} %get-tuple-element.213), channel_id=1, source_target_pairs={{0,4},{4,0},{8,12},{12,8},{16,20},{20,16},{24,28},{28,24},{32,36},... | collective-permute-start | bytes 786440 | tf_op jit(solution)/shard_map/ppermute | solution.py:25
  434.5 10.3 %collective-permute-start.71 = (bf16[64,2048]{1,0:T(8,128)(2,1)}, bf16[64,2048]{1,0:T(8,128)(2,1)S(1)}, u32[]{:S(2)}, u32[]{:S(2)}) collective-permute-start(bf16[64,2048]{1,0:T(8,128)(2,1)} %final.1), channel_id=1, source_target_pairs={{0,2},{1,3},{2,0},{3,1},{4,6},{5,7},{6,4},{7,5},{8,10},{9,11},{10,... | collective-permute-start | bytes 786440 | tf_op jit(solution)/shard_map/ppermute | solution.py:25
  435.5 14.0 %collective-permute-start.83 = (bf16[64,2048]{1,0:T(8,128)(2,1)S(1)}, bf16[64,2048]{1,0:T(8,128)(2,1)S(1)}, u32[]{:S(2)}, u32[]{:S(2)}) collective-permute-start(bf16[64,2048]{1,0:T(8,128)(2,1)S(1)} %copy-done.65), channel_id=1, source_target_pairs={{0,8},{4,12},{8,0},{12,4},{16,24},{20,28},{24,16},{28,20},{32,40},... | collective-permute-start | bytes 786440 | tf_op jit(solution)/shard_map/ppermute | solution.py:25
  437.3 13.2 %collective-permute-start.84 = (bf16[64,2048]{1,0:T(8,128)(2,1)S(1)}, bf16[64,2048]{1,0:T(8,128)(2,1)S(1)}, u32[]{:S(2)}, u32[]{:S(2)}) collective-permute-start(bf16[64,2048]{1,0:T(8,128)(2,1)S(1)} %copy-done.64), channel_id=1, source_target_pairs={{0,12},{4,8},{8,4},{12,0},{16,28},{20,24},{24,20},{28,16},{32,44},... | collective-permute-start | bytes 786440 | tf_op jit(solution)/shard_map/ppermute | solution.py:25
  439.4 17.9 %collective-permute-start.70 = (bf16[64,2048]{1,0:T(8,128)(2,1)}, bf16[64,2048]{1,0:T(8,128)(2,1)S(1)}, u32[]{:S(2)}, u32[]{:S(2)}) collective-permute-start(bf16[64,2048]{1,0:T(8,128)(2,1)} %final.1), channel_id=1, source_target_pairs={{0,1},{1,0},{2,3},{3,2},{4,5},{5,4},{6,7},{7,6},{8,9},{9,8},{10,11... | collective-permute-start | bytes 786440 | tf_op jit(solution)/shard_map/ppermute | solution.py:25
  444.8 12.5 %collective-permute-start.72 = (bf16[64,2048]{1,0:T(8,128)(2,1)S(1)}, bf16[64,2048]{1,0:T(8,128)(2,1)S(1)}, u32[]{:S(2)}, u32[]{:S(2)}) collective-permute-start(bf16[64,2048]{1,0:T(8,128)(2,1)S(1)} %collective-permute-done.71), channel_id=1, source_target_pairs={{0,1},{1,0},{2,3},{3,2},{4,5},{5,4},{6,7},{7,6},{8,9},{9,8},{10,11... | collective-permute-start | bytes 786440 | tf_op jit(solution)/shard_map/ppermute | solution.py:25
  (112 other events, 706.1 us)
Sparse Core Ops, SparseCore 0:
  47.3 36.3 all-gather.10
  85.3 48.6 all-gather.12
  140.0 47.7 all-gather.14
  189.4 48.6 all-gather.16
  256.4 61.1 reduce-scatter.5
  320.5 37.6 reduce-scatter.7
  360.6 38.9 reduce-scatter.3
  426.4 26.2 all-gather.18

commit v2 on v1

--- a/solution.py
+++ b/solution.py
@@ -1107,7 +1107,6 @@
     wide_cuts, down_cuts = ff_grads(where, grad_ff_parts, gate_pre, up_pre, w_down)
     kept, sent = ff_back(where, wide_cuts, w_gate, w_up)
     wide_cuts = [wide_cuts[0]] + [hop(wide_cuts[k], "ctx", k) for k in (1, 2, 3)]
-    down_cuts = [down_cuts[0]] + [hop(down_cuts[k], "ctx", 8 * k) for k in (1, 2, 3)]
     kept, came = scatter_wt(kept, sent)
 
     grad_attn, branch, own_part, gains_resid, small_mine, small_sent = in_one(
@@ -1156,7 +1155,6 @@
         (came_rest, wide),
     )
     wide = scatter_group(wide, GROUP_Y)
-    down = down_product(where, act_group, down_cuts, far[0])
     grad_query_b, gain_query_part = in_one(
         query_back_kernel,
         (heads_b, ((1, HEAD), F32)),
@@ -1174,14 +1172,12 @@
     small = small_mine.astype(F32) + hop(small_sent, "wt", 1).astype(F32)
     small_far = small[1].astype(BF)
     small = (small[0] + hop(small_far, "wt", 2).astype(F32)).astype(BF)
-    down_event = down
-    down = scatter_group(down, GROUP_Z).reshape(4, 64, -1)
     inner = in_one(
         inner_kernel,
         (blocks(2, F32),) * 2 + (blocks(2, BF),) * 6,
         (*bases[:2], *hops(bases[2:], (8, 24, 1, 3))),
         "inner",
-        (grad_query_b, down_event),
+        (grad_query_b,),
     )
     last = in_one(
         last_kernel,
@@ -1190,6 +1186,12 @@
         "last",
     )
     across = hop(last[2], "ctx", 4)
+    down_cuts = [down_cuts[0]] + [
+        hop(value, "ctx", 8 * k) for k, value in zip((1, 2, 3), hold(down_cuts[1:], last[2]))
+    ]
+    down = down_product(where, act_group, down_cuts, last[2])
+    down_event = down
+    down = scatter_group(down, GROUP_Z).reshape(4, 64, -1)
     (turn,) = in_one(
         turn_kernel,
         (((D, 768), BF),),
@@ -1215,7 +1217,7 @@
         + (((2 * STRETCH, 192), BF),) * 4,
         (home, hop(away, "wt", 1), grad_query_b, w_query, w_key, w_value, stream),
         "normed_back",
-        (wide,),
+        (wide, down_event),
         spots=spots,
     )
     def fold_z(value):

time: 479 us -> 532 us (1.11)
  waiting for transfers between devices: 116 us -> 165 us
    ppermute x87, waiting for transfers between devices: 114 us -> 164 us  [hop(): lax.ppermute(value, axis, [(i, i ^ mask) for i in range(lax.axis_size(axi...]
    ppermute x87, starting transfers between devices: 117 us -> 123 us  [hop(): lax.ppermute(value, axis, [(i, i ^ mask) for i in range(lax.axis_size(axi...]
    unnamed x166 -> x176, local copies, waits for them, and re-layouts: 20.3 us -> 21.6 us
  transfers between devices with their start and end apart: 95 -> 95, of which waited for: 37 -> 39; matrix products, arithmetic and copies ran while one was open for 10% -> 9% of each run, Pallas kernels for 31% -> 27%
where the time goes in v2:
time: 532 us; the launch traced here: 523 us
  waiting for transfers between devices  165 us (31%)
  Pallas kernels  150 us (28%)
  starting transfers between devices  123 us (23%)
  local copies, waits for them, and re-layouts  45.6 us (9%)
  other arithmetic  23 us (4%)
  between operations  15.6 us (3%)
    ppermute x87, waiting for transfers between devices, hop(): lax.ppermute(value, axis, [(i, i ^ mask) for i in range(lax.axis_size(axi...  164 us
    ppermute x87, starting transfers between devices, hop(): lax.ppermute(value, axis, [(i, i ^ mask) for i in range(lax.axis_size(axi...  123 us
    pallas_call x19, Pallas kernels, in_one(): pl.pallas_call(kernel, out_shape=tuple((jax.ShapeDtypeStruct(shape, kind)...  65.7 us
    unnamed x176, local copies, waits for them, and re-layouts  21.6 us
    pallas_call x1, Pallas kernels, ff_forward(): pl.pallas_call(ff_forward_kernel, grid=(units // UNITS,), out_shape=(jax....  15.7 us
    pallas_call x1, Pallas kernels, attend_backward(): pl.pallas_call(backward_kernel, out_shape=(jax.ShapeDtypeStruct((rows, 2...  15.2 us
    pallas_call x1, Pallas kernels, ff_grads(): pl.pallas_call(ff_grads_kernel, grid_spec=pltpu.PrefetchScalarGridSpec(nu...  11 us
    pallas_call x1, Pallas kernels, ff_back(): pl.pallas_call(ff_back_kernel, grid_spec=pltpu.PrefetchScalarGridSpec(num...  11 us
  transfers between devices with their start and end apart: 95, of which 39 were waited for; matrix products, arithmetic and copies ran while one was open for 9% of the time, Pallas kernels for 27%

profile of v2, /device:TPU:1, one launch (start us, length us, event | category | flops | bytes accessed | tf_op | source)
XLA Modules:
  0.0 522.7 jit_solution(14952669474505570195)
XLA Ops:
  7.9 3.2 input.1
  18.4 3.7 collective-permute-start.1
  23.0 3.2 collective-permute-done.1
  27.5 2.6 collective-permute-start.6
  31.5 2.4 collective-permute-start.3
  38.6 2.8 collective-permute-done.4.refs_3_
  44.4 2.7 pack.1
  48.0 2.7 collective-permute-start.9
  54.0 5.9 %collective-permute-done.8 = bf16[1024,256]{1,0:T(8,128)(2,1)S(1)} collective-permute-done((bf16[1024,256]{1,0:T(8,128)(2,1)S(1)}, bf16[1024,256]{1,0:T(8,128)(2,1)S(1)}, u32[]{:S(2)}, u32[]{:S(2)}) %collective-permute-start.8) | collective-permute-done | bytes 524320 | tf_op jit(solution)/shard_map/ppermute | solution.py:25
  59.9 2.7 collective-permute-start.10
  63.4 2.8 collective-permute-start.21
  72.0 3.4 collective-permute-done.14
  80.2 3.5 query.1
  84.7 10.8 %attend_forward.1 = (bf16[256,512]{1,0:T(8,128)(2,1)}, f32[256,512]{1,0:T(8,128)}, f32[2,8,256]{2,1,0:T(8,128)}, f32[128,2048]{1,0:T(8,128)}, bf16[128,2048]{1,0:T(8,128)(2,1)}) custom-call(s32[157]{0:T(256)} %concatenate.52.meta, bf16[256,512]{1,0:T(8,128)(2,1)} %get-tuple-element.133.q_ref, bf16[512,2048]{1,0:T(8,128)(2,1)} %w_ref.3, ...), custom_call_target="tpu_custom_call" | custom-call | flops 3000000000 | bytes 10000000 | tf_op jit(solution)/shard_map/attend_forward/pallas_call | solution.py:317
  102.6 5.1 collective-permute-done.27.came
  108.3 3.3 mid.1
  113.6 5.1 collective-permute-done.28.refs_1_
  122.5 15.7 %ff_forward.1 = (f32[256,2048]{1,0:T(8,128)}, f32[256,2048]{1,0:T(8,128)}, bf16[256,2048]{1,0:T(8,128)(2,1)}, bf16[256,2048]{1,0:T(8,128)(2,1)}, f32[128,2048]{1,0:T(8,128)}, /*index=5*/bf16[128,2048]{1,0:T(8,128)(2,1)}) custom-call(bf16[64,2048]{1,0:T(8,128)(2,1)} %get-tuple-element.137.refs_0_, bf16[64,2048]{1,0:T(8,128)(2,1)} %copy-done.22, ...), custom_call_target="tpu_custom_call" | custom-call | flops 6442450944 | bytes 30000000 | tf_op jit(solution)/shard_map/ff_forward/pallas_call | solution.py:402
  147.5 5.0 collective-permute-done.32.came
  153.2 8.2 %join.1 = (bf16[64,2048]{1,0:T(8,128)(2,1)}, f32[64,2048]{1,0:T(8,128)}, bf16[64,2304]{1,0:T(8,128)(2,1)}, f32[8,2048]{1,0:T(8,128)}, bf16[2,128,2048]{2,1,0:T(8,128)(2,1)}, /*index=5*/bf16[2,128,2048]{2,1,0:T(8,128)(2,1)}) custom-call(f32[64,2048]{1,0:T(8,128)} %slice.331.kept, bf16[64,2048]{1,0:T(8,128)(2,1)} %copy-done.34, ...), custom_call_target="tpu_custom_call" | custom-call | flops 1000000000 | bytes 5000000 | tf_op jit(solution)/shard_map/join/pallas_call | solution.py:767
  163.0 5.6 %collective-permute-done.33.refs_1_ = bf16[64,2048]{1,0:T(8,128)(2,1)S(1)} collective-permute-done((bf16[64,2048]{1,0:T(8,128)(2,1)}, bf16[64,2048]{1,0:T(8,128)(2,1)S(1)}, u32[]{:S(2)}, u32[]{:S(2)}) %collective-permute-start.33) | collective-permute-done | bytes 262176 | tf_op jit(solution)/shard_map/ppermute | solution.py:25
  172.6 11.0 %ff_grads.1 = (bf16[256,1024]{1,0:T(8,128)(2,1)}, bf16[256,1024]{1,0:T(8,128)(2,1)}, bf16[256,1024]{1,0:T(8,128)(2,1)}, bf16[256,1024]{1,0:T(8,128)(2,1)}, bf16[...) custom-call(s32[3]{0:T(128)} %pad_add_fusion.me.where, ...), custom_call_target="tpu_custom_call" | custom-call | flops 2147483648 | bytes 10000000 | tf_op jit(solution)/shard_map/ff_grads/pallas_call | solution.py:460
  183.5 11.0 %ff_back.1 = (f32[128,2048]{1,0:T(8,128)}, bf16[128,2048]{1,0:T(8,128)(2,1)}) custom-call(s32[3]{0:T(128)} %pad_add_fusion.me.where, bf16[256,1024]{1,0:T(8,128)(2,1)} %get-tuple-element.145.refs_0_, bf16[256,1024]{1,0:T(8,128)(2,1)} %get-tuple-element.146.refs_1_, bf16[256,1024]{1,0:T(8,128)(2,1)} %get-tuple-element.147.refs_2_, ...), custom_call_target="tpu_custom_call" | custom-call | flops 4294967296 | bytes 20000000 | tf_op jit(solution)/shard_map/ff_back/pallas_call | solution.py:506
  199.0 6.0 %collective-permute-start.42 = (bf16[256,1024]{1,0:T(8,128)(2,1)S(1)}, bf16[256,1024]{1,0:T(8,128)(2,1)}, u32[]{:S(2)}, u32[]{:S(2)}) collective-permute-start(bf16[256,1024]{1,0:T(8,128)(2,1)S(1)} %copy-done.13), channel_id=1, source_target_pairs={{0,8},{4,12},{8,0},{12,4},{16,24},{20,28},{24,16},{28,20},{32,40},... | collective-permute-start | bytes 1572872 | tf_op jit(solution)/shard_map/ppermute | solution.py:25
  206.7 5.9 %resid.1 = (bf16[64,2048]{1,0:T(8,128)(2,1)}, f32[64,2048]{1,0:T(8,128)}, f32[64,2048]{1,0:T(8,128)}, f32[8,2048]{1,0:T(8,128)}, bf16[2,160,2048]{2,1,0:T(8,128)(2,1)}, /*index=5*/bf16[2,160,2048]{2,1,0:T(8,128)(2,1)}) custom-call(f32[64,2048]{1,0:T(8,128)} %slice.334.kept, bf16[64,2048]{1,0:T(8,128)(2,1)} %copy-done.29, ...), custom_call_target="tpu_custom_call" | custom-call | flops 1000000000 | bytes 5000000 | tf_op jit(solution)/shard_map/resid/pallas_call | solution.py:767
  215.2 4.3 collective-permute-done.38.refs_1_
  221.6 6.3 %collective-permute-done.42.refs_25_.refs_2_ = bf16[256,1024]{1,0:T(8,128)(2,1)} collective-permute-done((bf16[256,1024]{1,0:T(8,128)(2,1)S(1)}, bf16[256,1024]{1,0:T(8,128)(2,1)}, u32[]{:S(2)}, u32[]{:S(2)}) %collective-permute-start.42) | collective-permute-done | bytes 524320 | tf_op jit(solution)/shard_map/ppermute | solution.py:25
  230.8 15.2 %attend_backward.1 = (f32[256,512]{1,0:T(8,128)}, bf16[16,128,256]{2,1,0:T(8,128)(2,1)}, bf16[48,128,256]{2,1,0:T(8,128)(2,1)}, bf16[16,128,256]{2,1,0:T(8,128)(2,1)}, bf16[48,128,256]{2,1,0:T(8,128)(2,1)}) custom-call(s32[157]{0:T(256)} %concatenate.52.meta, bf16[256,512]{1,0:T(8,128)(2,1)} %get-tuple-element.133.q_ref, ...), custom_call_target="tpu_custom_call" | custom-call | flops 10000000000 | bytes 20000000 | tf_op jit(solution)/shard_map/attend_backward/pallas_call | solution.py:344
  246.0 9.3 %wide_product.1.refs_1_ = bf16[2048,1024]{1,0:T(8,128)(2,1)} custom-call(s32[3]{0:T(128)} %pad_add_fusion.me.where, bf16[4,256,2048]{2,1,0:T(8,128)(2,1)} %bitcast.160, bf16[256,1024]{1,0:T(8,128)(2,1)} %get-tuple-element.145.refs_0_, bf16[256,1024]{1,0:T(8,128)(2,1)} %copy-done.57, bf16[256,1024]{1,0:T(8,128)(2,1)} %collective-permute-done.42.refs_25_.refs_2_, ...), custom_call_target="tpu_custom_call" | custom-call | flops 5000000000 | bytes 10000000 | tf_op jit(solution)/shard_map/wide_product/pallas_call | solution.py:815
  257.4 6.9 %collective-permute-done.45.came = bf16[16,128,256]{2,1,0:T(8,128)(2,1)S(1)} collective-permute-done((bf16[16,128,256]{2,1,0:T(8,128)(2,1)}, bf16[16,128,256]{2,1,0:T(8,128)(2,1)S(1)}, u32[]{:S(2)}, u32[]{:S(2)}) %collective-permute-start.45) | collective-permute-done | bytes 1048608 | tf_op jit(solution)/shard_map/ppermute | solution.py:25
  267.0 2.8 far.1
  270.9 6.1 %collective-permute-start.49 = (bf16[4,128,256]{2,1,0:T(8,128)(2,1)}, bf16[4,128,256]{2,1,0:T(8,128)(2,1)S(1)}, u32[]{:S(2)}, u32[]{:S(2)}) collective-permute-start(bf16[4,128,256]{2,1,0:T(8,128)(2,1)} %get-tuple-element.171), channel_id=1, source_target_pairs={{0,12},{4,8},{8,4},{12,0},{16,28},{20,24},{24,20},{28,16},{32,44},... | collective-permute-start | bytes 786440 | tf_op jit(solution)/shard_map/ppermute | solution.py:25
  276.9 6.8 %collective-permute-done.46.refs_0_ = bf16[4,128,256]{2,1,0:T(8,128)(2,1)S(1)} collective-permute-done((bf16[4,128,256]{2,1,0:T(8,128)(2,1)}, bf16[4,128,256]{2,1,0:T(8,128)(2,1)S(1)}, u32[]{:S(2)}, u32[]{:S(2)}) %collective-permute-start.46) | collective-permute-done | bytes 262176 | tf_op jit(solution)/shard_map/ppermute | solution.py:25
  286.9 5.3 %near.1 = (f32[8,128,256]{2,1,0:T(8,128)}, f32[8,128,256]{2,1,0:T(8,128)}, bf16[8,128,256]{2,1,0:T(8,128)(2,1)}, bf16[8,128,256]{2,1,0:T(8,128)(2,1)}, bf16[8,12...) custom-call(bf16[48,128,256]{2,1,0:T(8,128)(2,1)} %get-tuple-element.163.own, bf16[48,128,256]{2,1,0:T(8,128)(2,1)} %copy-done.2, ...), custom_call_target="tpu_custom_call" | custom-call | flops 1000000000 | bytes 5000000 | tf_op jit(solution)/shard_map/near/pallas_call | solution.py:767
  292.3 6.8 %collective-permute-start.55 = (bf16[8,128,256]{2,1,0:T(8,128)(2,1)}, bf16[8,128,256]{2,1,0:T(8,128)(2,1)S(1)}, u32[]{:S(2)}, u32[]{:S(2)}) collective-permute-start(bf16[8,128,256]{2,1,0:T(8,128)(2,1)} %get-tuple-element.178), channel_id=1, source_target_pairs={{0,12},{4,8},{8,4},{12,0},{16,28},{20,24},{24,20},{28,16},{32,44},... | collective-permute-start | bytes 1572872 | tf_op jit(solution)/shard_map/ppermute | solution.py:25
  301.4 15.9 %collective-permute-done.52.refs_0_ = bf16[8,128,256]{2,1,0:T(8,128)(2,1)S(1)} collective-permute-done((bf16[8,128,256]{2,1,0:T(8,128)(2,1)}, bf16[8,128,256]{2,1,0:T(8,128)(2,1)S(1)}, u32[]{:S(2)}, u32[]{:S(2)}) %collective-permute-start.52) | collective-permute-done | bytes 524320 | tf_op jit(solution)/shard_map/ppermute | solution.py:25
  319.6 3.3 inner.1
  322.9 4.0 collective-permute-start.57
  328.6 2.4 collective-permute-start.61
  332.6 2.6 collective-permute-done.58.refs_2_
  343.5 4.6 collective-permute-done.66.refs_2_
  348.1 5.2 %collective-permute-done.67.refs_3_ = bf16[256,512]{1,0:T(8,128)(2,1)S(1)} collective-permute-done((bf16[256,512]{1,0:T(8,128)(2,1)}, bf16[256,512]{1,0:T(8,128)(2,1)S(1)}, u32[]{:S(2)}, u32[]{:S(2)}) %collective-permute-start.67) | collective-permute-done | bytes 262176 | tf_op jit(solution)/shard_map/ppermute | solution.py:25
  354.0 6.2 %down_product.1.outs_1_ = bf16[2,4,64,2048]{3,2,1,0:T(8,128)(2,1)} custom-call(s32[3]{0:T(128)} %pad_add_fusion.me.where, bf16[4,256,2048]{2,1,0:T(8,128)(2,1)} %bitcast.209, bf16[256,512]{1,0:T(8,128)(2,1)} %get-tuple-element.196.refs_0_, bf16[256,512]{1,0:T(8,128)(2,1)} %copy-done.69, bf16[256,512]{1,0:T(8,128)(2,1)} %copy-done.70, ...), custom_call_target="tpu_custom_call" | custom-call | flops 3000000000 | bytes 10000000 | tf_op jit(solution)/shard_map/down_product/pallas_call | solution.py:928
  360.3 3.0 collective-permute-start.50
  363.3 2.9 collective-permute-done.50
  368.0 25.3 %collective-permute-done.51 = bf16[160,2048]{1,0:T(8,128)(2,1)S(1)} collective-permute-done((bf16[160,2048]{1,0:T(8,128)(2,1)S(1)}, bf16[160,2048]{1,0:T(8,128)(2,1)S(1)}, u32[]{:S(2)}, u32[]{:S(2)}) %collective-permute-start.51) | collective-permute-done | bytes 655392 | tf_op jit(solution)/shard_map/ppermute | solution.py:25
  394.4 4.3 turn.1.event
  400.9 4.0 collective-permute-done.63.came
  407.6 4.0 collective-permute-start.64
  413.8 4.9 normed_back.1
  423.3 3.5 collective-permute-start.76
  426.9 3.2 collective-permute-start.77
  436.4 2.6 collective-permute-done.78.refs_3_
  439.6 5.0 token_product.1
  448.0 11.4 %collective-permute-done.79 = bf16[2,2,256,256]{3,2,1,0:T(8,128)(2,1)S(1)} collective-permute-done((bf16[2,2,256,256]{3,2,1,0:T(8,128)(2,1)}, bf16[2,2,256,256]{3,2,1,0:T(8,128)(2,1)S(1)}, u32[]{:S(2)}, u32[]{:S(2)}) %collective-permute-start.79) | collective-permute-done | bytes 524320 | tf_op jit(solution)/shard_map/ppermute | solution.py:25
  462.5 2.5 collective-permute-start.86
  466.2 2.9 collective-permute-start.62
  471.1 6.0 %collective-permute-done.62 = bf16[256,768]{1,0:T(8,128)(2,1)S(1)} collective-permute-done((bf16[256,768]{1,0:T(8,128)(2,1)S(1)}, bf16[256,768]{1,0:T(8,128)(2,1)S(1)}, u32[]{:S(2)}, u32[]{:S(2)}) %collective-permute-start.62) | collective-permute-done | bytes 393248 | tf_op jit(solution)/shard_map/ppermute | solution.py:25
  483.6 2.5 final.1
  488.7 2.6 collective-permute-start.84
  491.3 3.3 collective-permute-start.70
  494.7 3.1 collective-permute-done.71
  497.7 3.7 collective-permute-start.72
  503.4 2.8 share.1
  (434 shorter events, 155.5 us)
Async XLA Ops:
  7.2 93.4 %all-gather.11.cloned.1.call-start = ((), (), s32[]{:S(2)}) async-start(), calls=%async_computation.6 | async-start | bytes 3604480 | tf_op jit(solution)/shard_map/all_gather | solution.py:1053
  27.5 9.3 %collective-permute-start.6 = (bf16[256,256]{1,0:T(8,128)(2,1)S(1)}, bf16[256,256]{1,0:T(8,128)(2,1)S(1)}, u32[]{:S(2)}, u32[]{:S(2)}) collective-permute-start(bf16[256,256]{1,0:T(8,128)(2,1)S(1)} %pad_maximum_fusion.6.refs_4_), channel_id=1, source_target_pairs={{0,64},{4,68},{8,72},{12,76},{16,80},{20,84},{24,88},{28,92},{32,9... | collective-permute-start | bytes 393224 | tf_op jit(solution)/shard_map/ppermute | solution.py:25
  30.2 8.3 %collective-permute-start.7 = (bf16[256,256]{1,0:T(8,128)(2,1)S(1)}, bf16[256,256]{1,0:T(8,128)(2,1)S(1)}, u32[]{:S(2)}, u32[]{:S(2)}) collective-permute-start(bf16[256,256]{1,0:T(8,128)(2,1)S(1)} %pad_maximum_fusion.6.refs_4_), channel_id=1, source_target_pairs={{0,96},{4,100},{8,104},{12,108},{16,112},{20,116},{24,120},{28,124... | collective-permute-start | bytes 393224 | tf_op jit(solution)/shard_map/ppermute | solution.py:25
  30.2 8.3 %collective-permute-start.2 = (bf16[256,256]{1,0:T(8,128)(2,1)S(1)}, bf16[256,256]{1,0:T(8,128)(2,1)S(1)}, u32[]{:S(2)}, u32[]{:S(2)}) collective-permute-start(bf16[256,256]{1,0:T(8,128)(2,1)S(1)} %pad_maximum_fusion.5.refs_0_), channel_id=1, source_target_pairs={{0,4},{4,0},{8,12},{12,8},{16,20},{20,16},{24,28},{28,24},{32,36},... | collective-permute-start | bytes 393224 | tf_op jit(solution)/shard_map/ppermute | solution.py:25
  47.1 105.3 %all-gather.13.cloned.1.call-start = ((), (), s32[]{:S(2)}) async-start(), calls=%async_computation.7 | async-start | bytes 5242880 | tf_op jit(solution)/shard_map/all_gather | solution.py:42
  47.9 158.2 %all-gather.15.cloned.1.call-start = ((), (), s32[]{:S(2)}) async-start(), calls=%async_computation.8 | async-start | bytes 5242880 | tf_op jit(solution)/shard_map/all_gather | solution.py:42
  47.9 11.9 %collective-permute-start.8 = (bf16[1024,256]{1,0:T(8,128)(2,1)S(1)}, bf16[1024,256]{1,0:T(8,128)(2,1)S(1)}, u32[]{:S(2)}, u32[]{:S(2)}) collective-permute-start(bf16[1024,256]{1,0:T(8,128)(2,1)S(1)} %copy-done.11), channel_id=1, source_target_pairs={{0,32},{4,36},{8,40},{12,44},{16,48},{20,52},{24,56},{28,60},{32,0... | collective-permute-start | bytes 1572872 | tf_op jit(solution)/shard_map/ppermute | solution.py:25
  48.0 14.5 %collective-permute-start.9 = (bf16[1024,256]{1,0:T(8,128)(2,1)S(1)}, bf16[1024,256]{1,0:T(8,128)(2,1)S(1)}, u32[]{:S(2)}, u32[]{:S(2)}) collective-permute-start(bf16[1024,256]{1,0:T(8,128)(2,1)S(1)} %copy-done.11), channel_id=1, source_target_pairs={{0,96},{4,100},{8,104},{12,108},{16,112},{20,116},{24,120},{28,124... | collective-permute-start | bytes 1572872 | tf_op jit(solution)/shard_map/ppermute | solution.py:25
  50.7 11.9 %collective-permute-start.12 = (bf16[1024,256]{1,0:T(8,128)(2,1)}, bf16[1024,256]{1,0:T(8,128)(2,1)S(1)}, u32[]{:S(2)}, u32[]{:S(2)}) collective-permute-start(bf16[1024,256]{1,0:T(8,128)(2,1)} %get-tuple-element.134), channel_id=1, source_target_pairs={{0,4},{4,0},{8,12},{12,8},{16,20},{20,16},{24,28},{28,24},{32,36},... | collective-permute-start | bytes 1572872 | tf_op jit(solution)/shard_map/ppermute | solution.py:25
  50.7 15.5 %collective-permute-start.13 = (bf16[1024,256]{1,0:T(8,128)(2,1)}, bf16[1024,256]{1,0:T(8,128)(2,1)S(1)}, u32[]{:S(2)}, u32[]{:S(2)}) collective-permute-start(bf16[1024,256]{1,0:T(8,128)(2,1)} %get-tuple-element.134), channel_id=1, source_target_pairs={{0,12},{4,8},{8,4},{12,0},{16,28},{20,24},{24,20},{28,16},{32,44},... | collective-permute-start | bytes 1572872 | tf_op jit(solution)/shard_map/ppermute | solution.py:25
  51.7 16.9 %collective-permute-start.16 = (bf16[1024,256]{1,0:T(8,128)(2,1)S(1)}, bf16[1024,256]{1,0:T(8,128)(2,1)}, u32[]{:S(2)}, u32[]{:S(2)}) collective-permute-start(bf16[1024,256]{1,0:T(8,128)(2,1)S(1)} %copy-done.11), channel_id=1, source_target_pairs={{0,1},{1,0},{2,3},{3,2},{4,5},{5,4},{6,7},{7,6},{8,9},{9,8},{10,11... | collective-permute-start | bytes 1572872 | tf_op jit(solution)/shard_map/ppermute | solution.py:25
  59.9 8.8 %collective-permute-start.10 = (bf16[512,256]{1,0:T(8,128)(2,1)S(1)}, bf16[512,256]{1,0:T(8,128)(2,1)S(1)}, u32[]{:S(2)}, u32[]{:S(2)}) collective-permute-start(bf16[512,256]{1,0:T(8,128)(2,1)S(1)} %slice.325), channel_id=1, source_target_pairs={{0,96},{4,100},{8,104},{12,108},{16,112},{20,116},{24,120},{28,124... | collective-permute-start | bytes 786440 | tf_op jit(solution)/shard_map/ppermute | solution.py:25
  63.4 13.2 %collective-permute-start.21 = (bf16[1024,256]{1,0:T(8,128)(2,1)}, bf16[1024,256]{1,0:T(8,128)(2,1)}, u32[]{:S(2)}, u32[]{:S(2)}) collective-permute-start(bf16[1024,256]{1,0:T(8,128)(2,1)} %get-tuple-element.134), channel_id=1, source_target_pairs={{0,1},{1,0},{2,3},{3,2},{4,5},{5,4},{6,7},{7,6},{8,9},{9,8},{10,11... | collective-permute-start | bytes 1572872 | tf_op jit(solution)/shard_map/ppermute | solution.py:25
  66.2 9.1 %collective-permute-start.14 = (bf16[512,256]{1,0:T(8,128)(2,1)S(1)}, bf16[512,256]{1,0:T(8,128)(2,1)}, u32[]{:S(2)}, u32[]{:S(2)}) collective-permute-start(bf16[512,256]{1,0:T(8,128)(2,1)S(1)} %slice.327), channel_id=1, source_target_pairs={{0,12},{4,8},{8,4},{12,0},{16,28},{20,24},{24,20},{28,16},{32,44},... | collective-permute-start | bytes 786440 | tf_op jit(solution)/shard_map/ppermute | solution.py:25
  68.6 8.0 %collective-permute-start.15 = (bf16[512,256]{1,0:T(8,128)(2,1)S(1)}, bf16[512,256]{1,0:T(8,128)(2,1)}, u32[]{:S(2)}, u32[]{:S(2)}) collective-permute-start(bf16[512,256]{1,0:T(8,128)(2,1)S(1)} %slice.328), channel_id=1, source_target_pairs={{0,4},{4,0},{8,12},{12,8},{16,20},{20,16},{24,28},{28,24},{32,36},... | collective-permute-start | bytes 786440 | tf_op jit(solution)/shard_map/ppermute | solution.py:25
  68.7 8.8 %collective-permute-start.19 = (bf16[512,256]{1,0:T(8,128)(2,1)S(1)}, bf16[512,256]{1,0:T(8,128)(2,1)}, u32[]{:S(2)}, u32[]{:S(2)}) collective-permute-start(bf16[512,256]{1,0:T(8,128)(2,1)S(1)} %collective-permute-done.10), channel_id=1, source_target_pairs={{0,1},{1,0},{2,3},{3,2},{4,5},{5,4},{6,7},{7,6},{8,9},{9,8},{10,11... | collective-permute-start | bytes 786440 | tf_op jit(solution)/shard_map/ppermute | solution.py:25
  112.2 8.4 %collective-permute-start.29 = (bf16[64,2048]{1,0:T(8,128)(2,1)}, bf16[64,2048]{1,0:T(8,128)(2,1)S(1)}, u32[]{:S(2)}, u32[]{:S(2)}) collective-permute-start(bf16[64,2048]{1,0:T(8,128)(2,1)} %get-tuple-element.137.refs_0_), channel_id=1, source_target_pairs={{0,1},{1,0},{2,3},{3,2},{4,5},{5,4},{6,7},{7,6},{8,9},{9,8},{10,11... | collective-permute-start | bytes 786440 | tf_op jit(solution)/shard_map/ppermute | solution.py:25
  138.2 203.9 %all-gather.19.cloned.1.call-start = ((), (), s32[]{:S(2)}) async-start(), calls=%async_computation.10 | async-start | bytes 5242880 | tf_op jit(solution)/shard_map/all_gather | solution.py:42
  138.8 274.4 %reduce-scatter.6.cloned.1.call-start = ((), (), s32[]{:S(2)}) async-start(), calls=%async_computation.4 | async-start | bytes 5242880 | tf_op jit(solution)/shard_map/reduce_scatter | solution.py:46
  144.5 8.0 %collective-permute-start.32 = (bf16[64,2048]{1,0:T(8,128)(2,1)S(1)}, bf16[64,2048]{1,0:T(8,128)(2,1)S(1)}, u32[]{:S(2)}, u32[]{:S(2)}) collective-permute-start(bf16[64,2048]{1,0:T(8,128)(2,1)S(1)} %slice.394), channel_id=1, source_target_pairs={{0,2},{1,3},{2,0},{3,1},{4,6},{5,7},{6,4},{7,5},{8,10},{9,11},{10,... | collective-permute-start | bytes 786440 | tf_op jit(solution)/shard_map/ppermute | solution.py:25
  161.8 9.5 %collective-permute-start.34 = (bf16[64,2048]{1,0:T(8,128)(2,1)}, bf16[64,2048]{1,0:T(8,128)(2,1)S(1)}, u32[]{:S(2)}, u32[]{:S(2)}) collective-permute-start(bf16[64,2048]{1,0:T(8,128)(2,1)} %get-tuple-element.142.refs_0_), channel_id=1, source_target_pairs={{0,1},{1,0},{2,3},{3,2},{4,5},{5,4},{6,7},{7,6},{8,9},{9,8},{10,11... | collective-permute-start | bytes 786440 | tf_op jit(solution)/shard_map/ppermute | solution.py:25
  198.8 22.7 %collective-permute-start.41 = (bf16[256,1024]{1,0:T(8,128)(2,1)S(1)}, bf16[256,1024]{1,0:T(8,128)(2,1)S(1)}, u32[]{:S(2)}, u32[]{:S(2)}) collective-permute-start(bf16[256,1024]{1,0:T(8,128)(2,1)S(1)} %copy-done.14), channel_id=1, source_target_pairs={{0,4},{4,0},{8,12},{12,8},{16,20},{20,16},{24,28},{28,24},{32,36},... | collective-permute-start | bytes 1572872 | tf_op jit(solution)/shard_map/ppermute | solution.py:25
  199.0 29.0 %collective-permute-start.42 = (bf16[256,1024]{1,0:T(8,128)(2,1)S(1)}, bf16[256,1024]{1,0:T(8,128)(2,1)}, u32[]{:S(2)}, u32[]{:S(2)}) collective-permute-start(bf16[256,1024]{1,0:T(8,128)(2,1)S(1)} %copy-done.13), channel_id=1, source_target_pairs={{0,8},{4,12},{8,0},{12,4},{16,24},{20,28},{24,16},{28,20},{32,40},... | collective-permute-start | bytes 1572872 | tf_op jit(solution)/shard_map/ppermute | solution.py:25
  204.9 25.0 %collective-permute-start.43 = (bf16[256,1024]{1,0:T(8,128)(2,1)S(1)}, bf16[256,1024]{1,0:T(8,128)(2,1)}, u32[]{:S(2)}, u32[]{:S(2)}) collective-permute-start(bf16[256,1024]{1,0:T(8,128)(2,1)S(1)} %copy-done.12), channel_id=1, source_target_pairs={{0,12},{4,8},{8,4},{12,0},{16,28},{20,24},{24,20},{28,16},{32,44},... | collective-permute-start | bytes 1572872 | tf_op jit(solution)/shard_map/ppermute | solution.py:25
  213.7 16.3 %collective-permute-start.39 = (bf16[64,2048]{1,0:T(8,128)(2,1)}, bf16[64,2048]{1,0:T(8,128)(2,1)S(1)}, u32[]{:S(2)}, u32[]{:S(2)}) collective-permute-start(bf16[64,2048]{1,0:T(8,128)(2,1)} %get-tuple-element.162.refs_0_), channel_id=1, source_target_pairs={{0,1},{1,0},{2,3},{3,2},{4,5},{5,4},{6,7},{7,6},{8,9},{9,8},{10,11... | collective-permute-start | bytes 786440 | tf_op jit(solution)/shard_map/ppermute | solution.py:25
  219.5 10.5 %collective-permute-start.40 = (bf16[64,2048]{1,0:T(8,128)(2,1)S(1)}, bf16[64,2048]{1,0:T(8,128)(2,1)S(1)}, u32[]{:S(2)}, u32[]{:S(2)}) collective-permute-start(bf16[64,2048]{1,0:T(8,128)(2,1)S(1)} %collective-permute-done.38.refs_1_), channel_id=1, source_target_pairs={{0,1},{1,0},{2,3},{3,2},{4,5},{5,4},{6,7},{7,6},{8,9},{9,8},{10,11... | collective-permute-start | bytes 786440 | tf_op jit(solution)/shard_map/ppermute | solution.py:25
  255.3 177.6 %reduce-scatter.8.cloned.1.call-start = ((), (), s32[]{:S(2)}) async-start(), calls=%async_computation.5 | async-start | bytes 3145728 | tf_op jit(solution)/shard_map/reduce_scatter | solution.py:46
  255.3 8.9 %collective-permute-start.44 = (bf16[48,128,256]{2,1,0:T(8,128)(2,1)}, bf16[48,128,256]{2,1,0:T(8,128)(2,1)S(1)}, u32[]{:S(2)}, u32[]{:S(2)}) collective-permute-start(bf16[48,128,256]{2,1,0:T(8,128)(2,1)} %get-tuple-element.164), channel_id=1, source_target_pairs={{0,1},{1,0},{2,3},{3,2},{4,5},{5,4},{6,7},{7,6},{8,9},{9,8},{10,11... | collective-permute-start | bytes 9437192 | tf_op jit(solution)/shard_map/ppermute | solution.py:25
  269.8 13.9 %collective-permute-start.46 = (bf16[4,128,256]{2,1,0:T(8,128)(2,1)}, bf16[4,128,256]{2,1,0:T(8,128)(2,1)S(1)}, u32[]{:S(2)}, u32[]{:S(2)}) collective-permute-start(bf16[4,128,256]{2,1,0:T(8,128)(2,1)} %get-tuple-element.168.event), channel_id=1, source_target_pairs={{0,32},{4,36},{8,40},{12,44},{16,48},{20,52},{24,56},{28,60},{32,0... | collective-permute-start | bytes 786440 | tf_op jit(solution)/shard_map/ppermute | solution.py:25
  270.9 15.1 %collective-permute-start.47 = (bf16[4,128,256]{2,1,0:T(8,128)(2,1)}, bf16[4,128,256]{2,1,0:T(8,128)(2,1)S(1)}, u32[]{:S(2)}, u32[]{:S(2)}) collective-permute-start(bf16[4,128,256]{2,1,0:T(8,128)(2,1)} %get-tuple-element.169), channel_id=1, source_target_pairs={{0,96},{4,100},{8,104},{12,108},{16,112},{20,116},{24,120},{28,124... | collective-permute-start | bytes 786440 | tf_op jit(solution)/shard_map/ppermute | solution.py:25
  270.9 15.1 %collective-permute-start.48 = (bf16[4,128,256]{2,1,0:T(8,128)(2,1)}, bf16[4,128,256]{2,1,0:T(8,128)(2,1)S(1)}, u32[]{:S(2)}, u32[]{:S(2)}) collective-permute-start(bf16[4,128,256]{2,1,0:T(8,128)(2,1)} %get-tuple-element.170), channel_id=1, source_target_pairs={{0,4},{4,0},{8,12},{12,8},{16,20},{20,16},{24,28},{28,24},{32,36},... | collective-permute-start | bytes 786440 | tf_op jit(solution)/shard_map/ppermute | solution.py:25
  270.9 15.1 %collective-permute-start.49 = (bf16[4,128,256]{2,1,0:T(8,128)(2,1)}, bf16[4,128,256]{2,1,0:T(8,128)(2,1)S(1)}, u32[]{:S(2)}, u32[]{:S(2)}) collective-permute-start(bf16[4,128,256]{2,1,0:T(8,128)(2,1)} %get-tuple-element.171), channel_id=1, source_target_pairs={{0,12},{4,8},{8,4},{12,0},{16,28},{20,24},{24,20},{28,16},{32,44},... | collective-permute-start | bytes 786440 | tf_op jit(solution)/shard_map/ppermute | solution.py:25
  292.2 25.1 %collective-permute-start.52 = (bf16[8,128,256]{2,1,0:T(8,128)(2,1)}, bf16[8,128,256]{2,1,0:T(8,128)(2,1)S(1)}, u32[]{:S(2)}, u32[]{:S(2)}) collective-permute-start(bf16[8,128,256]{2,1,0:T(8,128)(2,1)} %get-tuple-element.172.refs_1_), channel_id=1, source_target_pairs={{0,32},{4,36},{8,40},{12,44},{16,48},{20,52},{24,56},{28,60},{32,0... | collective-permute-start | bytes 1572872 | tf_op jit(solution)/shard_map/ppermute | solution.py:25
  292.2 26.3 %collective-permute-start.53 = (bf16[8,128,256]{2,1,0:T(8,128)(2,1)}, bf16[8,128,256]{2,1,0:T(8,128)(2,1)S(1)}, u32[]{:S(2)}, u32[]{:S(2)}) collective-permute-start(bf16[8,128,256]{2,1,0:T(8,128)(2,1)} %get-tuple-element.176), channel_id=1, source_target_pairs={{0,96},{4,100},{8,104},{12,108},{16,112},{20,116},{24,120},{28,124... | collective-permute-start | bytes 1572872 | tf_op jit(solution)/shard_map/ppermute | solution.py:25
  292.2 26.2 %collective-permute-start.54 = (bf16[8,128,256]{2,1,0:T(8,128)(2,1)}, bf16[8,128,256]{2,1,0:T(8,128)(2,1)S(1)}, u32[]{:S(2)}, u32[]{:S(2)}) collective-permute-start(bf16[8,128,256]{2,1,0:T(8,128)(2,1)} %get-tuple-element.177), channel_id=1, source_target_pairs={{0,4},{4,0},{8,12},{12,8},{16,20},{20,16},{24,28},{28,24},{32,36},... | collective-permute-start | bytes 1572872 | tf_op jit(solution)/shard_map/ppermute | solution.py:25
  292.3 26.2 %collective-permute-start.55 = (bf16[8,128,256]{2,1,0:T(8,128)(2,1)}, bf16[8,128,256]{2,1,0:T(8,128)(2,1)S(1)}, u32[]{:S(2)}, u32[]{:S(2)}) collective-permute-start(bf16[8,128,256]{2,1,0:T(8,128)(2,1)} %get-tuple-element.178), channel_id=1, source_target_pairs={{0,12},{4,8},{8,4},{12,0},{16,28},{20,24},{24,20},{28,16},{32,44},... | collective-permute-start | bytes 1572872 | tf_op jit(solution)/shard_map/ppermute | solution.py:25
  322.9 9.7 %collective-permute-start.57 = (bf16[2,128,256]{2,1,0:T(8,128)(2,1)}, bf16[2,128,256]{2,1,0:T(8,128)(2,1)S(1)}, u32[]{:S(2)}, u32[]{:S(2)}) collective-permute-start(bf16[2,128,256]{2,1,0:T(8,128)(2,1)} %get-tuple-element.184), channel_id=1, source_target_pairs={{0,8},{4,12},{8,0},{12,4},{16,24},{20,28},{24,16},{28,20},{32,40},... | collective-permute-start | bytes 393224 | tf_op jit(solution)/shard_map/ppermute | solution.py:25
  326.9 8.3 %collective-permute-start.58 = (bf16[2,128,256]{2,1,0:T(8,128)(2,1)}, bf16[2,128,256]{2,1,0:T(8,128)(2,1)S(1)}, u32[]{:S(2)}, u32[]{:S(2)}) collective-permute-start(bf16[2,128,256]{2,1,0:T(8,128)(2,1)} %get-tuple-element.185), channel_id=1, source_target_pairs={{0,12},{4,8},{8,4},{12,0},{16,28},{20,24},{24,20},{28,16},{32,44},... | collective-permute-start | bytes 393224 | tf_op jit(solution)/shard_map/ppermute | solution.py:25
  327.1 8.0 %collective-permute-start.59 = (bf16[2,128,256]{2,1,0:T(8,128)(2,1)}, bf16[2,128,256]{2,1,0:T(8,128)(2,1)S(1)}, u32[]{:S(2)}, u32[]{:S(2)}) collective-permute-start(bf16[2,128,256]{2,1,0:T(8,128)(2,1)} %get-tuple-element.186), channel_id=1, source_target_pairs={{0,32},{4,36},{8,40},{12,44},{16,48},{20,52},{24,56},{28,60},{32,0... | collective-permute-start | bytes 393224 | tf_op jit(solution)/shard_map/ppermute | solution.py:25
  327.2 8.0 %collective-permute-start.60 = (bf16[2,128,256]{2,1,0:T(8,128)(2,1)}, bf16[2,128,256]{2,1,0:T(8,128)(2,1)S(1)}, u32[]{:S(2)}, u32[]{:S(2)}) collective-permute-start(bf16[2,128,256]{2,1,0:T(8,128)(2,1)} %get-tuple-element.187), channel_id=1, source_target_pairs={{0,64},{4,68},{8,72},{12,76},{16,80},{20,84},{24,88},{28,92},{32,9... | collective-permute-start | bytes 393224 | tf_op jit(solution)/shard_map/ppermute | solution.py:25
  338.6 9.5 %collective-permute-start.66 = (bf16[256,512]{1,0:T(8,128)(2,1)}, bf16[256,512]{1,0:T(8,128)(2,1)S(1)}, u32[]{:S(2)}, u32[]{:S(2)}) collective-permute-start(bf16[256,512]{1,0:T(8,128)(2,1)} %get-tuple-element.201), channel_id=1, source_target_pairs={{0,64},{4,68},{8,72},{12,76},{16,80},{20,84},{24,88},{28,92},{32,9... | collective-permute-start | bytes 786440 | tf_op jit(solution)/shard_map/ppermute | solution.py:25
  340.3 13.0 %collective-permute-start.67 = (bf16[256,512]{1,0:T(8,128)(2,1)}, bf16[256,512]{1,0:T(8,128)(2,1)S(1)}, u32[]{:S(2)}, u32[]{:S(2)}) collective-permute-start(bf16[256,512]{1,0:T(8,128)(2,1)} %get-tuple-element.202), channel_id=1, source_target_pairs={{0,96},{4,100},{8,104},{12,108},{16,112},{20,116},{24,120},{28,124... | collective-permute-start | bytes 786440 | tf_op jit(solution)/shard_map/ppermute | solution.py:25
  360.2 104.8 %reduce-scatter.4.cloned.1.call-start = ((), (), s32[]{:S(2)}) async-start(), calls=%async_computation.3 | async-start | bytes 3932160 | tf_op jit(solution)/shard_map/reduce_scatter | solution.py:46
  366.7 26.6 %collective-permute-start.51 = (bf16[160,2048]{1,0:T(8,128)(2,1)S(1)}, bf16[160,2048]{1,0:T(8,128)(2,1)S(1)}, u32[]{:S(2)}, u32[]{:S(2)}) collective-permute-start(bf16[160,2048]{1,0:T(8,128)(2,1)S(1)} %fusion.4), channel_id=1, source_target_pairs={{0,2},{1,3},{2,0},{3,1},{4,6},{5,7},{6,4},{7,5},{8,10},{9,11},{10,... | collective-permute-start | bytes 1966088 | tf_op jit(solution)/shard_map/ppermute | solution.py:25
  398.7 112.6 %all-gather.17.cloned.1.call-start = ((), (), s32[]{:S(2)}) async-start(), calls=%async_computation.9 | async-start | bytes 1474560 | tf_op jit(solution)/shard_map/all_gather | solution.py:1253
  421.0 13.7 %collective-permute-start.75 = (f32[16,2048]{1,0:T(8,128)S(1)}, f32[16,2048]{1,0:T(8,128)S(1)}, u32[]{:S(2)}, u32[]{:S(2)}) collective-permute-start(f32[16,2048]{1,0:T(8,128)S(1)} %fusion.17), channel_id=1, source_target_pairs={{0,2},{1,3},{2,0},{3,1},{4,6},{5,7},{6,4},{7,5},{8,10},{9,11},{10,... | collective-permute-start | bytes 393224 | tf_op jit(solution)/shard_map/ppermute | solution.py:25
  423.3 8.2 %collective-permute-start.76 = (bf16[256,192]{1,0:T(8,128)(2,1)}, bf16[256,192]{1,0:T(8,128)(2,1)S(1)}, u32[]{:S(2)}, u32[]{:S(2)}) collective-permute-start(bf16[256,192]{1,0:T(8,128)(2,1)} %get-tuple-element.213), channel_id=1, source_target_pairs={{0,4},{4,0},{8,12},{12,8},{16,20},{20,16},{24,28},{28,24},{32,36},... | collective-permute-start | bytes 294920 | tf_op jit(solution)/shard_map/ppermute | solution.py:25
  426.9 9.5 %collective-permute-start.77 = (bf16[256,192]{1,0:T(8,128)(2,1)}, bf16[256,192]{1,0:T(8,128)(2,1)S(1)}, u32[]{:S(2)}, u32[]{:S(2)}) collective-permute-start(bf16[256,192]{1,0:T(8,128)(2,1)} %get-tuple-element.214), channel_id=1, source_target_pairs={{0,8},{4,12},{8,0},{12,4},{16,24},{20,28},{24,16},{28,20},{32,40},... | collective-permute-start | bytes 294920 | tf_op jit(solution)/shard_map/ppermute | solution.py:25
  430.1 8.8 %collective-permute-start.78 = (bf16[256,192]{1,0:T(8,128)(2,1)}, bf16[256,192]{1,0:T(8,128)(2,1)S(1)}, u32[]{:S(2)}, u32[]{:S(2)}) collective-permute-start(bf16[256,192]{1,0:T(8,128)(2,1)} %get-tuple-element.215), channel_id=1, source_target_pairs={{0,12},{4,8},{8,4},{12,0},{16,28},{20,24},{24,20},{28,16},{32,44},... | collective-permute-start | bytes 294920 | tf_op jit(solution)/shard_map/ppermute | solution.py:25
  431.0 14.9 %collective-permute-start.73 = (bf16[256,1024]{1,0:T(8,128)(2,1)}, bf16[256,1024]{1,0:T(8,128)(2,1)S(1)}, u32[]{:S(2)}, u32[]{:S(2)}) collective-permute-start(bf16[256,1024]{1,0:T(8,128)(2,1)} %dynamic-slice_bitcast_fusion), channel_id=1, source_target_pairs={{0,16},{4,20},{8,24},{12,28},{16,0},{20,4},{24,8},{28,12},{32,48},... | collective-permute-start | bytes 1572872 | tf_op jit(solution)/shard_map/ppermute | solution.py:25
  431.6 13.0 %collective-permute-start.68 = (bf16[128,2048]{1,0:T(8,128)(2,1)}, bf16[128,2048]{1,0:T(8,128)(2,1)S(1)}, u32[]{:S(2)}, u32[]{:S(2)}) collective-permute-start(bf16[128,2048]{1,0:T(8,128)(2,1)} %get-tuple-element.204), channel_id=1, source_target_pairs={{0,1},{1,0},{2,3},{3,2},{4,5},{5,4},{6,7},{7,6},{8,9},{9,8},{10,11... | collective-permute-start | bytes 1572872 | tf_op jit(solution)/shard_map/ppermute | solution.py:25
  434.8 13.1 %collective-permute-start.85 = (bf16[2,64,2048]{2,1,0:T(8,128)(2,1)}, bf16[2,64,2048]{2,1,0:T(8,128)(2,1)S(1)}, u32[]{:S(2)}, u32[]{:S(2)}) collective-permute-start(bf16[2,64,2048]{2,1,0:T(8,128)(2,1)} %slice.353), channel_id=1, source_target_pairs={{0,4},{4,0},{8,12},{12,8},{16,20},{20,16},{24,28},{28,24},{32,36},... | collective-permute-start | bytes 1572872 | tf_op jit(solution)/shard_map/ppermute | solution.py:25
  444.6 14.8 %collective-permute-start.79 = (bf16[2,2,256,256]{3,2,1,0:T(8,128)(2,1)}, bf16[2,2,256,256]{3,2,1,0:T(8,128)(2,1)S(1)}, u32[]{:S(2)}, u32[]{:S(2)}) collective-permute-start(bf16[2,2,256,256]{3,2,1,0:T(8,128)(2,1)} %get-tuple-element.217), channel_id=1, source_target_pairs={{0,32},{4,36},{8,40},{12,44},{16,48},{20,52},{24,56},{28,60},{32,0... | collective-permute-start | bytes 1572872 | tf_op jit(solution)/shard_map/ppermute | solution.py:25
  445.6 37.3 %collective-permute-start.69 = (bf16[64,2048]{1,0:T(8,128)(2,1)S(1)}, bf16[64,2048]{1,0:T(8,128)(2,1)S(1)}, u32[]{:S(2)}, u32[]{:S(2)}) collective-permute-start(bf16[64,2048]{1,0:T(8,128)(2,1)S(1)} %slice.392), channel_id=1, source_target_pairs={{0,2},{1,3},{2,0},{3,1},{4,6},{5,7},{6,4},{7,5},{8,10},{9,11},{10,... | collective-permute-start | bytes 786440 | tf_op jit(solution)/shard_map/ppermute | solution.py:25
  459.6 9.4 %collective-permute-start.80 = (bf16[2,256,256]{2,1,0:T(8,128)(2,1)S(1)}, bf16[2,256,256]{2,1,0:T(8,128)(2,1)S(1)}, u32[]{:S(2)}, u32[]{:S(2)}) collective-permute-start(bf16[2,256,256]{2,1,0:T(8,128)(2,1)S(1)} %slice_bitcast_fusion.3), channel_id=1, source_target_pairs={{0,96},{4,100},{8,104},{12,108},{16,112},{20,116},{24,120},{28,124... | collective-permute-start | bytes 786440 | tf_op jit(solution)/shard_map/ppermute | solution.py:25
  462.5 28.8 %collective-permute-start.86 = (bf16[64,2048]{1,0:T(8,128)(2,1)S(1)}, bf16[64,2048]{1,0:T(8,128)(2,1)S(1)}, u32[]{:S(2)}, u32[]{:S(2)}) collective-permute-start(bf16[64,2048]{1,0:T(8,128)(2,1)S(1)} %get-tuple-element.339), channel_id=1, source_target_pairs={{0,12},{4,8},{8,4},{12,0},{16,28},{20,24},{24,20},{28,16},{32,44},... | collective-permute-start | bytes 786440 | tf_op jit(solution)/shard_map/ppermute | solution.py:25
  466.2 10.9 %collective-permute-start.62 = (bf16[256,768]{1,0:T(8,128)(2,1)S(1)}, bf16[256,768]{1,0:T(8,128)(2,1)S(1)}, u32[]{:S(2)}, u32[]{:S(2)}) collective-permute-start(bf16[256,768]{1,0:T(8,128)(2,1)S(1)} %dynamic-slice_bitcast_fusion.1), channel_id=1, source_target_pairs={{0,16},{4,20},{8,24},{12,28},{16,0},{20,4},{24,8},{28,12},{32,48},... | collective-permute-start | bytes 1179656 | tf_op jit(solution)/shard_map/ppermute | solution.py:25
  469.1 10.8 %collective-permute-start.81 = (bf16[256,256]{1,0:T(8,128)(2,1)S(1)}, bf16[256,256]{1,0:T(8,128)(2,1)S(1)}, u32[]{:S(2)}, u32[]{:S(2)}) collective-permute-start(bf16[256,256]{1,0:T(8,128)(2,1)S(1)} %slice_bitcast_fusion.9), channel_id=1, source_target_pairs={{0,16},{4,20},{8,24},{12,28},{16,0},{20,4},{24,8},{28,12},{32,48},... | collective-permute-start | bytes 393224 | tf_op jit(solution)/shard_map/ppermute | solution.py:25
  482.9 18.6 %collective-permute-start.82 = (bf16[64,2048]{1,0:T(8,128)(2,1)}, bf16[64,2048]{1,0:T(8,128)(2,1)S(1)}, u32[]{:S(2)}, u32[]{:S(2)}) collective-permute-start(bf16[64,2048]{1,0:T(8,128)(2,1)} %get-tuple-element.219), channel_id=1, source_target_pairs={{0,4},{4,0},{8,12},{12,8},{16,20},{20,16},{24,28},{28,24},{32,36},... | collective-permute-start | bytes 786440 | tf_op jit(solution)/shard_map/ppermute | solution.py:25
  486.2 11.6 %collective-permute-start.71 = (bf16[64,2048]{1,0:T(8,128)(2,1)}, bf16[64,2048]{1,0:T(8,128)(2,1)S(1)}, u32[]{:S(2)}, u32[]{:S(2)}) collective-permute-start(bf16[64,2048]{1,0:T(8,128)(2,1)} %final.1), channel_id=1, source_target_pairs={{0,2},{1,3},{2,0},{3,1},{4,6},{5,7},{6,4},{7,5},{8,10},{9,11},{10,... | collective-permute-start | bytes 786440 | tf_op jit(solution)/shard_map/ppermute | solution.py:25
  487.5 14.0 %collective-permute-start.83 = (bf16[64,2048]{1,0:T(8,128)(2,1)S(1)}, bf16[64,2048]{1,0:T(8,128)(2,1)S(1)}, u32[]{:S(2)}, u32[]{:S(2)}) collective-permute-start(bf16[64,2048]{1,0:T(8,128)(2,1)S(1)} %copy-done.65), channel_id=1, source_target_pairs={{0,8},{4,12},{8,0},{12,4},{16,24},{20,28},{24,16},{28,20},{32,40},... | collective-permute-start | bytes 786440 | tf_op jit(solution)/shard_map/ppermute | solution.py:25
  488.7 14.0 %collective-permute-start.84 = (bf16[64,2048]{1,0:T(8,128)(2,1)S(1)}, bf16[64,2048]{1,0:T(8,128)(2,1)S(1)}, u32[]{:S(2)}, u32[]{:S(2)}) collective-permute-start(bf16[64,2048]{1,0:T(8,128)(2,1)S(1)} %copy-done.64), channel_id=1, source_target_pairs={{0,12},{4,8},{8,4},{12,0},{16,28},{20,24},{24,20},{28,16},{32,44},... | collective-permute-start | bytes 786440 | tf_op jit(solution)/shard_map/ppermute | solution.py:25
  491.3 18.1 %collective-permute-start.70 = (bf16[64,2048]{1,0:T(8,128)(2,1)}, bf16[64,2048]{1,0:T(8,128)(2,1)S(1)}, u32[]{:S(2)}, u32[]{:S(2)}) collective-permute-start(bf16[64,2048]{1,0:T(8,128)(2,1)} %final.1), channel_id=1, source_target_pairs={{0,1},{1,0},{2,3},{3,2},{4,5},{5,4},{6,7},{7,6},{8,9},{9,8},{10,11... | collective-permute-start | bytes 786440 | tf_op jit(solution)/shard_map/ppermute | solution.py:25
  497.7 11.7 %collective-permute-start.72 = (bf16[64,2048]{1,0:T(8,128)(2,1)S(1)}, bf16[64,2048]{1,0:T(8,128)(2,1)S(1)}, u32[]{:S(2)}, u32[]{:S(2)}) collective-permute-start(bf16[64,2048]{1,0:T(8,128)(2,1)S(1)} %collective-permute-done.71), channel_id=1, source_target_pairs={{0,1},{1,0},{2,3},{3,2},{4,5},{5,4},{6,7},{7,6},{8,9},{9,8},{10,11... | collective-permute-start | bytes 786440 | tf_op jit(solution)/shard_map/ppermute | solution.py:25
  (117 other events, 715.9 us)
Sparse Core Ops, SparseCore 0:
  47.3 36.3 all-gather.10
  85.3 48.6 all-gather.12
  138.4 47.5 all-gather.14
  187.4 48.6 all-gather.18
  255.4 66.1 reduce-scatter.5
  360.3 47.6 reduce-scatter.7
  410.4 40.4 reduce-scatter.3
  478.1 26.0 all-gather.16
